TPU v7x, 32 devices: a whole 2x2x4 slice. The times are simulated.
32 devices in a mesh: groups: 1, side: 2 (over core), dev: 16 (over z, y, x).
Axes of the slice: x: 2, y: 2, z: 4, core: 2. Of those that a mesh axis runs over, the one named last changes fastest.
Arguments:
- tokens: bfloat16 [256, 4096], P(('groups', 'side', 'dev')), may hold values from -6 to 6
- norm_gain: float32 [4096], replicated, may hold values from 0.1 to 1.9
- expert_ids: int32 [256, 8], P(('groups', 'side', 'dev')), may hold values from 0 to 15, all different within a row; in each aligned block of 8 rows (0 to 7, 8 to 15, ...) at most 8 rows name the same one
- route_weight: float32 [256, 8], P(('groups', 'side', 'dev')), may hold values from 0.05 to 1
- placement: int32 [16], replicated, may hold values from 0 to 15, each once
- w_gate: bfloat16 [16, 4096, 768], P('dev', None, 'side'), may hold values from -0.09375 to 0.09375
- w_up: bfloat16 [16, 4096, 768], P('dev', None, 'side'), may hold values from -0.09375 to 0.09375
- w_down: bfloat16 [16, 768, 4096], P('dev', 'side'), may hold values from -0.21875 to 0.21875
Outputs:
- combined: bfloat16 [256, 4096], P(('groups', 'side', 'dev'))
Inputs may be any that keep to these rules, and one draw needn't show every extreme that they name: `expert_ids`: each row names 8 different experts; among the rows of one device no expert is named more than 8 times. `placement`: A permutation of the weight slots.
All inputs are finite; a program needn't handle non-finite values.
Results may differ from a plain program's by a relative error of at most 0.007.
Values may be sent and summed in bfloat16 or wider, within the bound.
No kernel may reach another device: no remote copies, remote signals or barrier semaphores. Data moves between devices by JAX's collectives and lax.ppermute only.
A program may use at most 64 MiB of HBM per device.

v0:
```python
import jax
import jax.numpy as jnp
from jax import lax
from jax.sharding import PartitionSpec as P


def from_partner(block, axis, bit):
    count = lax.axis_size(axis)
    route = []
    for low in range(count):
        high = low | 1 << bit
        if high != low and high < count:
            route += [(low, high), (high, low)]
    return lax.ppermute(block, axis, route)


def expert_rows(inputs, w_gate, w_up, w_down):
    gate = jnp.dot(inputs, w_gate[0], preferred_element_type=jnp.float32)
    upward = jnp.dot(inputs, w_up[0], preferred_element_type=jnp.float32)
    hidden = (jax.nn.silu(gate) * upward).astype(jnp.bfloat16)
    return jnp.dot(hidden, w_down[0], preferred_element_type=jnp.float32)


def deliver(outgoing, w_gate, w_up, w_down):
    width = outgoing.shape[-1]
    arrived = lax.all_to_all(outgoing, "dev", split_axis=0, concat_axis=0, tiled=True)
    partner = from_partner(arrived, "side", 0)
    leading = lax.axis_index("side") == 0
    paired = jnp.where(leading, jnp.stack([arrived, partner]), jnp.stack([partner, arrived]))
    partial_value = expert_rows(paired.reshape(-1, width), w_gate, w_up, w_down).reshape(
        paired.shape
    )
    summed = lax.psum_scatter(partial_value, "side", scatter_dimension=0, tiled=True)
    finished = summed[0].astype(jnp.bfloat16)
    return lax.all_to_all(finished, "dev", split_axis=0, concat_axis=0, tiled=True)


def body(tokens, norm_gain, expert_ids, route_weight, placement, w_gate, w_up, w_down):
    count, width = tokens.shape
    chosen = expert_ids.shape[1]
    experts = placement.shape[0]
    owners = lax.axis_size("dev")
    capacity = 2 * ((count * chosen + experts - 1) // experts)
    places = owners * capacity
    values = tokens.astype(jnp.float32)
    scale = lax.rsqrt(jnp.mean(values * values, axis=-1, keepdims=True) + 1e-06)
    normed = (values * scale * norm_gain).astype(jnp.bfloat16)
    listed = expert_ids.reshape(-1)
    owner_of = jnp.sum(
        jnp.where(listed[:, None] == jnp.arange(experts)[None, :], placement[None, :], 0), axis=1
    )
    owner_hits = (owner_of[:, None] == jnp.arange(owners)[None, :]).astype(jnp.int32)
    earlier = jnp.cumsum(owner_hits, axis=0) - owner_hits
    position = jnp.sum(earlier * owner_hits, axis=1)
    target = owner_of * capacity + position
    matches = target[None, :] == jnp.arange(places)[:, None]
    selector = jnp.sum(matches.reshape(places, count, chosen).astype(jnp.float32), axis=2).astype(
        jnp.bfloat16
    )
    outgoing = jnp.dot(selector, normed, preferred_element_type=jnp.float32).astype(jnp.bfloat16)
    outgoing = outgoing.reshape(owners, capacity, width)
    received = deliver(outgoing, w_gate, w_up, w_down)
    landing = target.reshape(count, chosen)[:, :, None] == jnp.arange(places)[None, None, :]
    mixing = jnp.sum(jnp.where(landing, route_weight[:, :, None], 0.0), axis=1)
    combined = jnp.dot(
        mixing, received.reshape(places, width).astype(jnp.float32), precision=lax.Precision.HIGHEST
    )
    return combined.astype(jnp.bfloat16)


def solution(mesh):
    in_specs = (
        P(("groups", "side", "dev"), None),
        P(),
        P(("groups", "side", "dev"), None),
        P(("groups", "side", "dev"), None),
        P(),
        P("dev", None, "side"),
        P("dev", None, "side"),
        P("dev", "side", None),
    )
    out_specs = P(("groups", "side", "dev"), None)
    return jax.shard_map(body, mesh=mesh, in_specs=in_specs, out_specs=out_specs, check_vma=False)
```

profile of v0, /device:TPU:0, one launch (start us, length us, event | category | flops | bytes accessed | tf_op | source)
XLA Modules:
  0.0 112.5 jit_solution(15561726165720576254)
XLA Ops:
  6.5 0.0 copy-start
  6.5 0.0 reduce-scatter.2.cloned.1.call-start
  6.5 0.9 eq.58
  7.5 1.0 fusion.8
  8.5 0.8 select_reduce_fusion.2
  9.3 0.1 fusion.14
  9.4 0.1 reduce_window_sum.11
  9.5 0.2 select_reduce_fusion.1
  9.7 0.1 add.29
  9.8 0.1 convert_reduce_fusion
  9.9 1.3 %fusion = bf16[16,8,4096]{2,1,0:T(8,128)(2,1)S(1)} fusion(bf16[8,4096]{1,0:T(8,128)(2,1)} %param.8, f32[4096]{0:T(1024)} %param.9, f32[8]{0:T(128)S(1)} %add_rsqrt_fusion, bf16[128,8]{0,1:T(8,128)(2,1)S(1)} %convert_reduce_fusion), kind=kOutput, calls=%fused_computation.1 | convolution fusion | flops 9043968 | bytes 1132576 | tf_op jit(solution)/shard_map/dot_general | solution.py:60
  11.2 34.6 %all_to_all.10 = bf16[16,8,4096]{2,1,0:T(8,128)(2,1)} all-to-all(bf16[16,8,4096]{2,1,0:T(8,128)(2,1)S(1)} %fusion), channel_id=1, replica_groups=mesh['groups'=1,'side'=2,'dev'=16] {'dev'}, dimensions={0} | all-to-all | bytes 2097152 | tf_op jit(solution)/shard_map/all_to_all | solution.py:26
  45.8 0.0 collective-permute-start
  45.8 3.0 %collective-permute-done = bf16[16,8,4096]{2,1,0:T(8,128)(2,1)} collective-permute-done((bf16[16,8,4096]{2,1,0:T(8,128)(2,1)}, bf16[16,8,4096]{2,1,0:T(8,128)(2,1)}, u32[]{:S(2)}, u32[]{:S(2)}) %collective-permute-start) | collective-permute-done | bytes 1048608 | tf_op jit(solution)/shard_map/ppermute | solution.py:14
  48.8 0.0 copy-start.2
  48.8 2.7 %maximum_select_fusion = bf16[2,16,8,4096]{3,2,1,0:T(8,128)(2,1)S(1)} fusion(bf16[1,16,8,4096]{3,2,1,0:T(8,128)(2,1)} %bitcast.2, bf16[1,16,8,4096]{3,2,1,0:T(8,128)(2,1)} %bitcast.1, pred[]{:T(512)S(6)} %eq.68), kind=kLoop, calls=%fused_computation.9 | loop fusion | flops 3145728 | bytes 4194305 | tf_op jit(solution)/shard_map/jit(_where)/select_n | solution.py:29
  51.5 0.5 copy-done.2
  52.0 0.0 copy-start.3
  52.0 1.3 %fusion.5 = f32[256,384]{1,0:T(8,128)S(1)} fusion(bf16[256,4096]{1,0:T(8,128)(2,1)S(1)} %bitcast.31, bf16[1,4096,384]{2,1,0:T(8,128)(2,1)S(1)} %copy-done.2), kind=kOutput, calls=%fused_computation.7 | convolution fusion | flops 805306368 | bytes 5636096 | tf_op jit(solution)/shard_map/dot_general | solution.py:18
  53.3 0.6 copy-done.3
  53.9 1.3 %multiply_convert_fusion = bf16[256,384]{1,0:T(8,128)(2,1)S(1)} fusion(f32[256,384]{1,0:T(8,128)S(1)} %fusion.5, bf16[256,4096]{1,0:T(8,128)(2,1)S(1)} %bitcast.32, bf16[1,4096,384]{2,1,0:T(8,128)(2,1)S(1)} %copy-done.3), kind=kOutput, calls=%fused_computation.12 | convolution fusion | flops 805896192 | bytes 5832704 | tf_op jit(solution)/shard_map/dot_general | solution.py:19
  55.2 0.0 copy-done
  55.2 3.2 %fusion.1 = f32[2,16,8,4096]{3,2,1,0:T(8,128)} fusion(bf16[2,16,8,384]{3,2,1,0:T(8,128)(2,1)S(1)} %bitcast.33, bf16[1,384,4096]{2,1,0:T(8,128)(2,1)S(1)} %copy-done), kind=kOutput, calls=%fused_computation.3 | convolution fusion | flops 805306368 | bytes 7536640 | tf_op jit(solution)/shard_map/dot_general | solution.py:21
  58.4 0.0 reduce-scatter.2.cloned.1.call-update
  58.4 0.0 copy-start.1
  58.4 10.4 %reduce-scatter.2.cloned.1.call-done = f32[1,16,8,4096]{3,2,1,0:T(8,128)} async-done(((f32[2,16,8,4096]{3,2,1,0:T(8,128)}), f32[1,16,8,4096]{3,2,1,0:T(8,128)}) %reduce-scatter.2.cloned.1.call-update) | async-done | bytes 2097168 | tf_op jit(solution)/shard_map/reduce_scatter | solution.py:33
  68.9 2.7 %convert_bitcast_fusion = bf16[16,8,4096]{2,1,0:T(8,128)(2,1)} fusion(f32[1,16,8,4096]{3,2,1,0:T(8,128)} %reduce-scatter.2.cloned.1.call-done), kind=kLoop, calls=%fused_computation.11 | loop fusion | flops 524288 | bytes 3145728 | tf_op jit(solution)/shard_map/convert_element_type | solution.py:34
  71.6 7.0 %all-to-all-start.1 = ((bf16[16,8,4096]{2,1,0:T(8,128)(2,1)}), bf16[16,8,4096]{2,1,0:T(8,128)(2,1)}, u32[]{:S(2)}, u32[]{:S(2)}) async-start(bf16[16,8,4096]{2,1,0:T(8,128)(2,1)} %convert_bitcast_fusion), calls=%async_computation.2 | async-start | bytes 2097152 | tf_op jit(solution)/shard_map/all_to_all | solution.py:35
  78.6 0.0 copy-done.1
  78.6 0.1 select_reduce_fusion
  78.7 24.6 %all-to-all-done.1 = bf16[16,8,4096]{2,1,0:T(8,128)(2,1)} async-done(((bf16[16,8,4096]{2,1,0:T(8,128)(2,1)}), bf16[16,8,4096]{2,1,0:T(8,128)(2,1)}, u32[]{:S(2)}, u32[]{:S(2)}) %all-to-all-start.1) | async-done | bytes 1048608 | tf_op jit(solution)/shard_map/all_to_all | solution.py:35
  103.2 2.4 %convolution_convert_fusion.1 = bf16[8,4096]{1,0:T(8,128)(2,1)} fusion(f32[8,128]{1,0:T(8,128)S(1)} %select_reduce_fusion, bf16[16,8,4096]{2,1,0:T(8,128)(2,1)} %all-to-all-done.1), kind=kOutput, calls=%fused_computation.2 | convolution fusion | flops 50364416 | bytes 1118208 | tf_op jit(solution)/shard_map/dot_general | solution.py:65
  (2 shorter events, 0.0 us)
Async XLA Ops:
  6.5 48.6 %copy-start = (bf16[1,384,4096]{2,1,0:T(8,128)(2,1)S(1)}, bf16[1,384,4096]{2,1,0:T(8,128)(2,1)}, u32[]{:S(2)}) copy-start(bf16[1,384,4096]{2,1,0:T(8,128)(2,1)} %param.15) | copy-start | bytes 9437188
  6.5 62.3 %reduce-scatter.2.cloned.1.call-start = ((), (), s32[]{:S(2)}) async-start(), calls=%async_computation.3 | async-start | bytes 6291456 | tf_op jit(solution)/shard_map/reduce_scatter | solution.py:33
  45.8 3.0 %collective-permute-start = (bf16[16,8,4096]{2,1,0:T(8,128)(2,1)}, bf16[16,8,4096]{2,1,0:T(8,128)(2,1)}, u32[]{:S(2)}, u32[]{:S(2)}) collective-permute-start(bf16[16,8,4096]{2,1,0:T(8,128)(2,1)} %all_to_all.10), channel_id=1, source_target_pairs={{0,16},{16,0},{1,17},{17,1},{2,18},{18,2},{3,19},{19,3},{4,20},{20... | collective-permute-start | bytes 3145736 | tf_op jit(solution)/shard_map/ppermute | solution.py:14
  48.8 3.2 %copy-start.2 = (bf16[1,4096,384]{2,1,0:T(8,128)(2,1)S(1)}, bf16[1,4096,384]{2,1,0:T(8,128)(2,1)}, u32[]{:S(2)}) copy-start(bf16[1,4096,384]{2,1,0:T(8,128)(2,1)} %param.13) | copy-start | bytes 9437188
  52.0 1.9 %copy-start.3 = (bf16[1,4096,384]{2,1,0:T(8,128)(2,1)S(1)}, bf16[1,4096,384]{2,1,0:T(8,128)(2,1)}, u32[]{:S(2)}) copy-start(bf16[1,4096,384]{2,1,0:T(8,128)(2,1)} %param.14) | copy-start | bytes 9437188
  58.4 20.2 %copy-start.1 = (f32[8,8]{1,0:T(8,128)S(1)}, f32[8,8]{1,0:T(8,128)}, u32[]{:S(2)}) copy-start(f32[8,8]{1,0:T(8,128)} %param.11) | copy-start | bytes 772
  71.6 31.7 %all-to-all-start.1 = ((bf16[16,8,4096]{2,1,0:T(8,128)(2,1)}), bf16[16,8,4096]{2,1,0:T(8,128)(2,1)}, u32[]{:S(2)}, u32[]{:S(2)}) async-start(bf16[16,8,4096]{2,1,0:T(8,128)(2,1)} %convert_bitcast_fusion), calls=%async_computation.2 | async-start | bytes 2097152 | tf_op jit(solution)/shard_map/all_to_all | solution.py:35
Sparse Core Ops, SparseCore 0:
  58.5 10.2 reduce-scatter.1
where the time goes:
time: 113 us; the launch traced here: 112 us
  waiting for transfers between devices  38 us (34%)
  blocking collectives  34.6 us (31%)
  between operations  13.5 us (12%)
  matrix products  9.47 us (8%)
  other arithmetic  7.82 us (7%)
  starting transfers between devices  6.99 us (6%)
  local copies, waits for them, and re-layouts  2.07 us (2%)
    all_to_all x1, blocking collectives, deliver(): lax.all_to_all(outgoing, 'dev', split_axis=0, concat_axis=0, tiled=True)  34.6 us
    all_to_all x1, waiting for transfers between devices, deliver(): lax.all_to_all(finished, 'dev', split_axis=0, concat_axis=0, tiled=True)  24.6 us
    reduce_scatter x1, waiting for transfers between devices, deliver(): lax.psum_scatter(partial_value, 'side', scatter_dimension=0, tiled=True)  10.4 us
    all_to_all x1, starting transfers between devices, deliver(): lax.all_to_all(finished, 'dev', split_axis=0, concat_axis=0, tiled=True)  6.99 us
    dot_general x1, matrix products, expert_rows(): return jnp.dot(hidden, w_down[0], preferred_element_type=jnp.float32)  3.19 us
    ppermute x1, waiting for transfers between devices, from_partner(): return lax.ppermute(block, axis, route)  3 us
    convert_element_type x1, other arithmetic, deliver(): finished = summed[0].astype(jnp.bfloat16)  2.71 us
    select_n x1, other arithmetic, deliver(): jnp.where(leading, jnp.stack([arrived, partner]), jnp.stack([partner, arr...  2.68 us
  transfers between devices with their start and end apart: 3, of which 3 were waited for; matrix products, arithmetic and copies ran while one was open for 0% of the time, Pallas kernels for 0%

commit v1 on v0

v1 whole, which is shorter than its diff:
```python
import functools

import jax
import jax.numpy as jnp
from jax import lax
from jax.experimental import pallas as pl
from jax.experimental.pallas import tpu as pltpu
from jax.sharding import PartitionSpec as P


def swap(block, axis, offset):
    count = lax.axis_size(axis)
    return lax.ppermute(block, axis, [(i, i ^ offset) for i in range(count)])


def prepare_kernel(slots, tok_ref, gain_ref, ids_ref, weight_ref, placement_ref, out_ref):
    width = tok_ref.shape[1]
    values = tok_ref[...].astype(jnp.float32)
    scale = lax.rsqrt(jnp.mean(values * values, axis=-1, keepdims=True) + 1e-06)
    out_ref[:, :width] = (values * scale * gain_ref[...].reshape(1, width)).astype(jnp.bfloat16)
    ids = ids_ref[...]
    slot = jnp.zeros_like(ids)
    for expert in range(placement_ref.shape[0]):
        slot = jnp.where(ids == expert, placement_ref[expert], slot)
    lane = lax.broadcasted_iota(jnp.int32, (ids.shape[0], out_ref.shape[1] - width), 1)
    place = lax.rem(lane, slots)
    section = lax.div(lane, slots)
    mixing = jnp.zeros(lane.shape, jnp.float32)
    for k in range(ids.shape[1]):
        mixing += jnp.where(place == slot[:, k : k + 1], weight_ref[:, k : k + 1], 0.0)
    high = mixing.astype(jnp.bfloat16)
    rest = mixing - high.astype(jnp.float32)
    middle = rest.astype(jnp.bfloat16)
    low = rest - middle.astype(jnp.float32)
    parts = jnp.where(
        section == 0,
        high.astype(jnp.float32),
        jnp.where(section == 1, middle.astype(jnp.float32), jnp.where(section == 2, low, 0.0)),
    )
    out_ref[:, width:] = parts.astype(jnp.bfloat16)


def prepare(tokens, norm_gain, expert_ids, route_weight, placement, slots, extra):
    count, width = tokens.shape
    vmem = pl.BlockSpec(memory_space=pltpu.VMEM)
    return pl.pallas_call(
        functools.partial(prepare_kernel, slots),
        out_shape=jax.ShapeDtypeStruct((count, width + extra), jnp.bfloat16),
        in_specs=[vmem, vmem, vmem, vmem, pl.BlockSpec(memory_space=pltpu.SMEM)],
        out_specs=vmem,
    )(tokens, norm_gain, expert_ids, route_weight, placement)


def hidden_rows(rows, w_gate, w_up):
    gate = jnp.dot(rows, w_gate, preferred_element_type=jnp.float32)
    upward = jnp.dot(rows, w_up, preferred_element_type=jnp.float32)
    return (jax.nn.silu(gate) * upward).astype(jnp.bfloat16)


def body(tokens, norm_gain, expert_ids, route_weight, placement, w_gate, w_up, w_down):
    count, width = tokens.shape
    owners = lax.axis_size("dev")
    me = lax.axis_index("dev")
    half = width // 2
    extra = -(-3 * owners // 128) * 128
    packed = prepare(tokens, norm_gain, expert_ids, route_weight, placement, owners, extra)
    cold = list(range(4, owners, 4))
    column = jnp.concatenate([packed] + [swap(packed, "dev", r) for r in cold])
    span = column.shape[0]
    along_x = swap(column, "dev", 1)
    along_y = swap(column, "dev", 2)
    diag = jnp.concatenate(
        [swap(along_y[:, :half], "dev", 1), swap(along_x[:, half:], "dev", 2)], axis=1
    )
    own = jnp.concatenate([column, along_x, along_y, diag])
    other = swap(own, "side", 1)

    def routed(rows):
        chosen = lax.rem(lax.broadcasted_iota(jnp.int32, (1, extra), 1), owners) == me
        weight = jnp.sum(
            jnp.where(chosen, rows[:, width:].astype(jnp.float32), 0.0), axis=1, keepdims=True
        )
        hidden = hidden_rows(rows[:, :width], w_gate[0], w_up[0])
        return jnp.dot(hidden, w_down[0], preferred_element_type=jnp.float32) * weight

    away = routed(other).astype(jnp.bfloat16)
    total = routed(own) + swap(away, "side", 1).astype(jnp.float32)
    s_own, s_x, s_y, s_diag = (total[i * span : (i + 1) * span] for i in range(4))

    def send(value, offset):
        return swap(value.astype(jnp.bfloat16), "dev", offset).astype(jnp.float32)

    from_y = send(s_diag[:, :half], 2)
    from_x = send(s_diag[:, half:], 1)
    s_x = jnp.concatenate([s_x[:, :half] + from_y, s_x[:, half:]], axis=1)
    s_y = jnp.concatenate([s_y[:, :half], s_y[:, half:] + from_x], axis=1)
    column_sum = s_own + send(s_x, 1) + send(s_y, 2)
    result = column_sum[:count]
    for i, r in enumerate(cold):
        result = result + send(column_sum[(i + 1) * count : (i + 2) * count], r)
    return result.astype(jnp.bfloat16)


def solution(mesh):
    in_specs = (
        P(("groups", "side", "dev"), None),
        P(),
        P(("groups", "side", "dev"), None),
        P(("groups", "side", "dev"), None),
        P(),
        P("dev", None, "side"),
        P("dev", None, "side"),
        P("dev", "side", None),
    )
    out_specs = P(("groups", "side", "dev"), None)
    return jax.shard_map(body, mesh=mesh, in_specs=in_specs, out_specs=out_specs, check_vma=False)
```

time: 113 us -> 77.1 us (0.68)
  blocking collectives: 34.6 us -> 0 us
  between operations: 13.5 us -> 0.09 us
  starting transfers between devices: 6.99 us -> 19.7 us
  waiting for transfers between devices: 38 us -> 27.5 us
  matrix products: 9.47 us -> 16.1 us
  local copies, waits for them, and re-layouts: 2.07 us -> 6.08 us
  other arithmetic: 7.82 us -> 5.42 us
  Pallas kernels: 0 us -> 1.79 us
    all_to_all x1 -> x0, blocking collectives: 34.6 us -> none  [deliver(): lax.all_to_all(outgoing, 'dev', split_axis=0, concat_axis=0, tiled=True)]
    all_to_all x1 -> x0, waiting for transfers between devices: 24.6 us -> none  [deliver(): lax.all_to_all(finished, 'dev', split_axis=0, concat_axis=0, tiled=True)]
    ppermute x1 -> x16, waiting for transfers between devices: 3 us -> 27.5 us  [swap(): return lax.ppermute(block, axis, [(i, i ^ offset) for i in range(count)])]
    ppermute x1 -> x16, starting transfers between devices: 0.01 us -> 19.7 us  [swap(): return lax.ppermute(block, axis, [(i, i ^ offset) for i in range(count)])]
    reduce_scatter x1 -> x0, waiting for transfers between devices: 10.4 us -> none  [deliver(): lax.psum_scatter(partial_value, 'side', scatter_dimension=0, tiled=True)]
    all_to_all x1 -> x0, starting transfers between devices: 6.99 us -> none  [deliver(): lax.all_to_all(finished, 'dev', split_axis=0, concat_axis=0, tiled=True)]
    dot_general x5 -> x4, matrix products: 9.47 us -> 16.1 us  [the longest x2 10.2 us: routed(): jnp.dot(hidden, w_down[0], preferred_element_type=jnp.float32) * weight]
    unnamed x8, local copies, waits for them, and re-layouts: 1.08 us -> 4.91 us
  transfers between devices with their start and end apart: 3 -> 16, of which waited for: 3 -> 13; matrix products, arithmetic and copies ran while one was open for 0% -> 10% of each run, Pallas kernels for 0% -> 0%
where the time goes in v1:
time: 77.1 us; the launch traced here: 76.7 us
  waiting for transfers between devices  27.5 us (36%)
  starting transfers between devices  19.7 us (26%)
  matrix products  16.1 us (21%)
  local copies, waits for them, and re-layouts  6.08 us (8%)
  other arithmetic  5.42 us (7%)
  Pallas kernels  1.79 us (2%)
    ppermute x16, waiting for transfers between devices, swap(): return lax.ppermute(block, axis, [(i, i ^ offset) for i in range(count)])  27.5 us
    ppermute x16, starting transfers between devices, swap(): return lax.ppermute(block, axis, [(i, i ^ offset) for i in range(count)])  19.7 us
    dot_general x2, matrix products, routed(): jnp.dot(hidden, w_down[0], preferred_element_type=jnp.float32) * weight  10.2 us
    dot_general x2, matrix products, hidden_rows(): upward = jnp.dot(rows, w_up, preferred_element_type=jnp.float32)  5.85 us
    unnamed x8, local copies, waits for them, and re-layouts  4.91 us
    another operation x2, other arithmetic  2.21 us
    pallas_call x1, Pallas kernels, prepare(): pl.pallas_call(functools.partial(prepare_kernel, slots), out_shape=jax.Sh...  1.79 us
  transfers between devices with their start and end apart: 16, of which 13 were waited for; matrix products, arithmetic and copies ran while one was open for 10% of the time, Pallas kernels for 0%

profile of v1, /device:TPU:0, one launch (start us, length us, event | category | flops | bytes accessed | tf_op | source)
XLA Modules:
  0.0 76.7 jit_solution(9981549056572111933)
XLA Ops:
  0.0 1.8 %shard_map.82 = bf16[8,4224]{1,0:T(8,128)(2,1)} custom-call(bf16[8,4096]{1,0:T(8,128)(2,1)} %tok_ref.1, f32[4096]{0:T(1024)} %gain_ref.1, s32[8,8]{1,0:T(8,128)} %ids_ref.1, f32[8,8]{1,0:T(8,128)} %weight_ref.1, s32[16]{0:T(128)} %placement_ref.1), custom_call_target="tpu_custom_call" | custom-call | tf_op jit(solution)/shard_map/pallas_call | solution.py:46
  1.8 5.0 %collective-permute-start.2 = (bf16[8,4224]{1,0:T(8,128)(2,1)}, bf16[8,4224]{1,0:T(8,128)(2,1)S(1)}, u32[]{:S(2)}, u32[]{:S(2)}) collective-permute-start(bf16[8,4224]{1,0:T(8,128)(2,1)} %shard_map.82), channel_id=1, source_target_pairs={{0,12},{1,13},{2,14},{3,15},{4,8},{5,9},{6,10},{7,11},{8,4},{9,5},... | collective-permute-start | bytes 202760 | tf_op jit(solution)/shard_map/ppermute | solution.py:13
  6.8 0.0 collective-permute-start.1
  6.8 0.6 collective-permute-start
  7.4 1.5 %constant_dynamic-update-slice_fusion.5 = bf16[128,4224]{1,0:T(8,128)(2,1)} fusion(bf16[8,4224]{1,0:T(8,128)(2,1)} %shard_map.82), kind=kLoop, calls=%fused_computation.43 | loop fusion | bytes 135168
  9.0 0.7 collective-permute-done.2
  9.7 3.1 %collective-permute-done.1 = bf16[8,4224]{1,0:T(8,128)(2,1)S(1)} collective-permute-done((bf16[8,4224]{1,0:T(8,128)(2,1)}, bf16[8,4224]{1,0:T(8,128)(2,1)S(1)}, u32[]{:S(2)}, u32[]{:S(2)}) %collective-permute-start.1) | collective-permute-done | bytes 67616 | tf_op jit(solution)/shard_map/ppermute | solution.py:13
  12.8 0.9 %pad_maximum_fusion = bf16[32,4224]{1,0:T(8,128)(2,1)S(1)} fusion(bf16[8,4224]{1,0:T(8,128)(2,1)S(1)} %collective-permute-done.2, bf16[8,4224]{1,0:T(8,128)(2,1)S(1)} %collective-permute-done.1, bf16[8,4224]{1,0:T(8,128)(2,1)S(1)} %collective-permute-done, bf16[8,4224]{1,0:T(8,128)(2,1)} %shard_map.82), kind=kLoop, calls=%fused_computation.20 | loop fusion | flops 1081344 | bytes 540672 | tf_op jit(solution)/shard_map/concatenate | solution.py:68
  13.7 1.6 %collective-permute-start.4 = (bf16[32,4224]{1,0:T(8,128)(2,1)S(1)}, bf16[32,4224]{1,0:T(8,128)(2,1)S(1)}, u32[]{:S(2)}, u32[]{:S(2)}) collective-permute-start(bf16[32,4224]{1,0:T(8,128)(2,1)S(1)} %pad_maximum_fusion), channel_id=1, source_target_pairs={{0,2},{1,3},{2,0},{3,1},{4,6},{5,7},{6,4},{7,5},{8,10},{9,11},{10,... | collective-permute-start | bytes 811016 | tf_op jit(solution)/shard_map/ppermute | solution.py:13
  15.3 1.5 %collective-permute-start.3 = (bf16[32,4224]{1,0:T(8,128)(2,1)S(1)}, bf16[32,4224]{1,0:T(8,128)(2,1)S(1)}, u32[]{:S(2)}, u32[]{:S(2)}) collective-permute-start(bf16[32,4224]{1,0:T(8,128)(2,1)S(1)} %pad_maximum_fusion), channel_id=1, source_target_pairs={{0,1},{1,0},{2,3},{3,2},{4,5},{5,4},{6,7},{7,6},{8,9},{9,8},{10,11... | collective-permute-start | bytes 811016 | tf_op jit(solution)/shard_map/ppermute | solution.py:13
  16.8 0.6 constant_dynamic-update-slice_fusion.4
  17.4 0.6 constant_dynamic-update-slice_fusion.3
  18.1 0.6 constant_dynamic-update-slice_fusion.2
  18.7 3.1 %collective-permute-done.4 = bf16[32,4224]{1,0:T(8,128)(2,1)S(1)} collective-permute-done((bf16[32,4224]{1,0:T(8,128)(2,1)S(1)}, bf16[32,4224]{1,0:T(8,128)(2,1)S(1)}, u32[]{:S(2)}, u32[]{:S(2)}) %collective-permute-start.4) | collective-permute-done | bytes 270368 | tf_op jit(solution)/shard_map/ppermute | solution.py:13
  21.8 1.8 %collective-permute-start.5 = (bf16[32,2048]{1,0:T(8,128)(2,1)S(1)}, bf16[32,2048]{1,0:T(8,128)(2,1)S(1)}, u32[]{:S(2)}, u32[]{:S(2)}) collective-permute-start(bf16[32,2048]{1,0:T(8,128)(2,1)S(1)} %slice.84), channel_id=1, source_target_pairs={{0,1},{1,0},{2,3},{3,2},{4,5},{5,4},{6,7},{7,6},{8,9},{9,8},{10,11... | collective-permute-start | bytes 393224 | tf_op jit(solution)/shard_map/ppermute | solution.py:13
  23.6 1.6 %collective-permute-start.6 = (bf16[32,2176]{1,0:T(8,128)(2,1)S(1)}, bf16[32,2176]{1,0:T(8,128)(2,1)S(1)}, u32[]{:S(2)}, u32[]{:S(2)}) collective-permute-start(bf16[32,2176]{1,0:T(8,128)(2,1)S(1)} %slice.85), channel_id=1, source_target_pairs={{0,2},{1,3},{2,0},{3,1},{4,6},{5,7},{6,4},{7,5},{8,10},{9,11},{10,... | collective-permute-start | bytes 417800 | tf_op jit(solution)/shard_map/ppermute | solution.py:13
  25.2 0.7 constant_dynamic-update-slice_fusion.1
  25.9 0.7 constant_dynamic-update-slice_fusion
  26.7 0.2 collective-permute-done.5
  26.8 1.9 %collective-permute-done.6 = bf16[32,2176]{1,0:T(8,128)(2,1)S(1)} collective-permute-done((bf16[32,2176]{1,0:T(8,128)(2,1)S(1)}, bf16[32,2176]{1,0:T(8,128)(2,1)S(1)}, u32[]{:S(2)}, u32[]{:S(2)}) %collective-permute-start.6) | collective-permute-done | bytes 139296 | tf_op jit(solution)/shard_map/ppermute | solution.py:13
  28.7 0.7 maximum_dynamic-update-slice_fusion
  29.4 0.0 collective-permute-start.7
  29.5 3.0 %collective-permute-done.7 = bf16[128,4224]{1,0:T(8,128)(2,1)} collective-permute-done((bf16[128,4224]{1,0:T(8,128)(2,1)}, bf16[128,4224]{1,0:T(8,128)(2,1)}, u32[]{:S(2)}, u32[]{:S(2)}) %collective-permute-start.7) | collective-permute-done | bytes 1081376 | tf_op jit(solution)/shard_map/ppermute | solution.py:13
  32.5 0.9 %select_reduce_fusion.1 = (f32[128]{0:T(128)S(1)}, f32[128]{0:T(128)S(1)}) fusion(bf16[128,4224]{1,0:T(8,128)(2,1)} %maximum_dynamic-update-slice_fusion, pred[128]{0:T(512)(128)(4,1)S(1)} %and_compare_fusion, bf16[128,4224]{1,0:T(8,128)(2,1)} %collective-permute-done.7), kind=kLoop, calls=%fused_computation.37 | loop fusion | flops 98048 | bytes 66688 | tf_op jit(solution)/shard_map/reduce_sum | solution.py:80
  33.4 2.9 %fusion.3 = f32[128,384]{1,0:T(8,128)S(1)} fusion(bf16[1,4096,384]{2,1,0:T(8,128)(2,1)} %param.14, bf16[128,4224]{1,0:T(8,128)(2,1)} %collective-permute-done.7), kind=kOutput, calls=%fused_computation.4 | convolution fusion | flops 402653184 | bytes 4390912 | tf_op jit(solution)/shard_map/dot_general | solution.py:56
  36.3 4.6 %multiply_convert_fusion = bf16[128,4096]{1,0:T(8,128)(2,1)} fusion(f32[128]{0:T(128)S(1)} %get-tuple-element.6, bf16[1,384,4096]{2,1,0:T(8,128)(2,1)S(1)} %copy-done, f32[128,384]{1,0:T(8,128)S(1)} %fusion.3, bf16[1,4096,384]{2,1,0:T(8,128)(2,1)} %param.13, bf16[128,4224]{1,0:T(8,128)(2,1)} %collective-permute-done.7), kind=kOutput, calls=%fused_computation.13 | convolution fusion | flops 806649856 | bytes 8585728 | tf_op jit(solution)/shard_map/dot_general | solution.py:84
  40.9 0.1 collective-permute-start.8
  41.1 2.9 %fusion.5 = f32[128,384]{1,0:T(8,128)S(1)} fusion(bf16[1,4096,384]{2,1,0:T(8,128)(2,1)} %param.14, bf16[128,4224]{1,0:T(8,128)(2,1)} %maximum_dynamic-update-slice_fusion), kind=kOutput, calls=%fused_computation.6 | convolution fusion | flops 402653184 | bytes 4390912 | tf_op jit(solution)/shard_map/dot_general | solution.py:56
  44.0 0.0 collective-permute-done.8
  44.0 5.6 %fusion.49 = (bf16[128,4096]{1,0:T(8,128)(2,1)}, f32[128,4096]{1,0:T(8,128)}) fusion(bf16[128,4096]{1,0:T(8,128)(2,1)} %collective-permute-done.8, f32[128]{0:T(128)S(1)} %get-tuple-element.5, bf16[1,384,4096]{2,1,0:T(8,128)(2,1)S(1)} %copy-done, f32[128,384]{1,0:T(8,128)S(1)} %fusion.5, bf16[1,4096,384]{2,1,0:T(8,128)(2,1)} %param.13, ...), kind=kOutput, calls=%fused_computation.50 | convolution fusion | flops 807698432 | bytes 11731456 | tf_op jit(solution)/shard_map/dot_general | solution.py:84
  49.6 1.1 %fusion.47 = (bf16[32,2048]{1,0:T(8,128)(2,1)S(1)}, bf16[32,2048]{1,0:T(8,128)(2,1)S(1)}, bf16[32,2048]{1,0:T(8,128)(2,1)S(1)}, bf16[32,2048]{1,0:T(8,128)(2,1)S(1)}) fusion(bf16[128,4096]{1,0:T(8,128)(2,1)} %get-tuple-element.18), kind=kLoop, calls=%fused_computation.48 | loop fusion | bytes 1048576 | tf_op jit(solution)/shard_map/slice | solution.py:93
  50.8 1.6 %collective-permute-start.9 = (bf16[32,2048]{1,0:T(8,128)(2,1)S(1)}, bf16[32,2048]{1,0:T(8,128)(2,1)S(1)}, u32[]{:S(2)}, u32[]{:S(2)}) collective-permute-start(bf16[32,2048]{1,0:T(8,128)(2,1)S(1)} %get-tuple-element.11), channel_id=1, source_target_pairs={{0,2},{1,3},{2,0},{3,1},{4,6},{5,7},{6,4},{7,5},{8,10},{9,11},{10,... | collective-permute-start | bytes 393224 | tf_op jit(solution)/shard_map/ppermute | solution.py:13
  52.3 0.5 collective-permute-start.11
  52.9 3.7 %collective-permute-done.9 = bf16[32,2048]{1,0:T(8,128)(2,1)S(1)} collective-permute-done((bf16[32,2048]{1,0:T(8,128)(2,1)S(1)}, bf16[32,2048]{1,0:T(8,128)(2,1)S(1)}, u32[]{:S(2)}, u32[]{:S(2)}) %collective-permute-start.9) | collective-permute-done | bytes 131104 | tf_op jit(solution)/shard_map/ppermute | solution.py:13
  56.6 1.2 %collective-permute-done.11 = bf16[32,2048]{1,0:T(8,128)(2,1)S(1)} collective-permute-done((bf16[32,2048]{1,0:T(8,128)(2,1)S(1)}, bf16[32,2048]{1,0:T(8,128)(2,1)S(1)}, u32[]{:S(2)}, u32[]{:S(2)}) %collective-permute-start.11) | collective-permute-done | bytes 131104 | tf_op jit(solution)/shard_map/ppermute | solution.py:13
  57.8 1.1 %fusion.19 = (bf16[32,2048]{1,0:T(8,128)(2,1)S(1)}, bf16[32,2048]{1,0:T(8,128)(2,1)S(1)}) fusion(f32[128,4096]{1,0:T(8,128)} %get-tuple-element.19, bf16[32,2048]{1,0:T(8,128)(2,1)S(1)} %collective-permute-done.9, bf16[32,2048]{1,0:T(8,128)(2,1)S(1)} %collective-permute-done.11), kind=kLoop, calls=%fused_computation.25 | loop fusion | flops 393216 | bytes 1048576 | tf_op jit(solution)/shard_map/convert.7
  58.9 0.6 collective-permute-start.12
  59.5 1.2 %collective-permute-start.10 = (bf16[32,4096]{1,0:T(8,128)(2,1)S(1)}, bf16[32,4096]{1,0:T(8,128)(2,1)S(1)}, u32[]{:S(2)}, u32[]{:S(2)}) collective-permute-start(bf16[32,4096]{1,0:T(8,128)(2,1)S(1)} %pad_maximum_fusion.1), channel_id=1, source_target_pairs={{0,1},{1,0},{2,3},{3,2},{4,5},{5,4},{6,7},{7,6},{8,9},{9,8},{10,11... | collective-permute-start | bytes 786440 | tf_op jit(solution)/shard_map/ppermute | solution.py:13
  60.8 5.7 %collective-permute-done.12 = bf16[32,4096]{1,0:T(8,128)(2,1)S(1)} collective-permute-done((bf16[32,4096]{1,0:T(8,128)(2,1)S(1)}, bf16[32,4096]{1,0:T(8,128)(2,1)S(1)}, u32[]{:S(2)}, u32[]{:S(2)}) %collective-permute-start.12) | collective-permute-done | bytes 262176 | tf_op jit(solution)/shard_map/ppermute | solution.py:13
  66.5 0.4 collective-permute-done.10
  66.9 1.1 %fusion.45 = (bf16[32,4096]{1,0:T(8,128)(2,1)S(1)}, f32[32,4096]{1,0:T(8,128)S(1)}) fusion(bf16[32,4096]{1,0:T(8,128)(2,1)S(1)} %collective-permute-done.12, bf16[32,4096]{1,0:T(8,128)(2,1)S(1)} %collective-permute-done.10, f32[128,4096]{1,0:T(8,128)} %get-tuple-element.19), kind=kLoop, calls=%fused_computation.47 | loop fusion | flops 655360 | bytes 1835008 | tf_op jit(solution)/shard_map/convert.2
  68.0 0.3 collective-permute-start.13
  68.3 1.9 %collective-permute-start.15 = (bf16[8,4096]{1,0:T(8,128)(2,1)S(1)}, bf16[8,4096]{1,0:T(8,128)(2,1)S(1)}, u32[]{:S(2)}, u32[]{:S(2)}) collective-permute-start(bf16[8,4096]{1,0:T(8,128)(2,1)S(1)} %get-tuple-element.16), channel_id=1, source_target_pairs={{0,12},{1,13},{2,14},{3,15},{4,8},{5,9},{6,10},{7,11},{8,4},{9,5},... | collective-permute-start | bytes 196616 | tf_op jit(solution)/shard_map/ppermute | solution.py:13
  70.1 1.4 %collective-permute-start.14 = (bf16[8,4096]{1,0:T(8,128)(2,1)S(1)}, bf16[8,4096]{1,0:T(8,128)(2,1)S(1)}, u32[]{:S(2)}, u32[]{:S(2)}) collective-permute-start(bf16[8,4096]{1,0:T(8,128)(2,1)S(1)} %get-tuple-element.17), channel_id=1, source_target_pairs={{0,8},{1,9},{2,10},{3,11},{4,12},{5,13},{6,14},{7,15},{8,0},{9,1},... | collective-permute-start | bytes 196616 | tf_op jit(solution)/shard_map/ppermute | solution.py:13
  71.6 1.4 %collective-permute-done.13 = bf16[8,4096]{1,0:T(8,128)(2,1)S(1)} collective-permute-done((bf16[8,4096]{1,0:T(8,128)(2,1)S(1)}, bf16[8,4096]{1,0:T(8,128)(2,1)S(1)}, u32[]{:S(2)}, u32[]{:S(2)}) %collective-permute-start.13) | collective-permute-done | bytes 65568 | tf_op jit(solution)/shard_map/ppermute | solution.py:13
  73.0 1.5 %collective-permute-done.15 = bf16[8,4096]{1,0:T(8,128)(2,1)S(1)} collective-permute-done((bf16[8,4096]{1,0:T(8,128)(2,1)S(1)}, bf16[8,4096]{1,0:T(8,128)(2,1)S(1)}, u32[]{:S(2)}, u32[]{:S(2)}) %collective-permute-start.15) | collective-permute-done | bytes 65568 | tf_op jit(solution)/shard_map/ppermute | solution.py:13
  74.5 1.5 %collective-permute-done.14 = bf16[8,4096]{1,0:T(8,128)(2,1)S(1)} collective-permute-done((bf16[8,4096]{1,0:T(8,128)(2,1)S(1)}, bf16[8,4096]{1,0:T(8,128)(2,1)S(1)}, u32[]{:S(2)}, u32[]{:S(2)}) %collective-permute-start.14) | collective-permute-done | bytes 65568 | tf_op jit(solution)/shard_map/ppermute | solution.py:13
  76.0 0.7 fusion.22
  (10 shorter events, 0.1 us)
Async XLA Ops:
  0.0 36.3 %copy-start = (bf16[1,384,4096]{2,1,0:T(8,128)(2,1)S(1)}, bf16[1,384,4096]{2,1,0:T(8,128)(2,1)}, u32[]{:S(2)}) copy-start(bf16[1,384,4096]{2,1,0:T(8,128)(2,1)} %param.15) | copy-start | bytes 9437188
  1.8 7.9 %collective-permute-start.2 = (bf16[8,4224]{1,0:T(8,128)(2,1)}, bf16[8,4224]{1,0:T(8,128)(2,1)S(1)}, u32[]{:S(2)}, u32[]{:S(2)}) collective-permute-start(bf16[8,4224]{1,0:T(8,128)(2,1)} %shard_map.82), channel_id=1, source_target_pairs={{0,12},{1,13},{2,14},{3,15},{4,8},{5,9},{6,10},{7,11},{8,4},{9,5},... | collective-permute-start | bytes 202760 | tf_op jit(solution)/shard_map/ppermute | solution.py:13
  6.8 6.0 %collective-permute-start.1 = (bf16[8,4224]{1,0:T(8,128)(2,1)}, bf16[8,4224]{1,0:T(8,128)(2,1)S(1)}, u32[]{:S(2)}, u32[]{:S(2)}) collective-permute-start(bf16[8,4224]{1,0:T(8,128)(2,1)} %shard_map.82), channel_id=1, source_target_pairs={{0,8},{1,9},{2,10},{3,11},{4,12},{5,13},{6,14},{7,15},{8,0},{9,1},... | collective-permute-start | bytes 202760 | tf_op jit(solution)/shard_map/ppermute | solution.py:13
  6.8 6.0 %collective-permute-start = (bf16[8,4224]{1,0:T(8,128)(2,1)}, bf16[8,4224]{1,0:T(8,128)(2,1)S(1)}, u32[]{:S(2)}, u32[]{:S(2)}) collective-permute-start(bf16[8,4224]{1,0:T(8,128)(2,1)} %shard_map.82), channel_id=1, source_target_pairs={{0,4},{1,5},{2,6},{3,7},{4,0},{5,1},{6,2},{7,3},{8,12},{9,13},{10,... | collective-permute-start | bytes 202760 | tf_op jit(solution)/shard_map/ppermute | solution.py:13
  13.7 8.1 %collective-permute-start.4 = (bf16[32,4224]{1,0:T(8,128)(2,1)S(1)}, bf16[32,4224]{1,0:T(8,128)(2,1)S(1)}, u32[]{:S(2)}, u32[]{:S(2)}) collective-permute-start(bf16[32,4224]{1,0:T(8,128)(2,1)S(1)} %pad_maximum_fusion), channel_id=1, source_target_pairs={{0,2},{1,3},{2,0},{3,1},{4,6},{5,7},{6,4},{7,5},{8,10},{9,11},{10,... | collective-permute-start | bytes 811016 | tf_op jit(solution)/shard_map/ppermute | solution.py:13
  15.3 8.3 %collective-permute-start.3 = (bf16[32,4224]{1,0:T(8,128)(2,1)S(1)}, bf16[32,4224]{1,0:T(8,128)(2,1)S(1)}, u32[]{:S(2)}, u32[]{:S(2)}) collective-permute-start(bf16[32,4224]{1,0:T(8,128)(2,1)S(1)} %pad_maximum_fusion), channel_id=1, source_target_pairs={{0,1},{1,0},{2,3},{3,2},{4,5},{5,4},{6,7},{7,6},{8,9},{9,8},{10,11... | collective-permute-start | bytes 811016 | tf_op jit(solution)/shard_map/ppermute | solution.py:13
  21.8 5.0 %collective-permute-start.5 = (bf16[32,2048]{1,0:T(8,128)(2,1)S(1)}, bf16[32,2048]{1,0:T(8,128)(2,1)S(1)}, u32[]{:S(2)}, u32[]{:S(2)}) collective-permute-start(bf16[32,2048]{1,0:T(8,128)(2,1)S(1)} %slice.84), channel_id=1, source_target_pairs={{0,1},{1,0},{2,3},{3,2},{4,5},{5,4},{6,7},{7,6},{8,9},{9,8},{10,11... | collective-permute-start | bytes 393224 | tf_op jit(solution)/shard_map/ppermute | solution.py:13
  23.6 5.1 %collective-permute-start.6 = (bf16[32,2176]{1,0:T(8,128)(2,1)S(1)}, bf16[32,2176]{1,0:T(8,128)(2,1)S(1)}, u32[]{:S(2)}, u32[]{:S(2)}) collective-permute-start(bf16[32,2176]{1,0:T(8,128)(2,1)S(1)} %slice.85), channel_id=1, source_target_pairs={{0,2},{1,3},{2,0},{3,1},{4,6},{5,7},{6,4},{7,5},{8,10},{9,11},{10,... | collective-permute-start | bytes 417800 | tf_op jit(solution)/shard_map/ppermute | solution.py:13
  29.4 3.0 %collective-permute-start.7 = (bf16[128,4224]{1,0:T(8,128)(2,1)}, bf16[128,4224]{1,0:T(8,128)(2,1)}, u32[]{:S(2)}, u32[]{:S(2)}) collective-permute-start(bf16[128,4224]{1,0:T(8,128)(2,1)} %maximum_dynamic-update-slice_fusion), channel_id=1, source_target_pairs={{0,16},{16,0},{1,17},{17,1},{2,18},{18,2},{3,19},{19,3},{4,20},{20... | collective-permute-start | bytes 3244040 | tf_op jit(solution)/shard_map/ppermute | solution.py:13
  40.9 3.1 %collective-permute-start.8 = (bf16[128,4096]{1,0:T(8,128)(2,1)}, bf16[128,4096]{1,0:T(8,128)(2,1)}, u32[]{:S(2)}, u32[]{:S(2)}) collective-permute-start(bf16[128,4096]{1,0:T(8,128)(2,1)} %multiply_convert_fusion), channel_id=1, source_target_pairs={{0,16},{16,0},{1,17},{17,1},{2,18},{18,2},{3,19},{19,3},{4,20},{20... | collective-permute-start | bytes 3145736 | tf_op jit(solution)/shard_map/ppermute | solution.py:13
  50.8 5.8 %collective-permute-start.9 = (bf16[32,2048]{1,0:T(8,128)(2,1)S(1)}, bf16[32,2048]{1,0:T(8,128)(2,1)S(1)}, u32[]{:S(2)}, u32[]{:S(2)}) collective-permute-start(bf16[32,2048]{1,0:T(8,128)(2,1)S(1)} %get-tuple-element.11), channel_id=1, source_target_pairs={{0,2},{1,3},{2,0},{3,1},{4,6},{5,7},{6,4},{7,5},{8,10},{9,11},{10,... | collective-permute-start | bytes 393224 | tf_op jit(solution)/shard_map/ppermute | solution.py:13
  52.3 5.5 %collective-permute-start.11 = (bf16[32,2048]{1,0:T(8,128)(2,1)S(1)}, bf16[32,2048]{1,0:T(8,128)(2,1)S(1)}, u32[]{:S(2)}, u32[]{:S(2)}) collective-permute-start(bf16[32,2048]{1,0:T(8,128)(2,1)S(1)} %get-tuple-element.12), channel_id=1, source_target_pairs={{0,1},{1,0},{2,3},{3,2},{4,5},{5,4},{6,7},{7,6},{8,9},{9,8},{10,11... | collective-permute-start | bytes 393224 | tf_op jit(solution)/shard_map/ppermute | solution.py:13
  58.9 7.5 %collective-permute-start.12 = (bf16[32,4096]{1,0:T(8,128)(2,1)S(1)}, bf16[32,4096]{1,0:T(8,128)(2,1)S(1)}, u32[]{:S(2)}, u32[]{:S(2)}) collective-permute-start(bf16[32,4096]{1,0:T(8,128)(2,1)S(1)} %pad_maximum_fusion.2), channel_id=1, source_target_pairs={{0,2},{1,3},{2,0},{3,1},{4,6},{5,7},{6,4},{7,5},{8,10},{9,11},{10,... | collective-permute-start | bytes 786440 | tf_op jit(solution)/shard_map/ppermute | solution.py:13
  59.5 7.3 %collective-permute-start.10 = (bf16[32,4096]{1,0:T(8,128)(2,1)S(1)}, bf16[32,4096]{1,0:T(8,128)(2,1)S(1)}, u32[]{:S(2)}, u32[]{:S(2)}) collective-permute-start(bf16[32,4096]{1,0:T(8,128)(2,1)S(1)} %pad_maximum_fusion.1), channel_id=1, source_target_pairs={{0,1},{1,0},{2,3},{3,2},{4,5},{5,4},{6,7},{7,6},{8,9},{9,8},{10,11... | collective-permute-start | bytes 786440 | tf_op jit(solution)/shard_map/ppermute | solution.py:13
  68.0 5.0 %collective-permute-start.13 = (bf16[8,4096]{1,0:T(8,128)(2,1)S(1)}, bf16[8,4096]{1,0:T(8,128)(2,1)S(1)}, u32[]{:S(2)}, u32[]{:S(2)}) collective-permute-start(bf16[8,4096]{1,0:T(8,128)(2,1)S(1)} %get-tuple-element.15), channel_id=1, source_target_pairs={{0,4},{1,5},{2,6},{3,7},{4,0},{5,1},{6,2},{7,3},{8,12},{9,13},{10,... | collective-permute-start | bytes 196616 | tf_op jit(solution)/shard_map/ppermute | solution.py:13
  68.3 6.2 %collective-permute-start.15 = (bf16[8,4096]{1,0:T(8,128)(2,1)S(1)}, bf16[8,4096]{1,0:T(8,128)(2,1)S(1)}, u32[]{:S(2)}, u32[]{:S(2)}) collective-permute-start(bf16[8,4096]{1,0:T(8,128)(2,1)S(1)} %get-tuple-element.16), channel_id=1, source_target_pairs={{0,12},{1,13},{2,14},{3,15},{4,8},{5,9},{6,10},{7,11},{8,4},{9,5},... | collective-permute-start | bytes 196616 | tf_op jit(solution)/shard_map/ppermute | solution.py:13
  70.1 5.9 %collective-permute-start.14 = (bf16[8,4096]{1,0:T(8,128)(2,1)S(1)}, bf16[8,4096]{1,0:T(8,128)(2,1)S(1)}, u32[]{:S(2)}, u32[]{:S(2)}) collective-permute-start(bf16[8,4096]{1,0:T(8,128)(2,1)S(1)} %get-tuple-element.17), channel_id=1, source_target_pairs={{0,8},{1,9},{2,10},{3,11},{4,12},{5,13},{6,14},{7,15},{8,0},{9,1},... | collective-permute-start | bytes 196616 | tf_op jit(solution)/shard_map/ppermute | solution.py:13

commit v2 on v1

--- a/solution.py
+++ b/solution.py
@@ -1,4 +1,5 @@
 import functools
+import math
 
 import jax
 import jax.numpy as jnp
@@ -48,57 +49,192 @@
         out_shape=jax.ShapeDtypeStruct((count, width + extra), jnp.bfloat16),
         in_specs=[vmem, vmem, vmem, vmem, pl.BlockSpec(memory_space=pltpu.SMEM)],
         out_specs=vmem,
+        compiler_params=pltpu.CompilerParams(vmem_limit_bytes=LIMIT),
     )(tokens, norm_gain, expert_ids, route_weight, placement)
 
 
-def hidden_rows(rows, w_gate, w_up):
-    gate = jnp.dot(rows, w_gate, preferred_element_type=jnp.float32)
-    upward = jnp.dot(rows, w_up, preferred_element_type=jnp.float32)
-    return (jax.nn.silu(gate) * upward).astype(jnp.bfloat16)
+VMEM = pl.BlockSpec(memory_space=pltpu.VMEM)
+LIMIT = 56 * 1024 * 1024
+ROOM = int(53.0 * 1024 * 1024)
+
+
+def local_call(kernel, outs, *operands, hint=0):
+    held = sum(math.prod(x.shape) * x.dtype.itemsize for x in operands)
+    held += sum(math.prod(shape) * jnp.dtype(dtype).itemsize for shape, dtype in outs)
+    return pl.pallas_call(
+        kernel,
+        out_shape=[jax.ShapeDtypeStruct(shape, dtype) for shape, dtype in outs],
+        in_specs=[VMEM] * len(operands),
+        out_specs=[VMEM] * len(outs),
+        compiler_params=pltpu.CompilerParams(vmem_limit_bytes=min(LIMIT, 2 * held + (1 << 21))),
+        cost_estimate=pl.CostEstimate(flops=0, bytes_accessed=hint or held, transcendentals=0),
+    )(*operands)
+
+
+def stack_kernel(*refs):
+    out_ref = refs[-1]
+    start = 0
+    for ref in refs[:-1]:
+        out_ref[start : start + ref.shape[0]] = ref[...]
+        start += ref.shape[0]
+
+
+def stack(*blocks):
+    if len(blocks) == 1:
+        return blocks[0]
+    rows = sum(block.shape[0] for block in blocks)
+    return local_call(
+        stack_kernel, [((rows, blocks[0].shape[1]), blocks[0].dtype)], *blocks, hint=8 << 20
+    )[0]
+
+
+def turn(block, first, second):
+    owners = lax.axis_size("dev")
+    route = []
+    for side, offset in enumerate((first, second)):
+        route += [(side * owners + i, side * owners + (i ^ offset)) for i in range(owners)]
+    return lax.ppermute(block, ("side", "dev"), route)
+
+
+def expert_kernel(
+    column_ref, near_ref, far_ref, mine_ref, other_ref, gate_ref, up_ref, down_ref,
+    away_ref, keep_ref,
+):
+    span = mine_ref.shape[0]
+    width = keep_ref.shape[1]
+    extra = column_ref.shape[1] - width
+    owners = lax.axis_size("dev")
+    me = lax.axis_index("dev")
+    step = min(width, 1024)
+
+    def rows(start, size):
+        columns = slice(start, start + size)
+        return jnp.concatenate(
+            [
+                other_ref[:, columns],
+                far_ref[:, columns],
+                column_ref[span:, columns],
+                mine_ref[:, columns],
+                near_ref[:, columns],
+                column_ref[:span, columns],
+            ]
+        )
+
+    gate = up = 0.0
+    for k in range(0, width, step):
+        part = rows(k, step)
+        gate += jnp.dot(part, gate_ref[0, k : k + step], preferred_element_type=jnp.float32)
+        up += jnp.dot(part, up_ref[0, k : k + step], preferred_element_type=jnp.float32)
+    hidden = (gate / (1.0 + jnp.exp(-gate)) * up).astype(jnp.bfloat16)
+    lane = lax.broadcasted_iota(jnp.int32, (1, extra), 1)
+    parts = rows(width, extra).astype(jnp.float32)
+    weight = jnp.sum(jnp.where(lax.rem(lane, owners) == me, parts, 0.0), axis=1, keepdims=True)
+    half = 4 * span
+    for k in range(0, width, step):
+        down = down_ref[0, :, k : k + step]
+        value = jnp.dot(hidden, down, preferred_element_type=jnp.float32) * weight
+        away_ref[:, k : k + step] = value[:half].astype(jnp.bfloat16)
+        keep_ref[:, k : k + step] = value[half:]
+
+
+def corner_kernel(keep_ref, got_ref, out_ref):
+    span = out_ref.shape[0]
+    out_ref[...] = (keep_ref[:span] + got_ref[:span].astype(jnp.float32)).astype(jnp.bfloat16)
+
+
+def near_kernel(keep_ref, got_ref, corner_ref, out_ref):
+    span = corner_ref.shape[0]
+    total = keep_ref[span : 3 * span] + got_ref[span : 3 * span].astype(jnp.float32)
+    out_ref[:span] = (total[:span] + corner_ref[...].astype(jnp.float32)).astype(jnp.bfloat16)
+    out_ref[span:] = total[span:].astype(jnp.bfloat16)
+
+
+def column_kernel(keep_ref, got_ref, near_ref, other_ref, *out_refs):
+    count = out_refs[0].shape[0]
+    base = 3 * other_ref.shape[0]
+    for i, out_ref in enumerate(out_refs):
+        rows = slice(i * count, (i + 1) * count)
+        kept = slice(base + i * count, base + (i + 1) * count)
+        total = keep_ref[kept] + got_ref[kept].astype(jnp.float32)
+        total = total + near_ref[rows].astype(jnp.float32) + other_ref[rows].astype(jnp.float32)
+        out_ref[...] = total.astype(out_ref.dtype)
+
+
+def finish_kernel(first_ref, *refs):
+    total = first_ref[...]
+    for ref in refs[:-1]:
+        total = total + ref[...].astype(jnp.float32)
+    refs[-1][...] = total.astype(jnp.bfloat16)
+
+
+def load_kernel(*refs):
+    count = len(refs) // 2
+    sources, targets, sem = refs[:count], refs[count:-1], refs[-1]
+    copies = [pltpu.make_async_copy(*pair, sem.at[i]) for i, pair in enumerate(zip(sources, targets))]
+    for copy in copies:
+        copy.start()
+    for copy in copies:
+        copy.wait()
+
+
+def load(*arrays):
+    held = sum(math.prod(x.shape) * x.dtype.itemsize for x in arrays)
+    return pl.pallas_call(
+        load_kernel,
+        out_shape=[jax.ShapeDtypeStruct(x.shape, x.dtype) for x in arrays],
+        in_specs=[pl.BlockSpec(memory_space=pl.ANY)] * len(arrays),
+        out_specs=[VMEM] * len(arrays),
+        scratch_shapes=[pltpu.SemaphoreType.DMA((len(arrays),))],
+        compiler_params=pltpu.CompilerParams(vmem_limit_bytes=ROOM - held),
+        cost_estimate=pl.CostEstimate(flops=0, bytes_accessed=2 * held, transcendentals=0),
+    )(*arrays)
 
 
 def body(tokens, norm_gain, expert_ids, route_weight, placement, w_gate, w_up, w_down):
     count, width = tokens.shape
     owners = lax.axis_size("dev")
-    me = lax.axis_index("dev")
-    half = width // 2
     extra = -(-3 * owners // 128) * 128
+    bf16, f32 = jnp.bfloat16, jnp.float32
     packed = prepare(tokens, norm_gain, expert_ids, route_weight, placement, owners, extra)
-    cold = list(range(4, owners, 4))
-    column = jnp.concatenate([packed] + [swap(packed, "dev", r) for r in cold])
-    span = column.shape[0]
-    along_x = swap(column, "dev", 1)
-    along_y = swap(column, "dev", 2)
-    diag = jnp.concatenate(
-        [swap(along_y[:, :half], "dev", 1), swap(along_x[:, half:], "dev", 2)], axis=1
-    )
-    own = jnp.concatenate([column, along_x, along_y, diag])
-    other = swap(own, "side", 1)
-
-    def routed(rows):
-        chosen = lax.rem(lax.broadcasted_iota(jnp.int32, (1, extra), 1), owners) == me
-        weight = jnp.sum(
-            jnp.where(chosen, rows[:, width:].astype(jnp.float32), 0.0), axis=1, keepdims=True
+    offsets = list(range(0, owners, 4))
+    odd = [r for r in offsets if r // 4 % 2 == 1]
+    even = [r for r in offsets if r // 4 % 2 == 0]
+    groups = [group for group in (even, odd) if group]
+    blocks = {r: swap(packed, "dev", r) for group in groups for r in group if r}
+    *weights, blocks[0] = load(w_gate, w_up, w_down, packed)
+    blocks, weights = lax.optimization_barrier((blocks, weights))
+    pieces = []
+    for group in groups:
+        mine = stack(*[blocks[r] for r in group])
+        span = mine.shape[0]
+        column = stack(mine, swap(mine, "side", 1))
+        near = turn(column, 1, 2)
+        corner = turn(near[:span], 2, 1)
+        far = swap(near, "side", 1)
+        if pieces:
+            corner = lax.optimization_barrier((corner, pieces[-1]))[0]
+        pieces.append(
+            local_call(
+                expert_kernel,
+                [((4 * span, width), bf16), ((4 * span, width), f32)],
+                column, near, far, corner, swap(corner, "side", 1), *weights,
+            )
         )
-        hidden = hidden_rows(rows[:, :width], w_gate[0], w_up[0])
-        return jnp.dot(hidden, w_down[0], preferred_element_type=jnp.float32) * weight
-
-    away = routed(other).astype(jnp.bfloat16)
-    total = routed(own) + swap(away, "side", 1).astype(jnp.float32)
-    s_own, s_x, s_y, s_diag = (total[i * span : (i + 1) * span] for i in range(4))
-
-    def send(value, offset):
-        return swap(value.astype(jnp.bfloat16), "dev", offset).astype(jnp.float32)
-
-    from_y = send(s_diag[:, :half], 2)
-    from_x = send(s_diag[:, half:], 1)
-    s_x = jnp.concatenate([s_x[:, :half] + from_y, s_x[:, half:]], axis=1)
-    s_y = jnp.concatenate([s_y[:, :half], s_y[:, half:] + from_x], axis=1)
-    column_sum = s_own + send(s_x, 1) + send(s_y, 2)
-    result = column_sum[:count]
-    for i, r in enumerate(cold):
-        result = result + send(column_sum[(i + 1) * count : (i + 2) * count], r)
-    return result.astype(jnp.bfloat16)
+    sums = {}
+    for group, (away, keep) in zip(groups, pieces):
+        span = len(group) * count
+        got = swap(away, "side", 1)
+        corner = turn(local_call(corner_kernel, [((span, width), bf16)], keep, got)[0], 2, 1)
+        near = local_call(near_kernel, [((2 * span, width), bf16)], keep, got, corner)[0]
+        near = turn(near, 1, 2)
+        totals = local_call(
+            column_kernel,
+            [((count, width), bf16 if r else f32) for r in group],
+            keep, got, near, swap(near[span:], "side", 1),
+        )
+        for r, total in zip(group, totals):
+            sums[r] = swap(total, "dev", r) if r else total
+    return local_call(finish_kernel, [((count, width), bf16)], *[sums[r] for r in sorted(sums)])[0]
 
 
 def solution(mesh):

time: 77.1 us -> 59.8 us (0.78)
  matrix products: 16.1 us -> 0 us
  Pallas kernels: 1.79 us -> 10.3 us
  other arithmetic: 5.42 us -> 0 us
  local copies, waits for them, and re-layouts: 6.08 us -> 0.99 us
  starting transfers between devices: 19.7 us -> 23.4 us
  waiting for transfers between devices: 27.5 us -> 24.7 us
    ppermute x16, waiting for transfers between devices: 27.5 us -> 9.8 us  [swap(): return lax.ppermute(block, axis, [(i, i ^ offset) for i in range(count)])]
    dot_general x4 -> x0, matrix products: 16.1 us -> none  [the longest x2 10.2 us: routed(): jnp.dot(hidden, w_down[0], preferred_element_type=jnp.float32) * weight]
    ppermute x0 -> x8, waiting for transfers between devices: none -> 14.9 us  [turn(): return lax.ppermute(block, ('side', 'dev'), route)]
    ppermute x0 -> x8, starting transfers between devices: none -> 12.1 us  [turn(): return lax.ppermute(block, ('side', 'dev'), route)]
    pallas_call x0 -> x14, Pallas kernels: none -> 8.7 us  [the longest x13 4.91 us: local_call(): pl.pallas_call(kernel, out_shape=[jax.ShapeDtypeStruct(shape, dtype) for...]
    ppermute x16, starting transfers between devices: 19.7 us -> 11.3 us  [swap(): return lax.ppermute(block, axis, [(i, i ^ offset) for i in range(count)])]
    unnamed x8 -> x2, local copies, waits for them, and re-layouts: 4.91 us -> 0.95 us
    another operation x2 -> x0, other arithmetic: 2.21 us -> none
  transfers between devices with their start and end apart: 16 -> 24, of which waited for: 13 -> 16; matrix products, arithmetic and copies ran while one was open for 10% -> 0% of each run, Pallas kernels for 0% -> 13%
where the time goes in v2:
time: 59.8 us; the launch traced here: 59.6 us
  waiting for transfers between devices  24.7 us (41%)
  starting transfers between devices  23.4 us (39%)
  Pallas kernels  10.3 us (17%)
  local copies, waits for them, and re-layouts  0.99 us (2%)
    ppermute x8, waiting for transfers between devices, turn(): return lax.ppermute(block, ('side', 'dev'), route)  14.9 us
    ppermute x8, starting transfers between devices, turn(): return lax.ppermute(block, ('side', 'dev'), route)  12.1 us
    ppermute x16, starting transfers between devices, swap(): return lax.ppermute(block, axis, [(i, i ^ offset) for i in range(count)])  11.3 us
    ppermute x16, waiting for transfers between devices, swap(): return lax.ppermute(block, axis, [(i, i ^ offset) for i in range(count)])  9.8 us
    pallas_call x13, Pallas kernels, local_call(): pl.pallas_call(kernel, out_shape=[jax.ShapeDtypeStruct(shape, dtype) for...  4.91 us
    pallas_call x1, Pallas kernels, load(): pl.pallas_call(load_kernel, out_shape=[jax.ShapeDtypeStruct(x.shape, x.dt...  3.79 us
    pallas_call x1, Pallas kernels, prepare(): pl.pallas_call(functools.partial(prepare_kernel, slots), out_shape=jax.Sh...  1.63 us
  transfers between devices with their start and end apart: 24, of which 16 were waited for; matrix products, arithmetic and copies ran while one was open for 0% of the time, Pallas kernels for 13%

profile of v2, /device:TPU:0, one launch (start us, length us, event | category | flops | bytes accessed | tf_op | source)
XLA Modules:
  0.0 59.6 jit_solution(10283772361174790176)
XLA Ops:
  0.0 1.6 %shard_map.82.refs_3_ = bf16[8,4224]{1,0:T(8,128)(2,1)} custom-call(bf16[8,4096]{1,0:T(8,128)(2,1)} %tok_ref.1, f32[4096]{0:T(1024)} %gain_ref.1, s32[8,8]{1,0:T(8,128)} %ids_ref.1, f32[8,8]{1,0:T(8,128)} %weight_ref.1, s32[16]{0:T(128)} %placement_ref.1), custom_call_target="tpu_custom_call" | custom-call | tf_op jit(solution)/shard_map/pallas_call | solution.py:47
  1.6 3.0 %collective-permute-start = (bf16[8,4224]{1,0:T(8,128)(2,1)}, bf16[8,4224]{1,0:T(8,128)(2,1)S(1)}, u32[]{:S(2)}, u32[]{:S(2)}) collective-permute-start(bf16[8,4224]{1,0:T(8,128)(2,1)} %shard_map.82.refs_3_), channel_id=1, source_target_pairs={{0,4},{1,5},{2,6},{3,7},{4,0},{5,1},{6,2},{7,3},{8,12},{9,13},{10,... | collective-permute-start | bytes 202760 | tf_op jit(solution)/shard_map/ppermute | solution.py:14
  4.7 2.6 %collective-permute-start.1 = (bf16[8,4224]{1,0:T(8,128)(2,1)}, bf16[8,4224]{1,0:T(8,128)(2,1)S(1)}, u32[]{:S(2)}, u32[]{:S(2)}) collective-permute-start(bf16[8,4224]{1,0:T(8,128)(2,1)} %shard_map.82.refs_3_), channel_id=1, source_target_pairs={{0,8},{1,9},{2,10},{3,11},{4,12},{5,13},{6,14},{7,15},{8,0},{9,1},... | collective-permute-start | bytes 202760 | tf_op jit(solution)/shard_map/ppermute | solution.py:14
  7.2 0.0 collective-permute-start.2
  7.2 0.9 %copy-done = bf16[8,4224]{1,0:T(8,128)(2,1)S(1)} copy-done((bf16[8,4224]{1,0:T(8,128)(2,1)S(1)}, bf16[8,4224]{1,0:T(8,128)(2,1)}, u32[]{:S(2)}) %copy-start) | copy-done | bytes 67608
  8.2 3.8 %shard_map.83 = (bf16[1,4096,384]{2,1,0:T(8,128)(2,1)S(1)}, bf16[1,4096,384]{2,1,0:T(8,128)(2,1)S(1)}, bf16[1,384,4096]{2,1,0:T(8,128)(2,1)S(1)}, bf16[8,4224]{1,0:T(8,128)(2,1)S(1)}) custom-call(bf16[1,4096,384]{2,1,0:T(8,128)(2,1)} %refs_0_.1, bf16[1,4096,384]{2,1,0:T(8,128)(2,1)} %refs_1_.1, bf16[1,384,4096]{2,1,0:T(8,128)(2,1)} %refs_2_.1, ...), custom_call_target="tpu_custom_call" | custom-call | bytes 19009536 | tf_op jit(solution)/shard_map/pallas_call | solution.py:182
  12.0 0.0 collective-permute-done.refs_0_
  12.0 0.3 collective-permute-done.1.refs_1_
  12.3 1.4 %collective-permute-done.2.refs_1_ = bf16[8,4224]{1,0:T(8,128)(2,1)S(1)} collective-permute-done((bf16[8,4224]{1,0:T(8,128)(2,1)}, bf16[8,4224]{1,0:T(8,128)(2,1)S(1)}, u32[]{:S(2)}, u32[]{:S(2)}) %collective-permute-start.2) | collective-permute-done | bytes 67616 | tf_op jit(solution)/shard_map/ppermute | solution.py:14
  13.7 0.1 collective-permute-start.3
  13.7 1.3 %collective-permute-done.3.refs_1_ = bf16[16,4224]{1,0:T(8,128)(2,1)S(1)} collective-permute-done((bf16[16,4224]{1,0:T(8,128)(2,1)S(1)}, bf16[16,4224]{1,0:T(8,128)(2,1)S(1)}, u32[]{:S(2)}, u32[]{:S(2)}) %collective-permute-start.3) | collective-permute-done | bytes 135200 | tf_op jit(solution)/shard_map/ppermute | solution.py:14
  15.1 1.6 %collective-permute-start.4 = (bf16[32,4224]{1,0:T(8,128)(2,1)S(1)}, bf16[32,4224]{1,0:T(8,128)(2,1)S(1)}, u32[]{:S(2)}, u32[]{:S(2)}) collective-permute-start(bf16[32,4224]{1,0:T(8,128)(2,1)S(1)} %shard_map.85.column_ref), channel_id=1, source_target_pairs={{0,1},{1,0},{2,3},{3,2},{4,5},{5,4},{6,7},{7,6},{8,9},{9,8},{10,11... | collective-permute-start | bytes 811016 | tf_op jit(solution)/shard_map/ppermute | solution.py:96
  16.7 0.1 collective-permute-start.12
  16.7 1.3 %collective-permute-done.12.refs_1_ = bf16[16,4224]{1,0:T(8,128)(2,1)S(1)} collective-permute-done((bf16[16,4224]{1,0:T(8,128)(2,1)S(1)}, bf16[16,4224]{1,0:T(8,128)(2,1)S(1)}, u32[]{:S(2)}, u32[]{:S(2)}) %collective-permute-start.12) | collective-permute-done | bytes 135200 | tf_op jit(solution)/shard_map/ppermute | solution.py:14
  18.1 1.1 %collective-permute-start.13 = (bf16[32,4224]{1,0:T(8,128)(2,1)S(1)}, bf16[32,4224]{1,0:T(8,128)(2,1)S(1)}, u32[]{:S(2)}, u32[]{:S(2)}) collective-permute-start(bf16[32,4224]{1,0:T(8,128)(2,1)S(1)} %shard_map.91.column_ref), channel_id=1, source_target_pairs={{0,1},{1,0},{2,3},{3,2},{4,5},{5,4},{6,7},{7,6},{8,9},{9,8},{10,11... | collective-permute-start | bytes 811016 | tf_op jit(solution)/shard_map/ppermute | solution.py:96
  19.2 2.4 %collective-permute-done.4.near_ref = bf16[32,4224]{1,0:T(8,128)(2,1)S(1)} collective-permute-done((bf16[32,4224]{1,0:T(8,128)(2,1)S(1)}, bf16[32,4224]{1,0:T(8,128)(2,1)S(1)}, u32[]{:S(2)}, u32[]{:S(2)}) %collective-permute-start.4) | collective-permute-done | bytes 270368 | tf_op jit(solution)/shard_map/ppermute | solution.py:96
  21.6 1.6 %collective-permute-start.6 = (bf16[16,4224]{1,0:T(8,128)(2,1)S(1)}, bf16[16,4224]{1,0:T(8,128)(2,1)S(1)}, u32[]{:S(2)}, u32[]{:S(2)}) collective-permute-start(bf16[16,4224]{1,0:T(8,128)(2,1)S(1)} %slice.16), channel_id=1, source_target_pairs={{0,2},{1,3},{2,0},{3,1},{4,6},{5,7},{6,4},{7,5},{8,10},{9,11},{10,... | collective-permute-start | bytes 405512 | tf_op jit(solution)/shard_map/ppermute | solution.py:96
  23.2 3.5 %collective-permute-done.6.mine_ref = bf16[16,4224]{1,0:T(8,128)(2,1)S(1)} collective-permute-done((bf16[16,4224]{1,0:T(8,128)(2,1)S(1)}, bf16[16,4224]{1,0:T(8,128)(2,1)S(1)}, u32[]{:S(2)}, u32[]{:S(2)}) %collective-permute-start.6) | collective-permute-done | bytes 135200 | tf_op jit(solution)/shard_map/ppermute | solution.py:96
  26.7 1.6 %collective-permute-start.15 = (bf16[16,4224]{1,0:T(8,128)(2,1)S(1)}, bf16[16,4224]{1,0:T(8,128)(2,1)S(1)}, u32[]{:S(2)}, u32[]{:S(2)}) collective-permute-start(bf16[16,4224]{1,0:T(8,128)(2,1)S(1)} %slice.18), channel_id=1, source_target_pairs={{0,2},{1,3},{2,0},{3,1},{4,6},{5,7},{6,4},{7,5},{8,10},{9,11},{10,... | collective-permute-start | bytes 405512 | tf_op jit(solution)/shard_map/ppermute | solution.py:96
  28.3 0.2 collective-permute-start.14
  28.5 1.9 %shard_map.86 = (bf16[64,4096]{1,0:T(8,128)(2,1)S(1)}, f32[64,4096]{1,0:T(8,128)S(1)}) custom-call(bf16[32,4224]{1,0:T(8,128)(2,1)S(1)} %shard_map.85.column_ref, bf16[32,4224]{1,0:T(8,128)(2,1)S(1)} %collective-permute-done.4.near_ref, bf16[32,4224]{1,0:T(8,128)(2,1)S(1)} %collective-permute-done.5.far_ref, ...), custom_call_target="tpu_custom_call" | custom-call | bytes 12091392 | tf_op jit(solution)/shard_map/pallas_call | solution.py:64
  30.5 1.3 %collective-permute-done.15.mine_ref = bf16[16,4224]{1,0:T(8,128)(2,1)S(1)} collective-permute-done((bf16[16,4224]{1,0:T(8,128)(2,1)S(1)}, bf16[16,4224]{1,0:T(8,128)(2,1)S(1)}, u32[]{:S(2)}, u32[]{:S(2)}) %collective-permute-start.15) | collective-permute-done | bytes 135200 | tf_op jit(solution)/shard_map/ppermute | solution.py:96
  31.8 0.5 collective-permute-start.8
  32.3 0.8 %collective-permute-done.16.other_ref = bf16[16,4224]{1,0:T(8,128)(2,1)S(1)} collective-permute-done((bf16[16,4224]{1,0:T(8,128)(2,1)S(1)}, bf16[16,4224]{1,0:T(8,128)(2,1)S(1)}, u32[]{:S(2)}, u32[]{:S(2)}) %collective-permute-start.16) | collective-permute-done | bytes 135200 | tf_op jit(solution)/shard_map/ppermute | solution.py:14
  33.2 1.9 %shard_map.92 = (bf16[64,4096]{1,0:T(8,128)(2,1)S(1)}, f32[64,4096]{1,0:T(8,128)S(1)}) custom-call(bf16[32,4224]{1,0:T(8,128)(2,1)S(1)} %shard_map.91.column_ref, bf16[32,4224]{1,0:T(8,128)(2,1)S(1)} %collective-permute-done.13.near_ref, bf16[32,4224]{1,0:T(8,128)(2,1)S(1)} %collective-permute-done.14.far_ref, ...), custom_call_target="tpu_custom_call" | custom-call | bytes 12091392 | tf_op jit(solution)/shard_map/pallas_call | solution.py:64
  35.1 0.2 collective-permute-start.17
  35.4 1.6 %collective-permute-start.9 = (bf16[16,4096]{1,0:T(8,128)(2,1)S(1)}, bf16[16,4096]{1,0:T(8,128)(2,1)S(1)}, u32[]{:S(2)}, u32[]{:S(2)}) collective-permute-start(bf16[16,4096]{1,0:T(8,128)(2,1)S(1)} %shard_map.87), channel_id=1, source_target_pairs={{0,2},{1,3},{2,0},{3,1},{4,6},{5,7},{6,4},{7,5},{8,10},{9,11},{10,... | collective-permute-start | bytes 393224 | tf_op jit(solution)/shard_map/ppermute | solution.py:96
  36.9 0.1 collective-permute-done.17.got_ref
  37.1 1.6 %collective-permute-start.18 = (bf16[16,4096]{1,0:T(8,128)(2,1)S(1)}, bf16[16,4096]{1,0:T(8,128)(2,1)S(1)}, u32[]{:S(2)}, u32[]{:S(2)}) collective-permute-start(bf16[16,4096]{1,0:T(8,128)(2,1)S(1)} %shard_map.93), channel_id=1, source_target_pairs={{0,2},{1,3},{2,0},{3,1},{4,6},{5,7},{6,4},{7,5},{8,10},{9,11},{10,... | collective-permute-start | bytes 393224 | tf_op jit(solution)/shard_map/ppermute | solution.py:96
  38.7 1.7 %collective-permute-done.9.corner_ref = bf16[16,4096]{1,0:T(8,128)(2,1)S(1)} collective-permute-done((bf16[16,4096]{1,0:T(8,128)(2,1)S(1)}, bf16[16,4096]{1,0:T(8,128)(2,1)S(1)}, u32[]{:S(2)}, u32[]{:S(2)}) %collective-permute-start.9) | collective-permute-done | bytes 131104 | tf_op jit(solution)/shard_map/ppermute | solution.py:96
  40.4 0.1 shard_map.88
  40.5 1.6 %collective-permute-start.10 = (bf16[32,4096]{1,0:T(8,128)(2,1)S(1)}, bf16[32,4096]{1,0:T(8,128)(2,1)S(1)}, u32[]{:S(2)}, u32[]{:S(2)}) collective-permute-start(bf16[32,4096]{1,0:T(8,128)(2,1)S(1)} %shard_map.88), channel_id=1, source_target_pairs={{0,1},{1,0},{2,3},{3,2},{4,5},{5,4},{6,7},{7,6},{8,9},{9,8},{10,11... | collective-permute-start | bytes 786440 | tf_op jit(solution)/shard_map/ppermute | solution.py:96
  42.0 0.1 collective-permute-done.18.corner_ref
  42.2 0.1 shard_map.94
  42.2 1.6 %collective-permute-start.19 = (bf16[32,4096]{1,0:T(8,128)(2,1)S(1)}, bf16[32,4096]{1,0:T(8,128)(2,1)S(1)}, u32[]{:S(2)}, u32[]{:S(2)}) collective-permute-start(bf16[32,4096]{1,0:T(8,128)(2,1)S(1)} %shard_map.94), channel_id=1, source_target_pairs={{0,1},{1,0},{2,3},{3,2},{4,5},{5,4},{6,7},{7,6},{8,9},{9,8},{10,11... | collective-permute-start | bytes 786440 | tf_op jit(solution)/shard_map/ppermute | solution.py:96
  43.8 3.1 %collective-permute-done.10.near_ref = bf16[32,4096]{1,0:T(8,128)(2,1)S(1)} collective-permute-done((bf16[32,4096]{1,0:T(8,128)(2,1)S(1)}, bf16[32,4096]{1,0:T(8,128)(2,1)S(1)}, u32[]{:S(2)}, u32[]{:S(2)}) %collective-permute-start.10) | collective-permute-done | bytes 262176 | tf_op jit(solution)/shard_map/ppermute | solution.py:96
  46.9 0.1 collective-permute-start.11
  47.0 2.7 %collective-permute-done.19.near_ref = bf16[32,4096]{1,0:T(8,128)(2,1)S(1)} collective-permute-done((bf16[32,4096]{1,0:T(8,128)(2,1)S(1)}, bf16[32,4096]{1,0:T(8,128)(2,1)S(1)}, u32[]{:S(2)}, u32[]{:S(2)}) %collective-permute-start.19) | collective-permute-done | bytes 262176 | tf_op jit(solution)/shard_map/ppermute | solution.py:96
  49.7 0.1 collective-permute-start.20
  49.8 0.1 shard_map.89
  49.9 1.7 %collective-permute-start.22 = (bf16[8,4096]{1,0:T(8,128)(2,1)S(1)}, bf16[8,4096]{1,0:T(8,128)(2,1)S(1)}, u32[]{:S(2)}, u32[]{:S(2)}) collective-permute-start(bf16[8,4096]{1,0:T(8,128)(2,1)S(1)} %get-tuple-element.43), channel_id=1, source_target_pairs={{0,8},{1,9},{2,10},{3,11},{4,12},{5,13},{6,14},{7,15},{8,0},{9,1},... | collective-permute-start | bytes 196616 | tf_op jit(solution)/shard_map/ppermute | solution.py:14
  51.6 0.1 shard_map.95
  51.6 1.2 %collective-permute-start.21 = (bf16[8,4096]{1,0:T(8,128)(2,1)S(1)}, bf16[8,4096]{1,0:T(8,128)(2,1)S(1)}, u32[]{:S(2)}, u32[]{:S(2)}) collective-permute-start(bf16[8,4096]{1,0:T(8,128)(2,1)S(1)} %get-tuple-element.42), channel_id=1, source_target_pairs={{0,4},{1,5},{2,6},{3,7},{4,0},{5,1},{6,2},{7,3},{8,12},{9,13},{10,... | collective-permute-start | bytes 196616 | tf_op jit(solution)/shard_map/ppermute | solution.py:14
  52.8 1.6 %collective-permute-start.23 = (bf16[8,4096]{1,0:T(8,128)(2,1)S(1)}, bf16[8,4096]{1,0:T(8,128)(2,1)S(1)}, u32[]{:S(2)}, u32[]{:S(2)}) collective-permute-start(bf16[8,4096]{1,0:T(8,128)(2,1)S(1)} %get-tuple-element.44), channel_id=1, source_target_pairs={{0,12},{1,13},{2,14},{3,15},{4,8},{5,9},{6,10},{7,11},{8,4},{9,5},... | collective-permute-start | bytes 196616 | tf_op jit(solution)/shard_map/ppermute | solution.py:14
  54.5 2.4 %collective-permute-done.22.refs_1_ = bf16[8,4096]{1,0:T(8,128)(2,1)S(1)} collective-permute-done((bf16[8,4096]{1,0:T(8,128)(2,1)S(1)}, bf16[8,4096]{1,0:T(8,128)(2,1)S(1)}, u32[]{:S(2)}, u32[]{:S(2)}) %collective-permute-start.22) | collective-permute-done | bytes 65568 | tf_op jit(solution)/shard_map/ppermute | solution.py:14
  56.9 0.3 collective-permute-done.21.refs_0_
  57.2 1.7 %collective-permute-done.23.refs_2_ = bf16[8,4096]{1,0:T(8,128)(2,1)S(1)} collective-permute-done((bf16[8,4096]{1,0:T(8,128)(2,1)S(1)}, bf16[8,4096]{1,0:T(8,128)(2,1)S(1)}, u32[]{:S(2)}, u32[]{:S(2)}) %collective-permute-start.23) | collective-permute-done | bytes 65568 | tf_op jit(solution)/shard_map/ppermute | solution.py:14
  58.9 0.7 %shard_map.96 = bf16[8,4096]{1,0:T(8,128)(2,1)} custom-call(f32[8,4096]{1,0:T(8,128)S(1)} %get-tuple-element.36.first_ref, bf16[8,4096]{1,0:T(8,128)(2,1)S(1)} %collective-permute-done.21.refs_0_, bf16[8,4096]{1,0:T(8,128)(2,1)S(1)} %collective-permute-done.22.refs_1_, bf16[8,4096]{1,0:T(8,128)(2,1)S(1)} %collective-permute-done.23.refs_2_), custom_call_target="tpu_custom_call" | custom-call | bytes 393216 | tf_op jit(solution)/shard_map/pallas_call | solution.py:64
  (21 shorter events, 0.2 us)
Async XLA Ops:
  1.6 10.4 %collective-permute-start = (bf16[8,4224]{1,0:T(8,128)(2,1)}, bf16[8,4224]{1,0:T(8,128)(2,1)S(1)}, u32[]{:S(2)}, u32[]{:S(2)}) collective-permute-start(bf16[8,4224]{1,0:T(8,128)(2,1)} %shard_map.82.refs_3_), channel_id=1, source_target_pairs={{0,4},{1,5},{2,6},{3,7},{4,0},{5,1},{6,2},{7,3},{8,12},{9,13},{10,... | collective-permute-start | bytes 202760 | tf_op jit(solution)/shard_map/ppermute | solution.py:14
  4.7 7.6 %collective-permute-start.1 = (bf16[8,4224]{1,0:T(8,128)(2,1)}, bf16[8,4224]{1,0:T(8,128)(2,1)S(1)}, u32[]{:S(2)}, u32[]{:S(2)}) collective-permute-start(bf16[8,4224]{1,0:T(8,128)(2,1)} %shard_map.82.refs_3_), channel_id=1, source_target_pairs={{0,8},{1,9},{2,10},{3,11},{4,12},{5,13},{6,14},{7,15},{8,0},{9,1},... | collective-permute-start | bytes 202760 | tf_op jit(solution)/shard_map/ppermute | solution.py:14
  7.2 6.4 %collective-permute-start.2 = (bf16[8,4224]{1,0:T(8,128)(2,1)}, bf16[8,4224]{1,0:T(8,128)(2,1)S(1)}, u32[]{:S(2)}, u32[]{:S(2)}) collective-permute-start(bf16[8,4224]{1,0:T(8,128)(2,1)} %shard_map.82.refs_3_), channel_id=1, source_target_pairs={{0,12},{1,13},{2,14},{3,15},{4,8},{5,9},{6,10},{7,11},{8,4},{9,5},... | collective-permute-start | bytes 202760 | tf_op jit(solution)/shard_map/ppermute | solution.py:14
  7.2 0.9 %copy-start = (bf16[8,4224]{1,0:T(8,128)(2,1)S(1)}, bf16[8,4224]{1,0:T(8,128)(2,1)}, u32[]{:S(2)}) copy-start(bf16[8,4224]{1,0:T(8,128)(2,1)} %shard_map.82.refs_3_) | copy-start | bytes 202756
  13.7 1.4 %collective-permute-start.3 = (bf16[16,4224]{1,0:T(8,128)(2,1)S(1)}, bf16[16,4224]{1,0:T(8,128)(2,1)S(1)}, u32[]{:S(2)}, u32[]{:S(2)}) collective-permute-start(bf16[16,4224]{1,0:T(8,128)(2,1)S(1)} %shard_map.84.refs_0_), channel_id=1, source_target_pairs={{0,16},{16,0},{1,17},{17,1},{2,18},{18,2},{3,19},{19,3},{4,20},{20... | collective-permute-start | bytes 405512 | tf_op jit(solution)/shard_map/ppermute | solution.py:14
  15.1 6.5 %collective-permute-start.4 = (bf16[32,4224]{1,0:T(8,128)(2,1)S(1)}, bf16[32,4224]{1,0:T(8,128)(2,1)S(1)}, u32[]{:S(2)}, u32[]{:S(2)}) collective-permute-start(bf16[32,4224]{1,0:T(8,128)(2,1)S(1)} %shard_map.85.column_ref), channel_id=1, source_target_pairs={{0,1},{1,0},{2,3},{3,2},{4,5},{5,4},{6,7},{7,6},{8,9},{9,8},{10,11... | collective-permute-start | bytes 811016 | tf_op jit(solution)/shard_map/ppermute | solution.py:96
  16.7 1.4 %collective-permute-start.12 = (bf16[16,4224]{1,0:T(8,128)(2,1)S(1)}, bf16[16,4224]{1,0:T(8,128)(2,1)S(1)}, u32[]{:S(2)}, u32[]{:S(2)}) collective-permute-start(bf16[16,4224]{1,0:T(8,128)(2,1)S(1)} %shard_map.90.refs_0_), channel_id=1, source_target_pairs={{0,16},{16,0},{1,17},{17,1},{2,18},{18,2},{3,19},{19,3},{4,20},{20... | collective-permute-start | bytes 405512 | tf_op jit(solution)/shard_map/ppermute | solution.py:14
  18.1 8.6 %collective-permute-start.13 = (bf16[32,4224]{1,0:T(8,128)(2,1)S(1)}, bf16[32,4224]{1,0:T(8,128)(2,1)S(1)}, u32[]{:S(2)}, u32[]{:S(2)}) collective-permute-start(bf16[32,4224]{1,0:T(8,128)(2,1)S(1)} %shard_map.91.column_ref), channel_id=1, source_target_pairs={{0,1},{1,0},{2,3},{3,2},{4,5},{5,4},{6,7},{7,6},{8,9},{9,8},{10,11... | collective-permute-start | bytes 811016 | tf_op jit(solution)/shard_map/ppermute | solution.py:96
  21.6 5.1 %collective-permute-start.6 = (bf16[16,4224]{1,0:T(8,128)(2,1)S(1)}, bf16[16,4224]{1,0:T(8,128)(2,1)S(1)}, u32[]{:S(2)}, u32[]{:S(2)}) collective-permute-start(bf16[16,4224]{1,0:T(8,128)(2,1)S(1)} %slice.16), channel_id=1, source_target_pairs={{0,2},{1,3},{2,0},{3,1},{4,6},{5,7},{6,4},{7,5},{8,10},{9,11},{10,... | collective-permute-start | bytes 405512 | tf_op jit(solution)/shard_map/ppermute | solution.py:96
  23.2 5.3 %collective-permute-start.5 = (bf16[32,4224]{1,0:T(8,128)(2,1)S(1)}, bf16[32,4224]{1,0:T(8,128)(2,1)S(1)}, u32[]{:S(2)}, u32[]{:S(2)}) collective-permute-start(bf16[32,4224]{1,0:T(8,128)(2,1)S(1)} %collective-permute-done.4.near_ref), channel_id=1, source_target_pairs={{0,16},{16,0},{1,17},{17,1},{2,18},{18,2},{3,19},{19,3},{4,20},{20... | collective-permute-start | bytes 811016 | tf_op jit(solution)/shard_map/ppermute | solution.py:14
  26.7 1.8 %collective-permute-start.7 = (bf16[16,4224]{1,0:T(8,128)(2,1)S(1)}, bf16[16,4224]{1,0:T(8,128)(2,1)S(1)}, u32[]{:S(2)}, u32[]{:S(2)}) collective-permute-start(bf16[16,4224]{1,0:T(8,128)(2,1)S(1)} %collective-permute-done.6.mine_ref), channel_id=1, source_target_pairs={{0,16},{16,0},{1,17},{17,1},{2,18},{18,2},{3,19},{19,3},{4,20},{20... | collective-permute-start | bytes 405512 | tf_op jit(solution)/shard_map/ppermute | solution.py:14
  26.7 5.1 %collective-permute-start.15 = (bf16[16,4224]{1,0:T(8,128)(2,1)S(1)}, bf16[16,4224]{1,0:T(8,128)(2,1)S(1)}, u32[]{:S(2)}, u32[]{:S(2)}) collective-permute-start(bf16[16,4224]{1,0:T(8,128)(2,1)S(1)} %slice.18), channel_id=1, source_target_pairs={{0,2},{1,3},{2,0},{3,1},{4,6},{5,7},{6,4},{7,5},{8,10},{9,11},{10,... | collective-permute-start | bytes 405512 | tf_op jit(solution)/shard_map/ppermute | solution.py:96
  28.3 4.0 %collective-permute-start.14 = (bf16[32,4224]{1,0:T(8,128)(2,1)S(1)}, bf16[32,4224]{1,0:T(8,128)(2,1)S(1)}, u32[]{:S(2)}, u32[]{:S(2)}) collective-permute-start(bf16[32,4224]{1,0:T(8,128)(2,1)S(1)} %collective-permute-done.13.near_ref), channel_id=1, source_target_pairs={{0,16},{16,0},{1,17},{17,1},{2,18},{18,2},{3,19},{19,3},{4,20},{20... | collective-permute-start | bytes 811016 | tf_op jit(solution)/shard_map/ppermute | solution.py:14
  31.8 1.4 %collective-permute-start.16 = (bf16[16,4224]{1,0:T(8,128)(2,1)S(1)}, bf16[16,4224]{1,0:T(8,128)(2,1)S(1)}, u32[]{:S(2)}, u32[]{:S(2)}) collective-permute-start(bf16[16,4224]{1,0:T(8,128)(2,1)S(1)} %collective-permute-done.15.mine_ref), channel_id=1, source_target_pairs={{0,16},{16,0},{1,17},{17,1},{2,18},{18,2},{3,19},{19,3},{4,20},{20... | collective-permute-start | bytes 405512 | tf_op jit(solution)/shard_map/ppermute | solution.py:14
  31.8 3.5 %collective-permute-start.8 = (bf16[64,4096]{1,0:T(8,128)(2,1)S(1)}, bf16[64,4096]{1,0:T(8,128)(2,1)S(1)}, u32[]{:S(2)}, u32[]{:S(2)}) collective-permute-start(bf16[64,4096]{1,0:T(8,128)(2,1)S(1)} %get-tuple-element.35), channel_id=1, source_target_pairs={{0,16},{16,0},{1,17},{17,1},{2,18},{18,2},{3,19},{19,3},{4,20},{20... | collective-permute-start | bytes 1572872 | tf_op jit(solution)/shard_map/ppermute | solution.py:14
  35.1 2.0 %collective-permute-start.17 = (bf16[64,4096]{1,0:T(8,128)(2,1)S(1)}, bf16[64,4096]{1,0:T(8,128)(2,1)S(1)}, u32[]{:S(2)}, u32[]{:S(2)}) collective-permute-start(bf16[64,4096]{1,0:T(8,128)(2,1)S(1)} %get-tuple-element.41), channel_id=1, source_target_pairs={{0,16},{16,0},{1,17},{17,1},{2,18},{18,2},{3,19},{19,3},{4,20},{20... | collective-permute-start | bytes 1572872 | tf_op jit(solution)/shard_map/ppermute | solution.py:14
  35.4 5.0 %collective-permute-start.9 = (bf16[16,4096]{1,0:T(8,128)(2,1)S(1)}, bf16[16,4096]{1,0:T(8,128)(2,1)S(1)}, u32[]{:S(2)}, u32[]{:S(2)}) collective-permute-start(bf16[16,4096]{1,0:T(8,128)(2,1)S(1)} %shard_map.87), channel_id=1, source_target_pairs={{0,2},{1,3},{2,0},{3,1},{4,6},{5,7},{6,4},{7,5},{8,10},{9,11},{10,... | collective-permute-start | bytes 393224 | tf_op jit(solution)/shard_map/ppermute | solution.py:96
  37.1 5.0 %collective-permute-start.18 = (bf16[16,4096]{1,0:T(8,128)(2,1)S(1)}, bf16[16,4096]{1,0:T(8,128)(2,1)S(1)}, u32[]{:S(2)}, u32[]{:S(2)}) collective-permute-start(bf16[16,4096]{1,0:T(8,128)(2,1)S(1)} %shard_map.93), channel_id=1, source_target_pairs={{0,2},{1,3},{2,0},{3,1},{4,6},{5,7},{6,4},{7,5},{8,10},{9,11},{10,... | collective-permute-start | bytes 393224 | tf_op jit(solution)/shard_map/ppermute | solution.py:96
  40.5 6.4 %collective-permute-start.10 = (bf16[32,4096]{1,0:T(8,128)(2,1)S(1)}, bf16[32,4096]{1,0:T(8,128)(2,1)S(1)}, u32[]{:S(2)}, u32[]{:S(2)}) collective-permute-start(bf16[32,4096]{1,0:T(8,128)(2,1)S(1)} %shard_map.88), channel_id=1, source_target_pairs={{0,1},{1,0},{2,3},{3,2},{4,5},{5,4},{6,7},{7,6},{8,9},{9,8},{10,11... | collective-permute-start | bytes 786440 | tf_op jit(solution)/shard_map/ppermute | solution.py:96
  42.2 7.5 %collective-permute-start.19 = (bf16[32,4096]{1,0:T(8,128)(2,1)S(1)}, bf16[32,4096]{1,0:T(8,128)(2,1)S(1)}, u32[]{:S(2)}, u32[]{:S(2)}) collective-permute-start(bf16[32,4096]{1,0:T(8,128)(2,1)S(1)} %shard_map.94), channel_id=1, source_target_pairs={{0,1},{1,0},{2,3},{3,2},{4,5},{5,4},{6,7},{7,6},{8,9},{9,8},{10,11... | collective-permute-start | bytes 786440 | tf_op jit(solution)/shard_map/ppermute | solution.py:96
  46.9 2.9 %collective-permute-start.11 = (bf16[16,4096]{1,0:T(8,128)(2,1)S(1)}, bf16[16,4096]{1,0:T(8,128)(2,1)S(1)}, u32[]{:S(2)}, u32[]{:S(2)}) collective-permute-start(bf16[16,4096]{1,0:T(8,128)(2,1)S(1)} %slice.17), channel_id=1, source_target_pairs={{0,16},{16,0},{1,17},{17,1},{2,18},{18,2},{3,19},{19,3},{4,20},{20... | collective-permute-start | bytes 393224 | tf_op jit(solution)/shard_map/ppermute | solution.py:14
  49.7 1.9 %collective-permute-start.20 = (bf16[16,4096]{1,0:T(8,128)(2,1)S(1)}, bf16[16,4096]{1,0:T(8,128)(2,1)S(1)}, u32[]{:S(2)}, u32[]{:S(2)}) collective-permute-start(bf16[16,4096]{1,0:T(8,128)(2,1)S(1)} %slice.19), channel_id=1, source_target_pairs={{0,16},{16,0},{1,17},{17,1},{2,18},{18,2},{3,19},{19,3},{4,20},{20... | collective-permute-start | bytes 393224 | tf_op jit(solution)/shard_map/ppermute | solution.py:14
  49.9 7.0 %collective-permute-start.22 = (bf16[8,4096]{1,0:T(8,128)(2,1)S(1)}, bf16[8,4096]{1,0:T(8,128)(2,1)S(1)}, u32[]{:S(2)}, u32[]{:S(2)}) collective-permute-start(bf16[8,4096]{1,0:T(8,128)(2,1)S(1)} %get-tuple-element.43), channel_id=1, source_target_pairs={{0,8},{1,9},{2,10},{3,11},{4,12},{5,13},{6,14},{7,15},{8,0},{9,1},... | collective-permute-start | bytes 196616 | tf_op jit(solution)/shard_map/ppermute | solution.py:14
  51.6 5.6 %collective-permute-start.21 = (bf16[8,4096]{1,0:T(8,128)(2,1)S(1)}, bf16[8,4096]{1,0:T(8,128)(2,1)S(1)}, u32[]{:S(2)}, u32[]{:S(2)}) collective-permute-start(bf16[8,4096]{1,0:T(8,128)(2,1)S(1)} %get-tuple-element.42), channel_id=1, source_target_pairs={{0,4},{1,5},{2,6},{3,7},{4,0},{5,1},{6,2},{7,3},{8,12},{9,13},{10,... | collective-permute-start | bytes 196616 | tf_op jit(solution)/shard_map/ppermute | solution.py:14
  52.8 6.1 %collective-permute-start.23 = (bf16[8,4096]{1,0:T(8,128)(2,1)S(1)}, bf16[8,4096]{1,0:T(8,128)(2,1)S(1)}, u32[]{:S(2)}, u32[]{:S(2)}) collective-permute-start(bf16[8,4096]{1,0:T(8,128)(2,1)S(1)} %get-tuple-element.44), channel_id=1, source_target_pairs={{0,12},{1,13},{2,14},{3,15},{4,8},{5,9},{6,10},{7,11},{8,4},{9,5},... | collective-permute-start | bytes 196616 | tf_op jit(solution)/shard_map/ppermute | solution.py:14

commit v3 on v2

--- a/solution.py
+++ b/solution.py
@@ -88,75 +88,62 @@
     )[0]
 
 
-def turn(block, first, second):
-    owners = lax.axis_size("dev")
-    route = []
-    for side, offset in enumerate((first, second)):
-        route += [(side * owners + i, side * owners + (i ^ offset)) for i in range(owners)]
-    return lax.ppermute(block, ("side", "dev"), route)
-
-
-def expert_kernel(
-    column_ref, near_ref, far_ref, mine_ref, other_ref, gate_ref, up_ref, down_ref,
-    away_ref, keep_ref,
-):
-    span = mine_ref.shape[0]
-    width = keep_ref.shape[1]
-    extra = column_ref.shape[1] - width
+def collect_kernel(column_ref, x_ref, y_ref, left_ref, right_ref, out_ref):
+    span = column_ref.shape[0]
+    half = left_ref.shape[1]
+    out_ref[:span] = column_ref[...]
+    out_ref[span : 2 * span] = x_ref[...]
+    out_ref[2 * span : 3 * span] = y_ref[...]
+    out_ref[3 * span :, :half] = left_ref[...]
+    out_ref[3 * span :, half:] = right_ref[...]
+
+
+def expert_kernel(own_ref, other_ref, gate_ref, up_ref, down_ref, away_ref, keep_ref):
+    rows, width = keep_ref.shape
+    extra = own_ref.shape[1] - width
     owners = lax.axis_size("dev")
     me = lax.axis_index("dev")
     step = min(width, 1024)
-
-    def rows(start, size):
-        columns = slice(start, start + size)
-        return jnp.concatenate(
-            [
-                other_ref[:, columns],
-                far_ref[:, columns],
-                column_ref[span:, columns],
-                mine_ref[:, columns],
-                near_ref[:, columns],
-                column_ref[:span, columns],
-            ]
-        )
-
     gate = up = 0.0
     for k in range(0, width, step):
-        part = rows(k, step)
+        part = jnp.concatenate([other_ref[:, k : k + step], own_ref[:, k : k + step]])
         gate += jnp.dot(part, gate_ref[0, k : k + step], preferred_element_type=jnp.float32)
         up += jnp.dot(part, up_ref[0, k : k + step], preferred_element_type=jnp.float32)
     hidden = (gate / (1.0 + jnp.exp(-gate)) * up).astype(jnp.bfloat16)
+    parts = jnp.concatenate([other_ref[:, width:], own_ref[:, width:]]).astype(jnp.float32)
     lane = lax.broadcasted_iota(jnp.int32, (1, extra), 1)
-    parts = rows(width, extra).astype(jnp.float32)
     weight = jnp.sum(jnp.where(lax.rem(lane, owners) == me, parts, 0.0), axis=1, keepdims=True)
-    half = 4 * span
     for k in range(0, width, step):
         down = down_ref[0, :, k : k + step]
         value = jnp.dot(hidden, down, preferred_element_type=jnp.float32) * weight
-        away_ref[:, k : k + step] = value[:half].astype(jnp.bfloat16)
-        keep_ref[:, k : k + step] = value[half:]
-
-
-def corner_kernel(keep_ref, got_ref, out_ref):
-    span = out_ref.shape[0]
-    out_ref[...] = (keep_ref[:span] + got_ref[:span].astype(jnp.float32)).astype(jnp.bfloat16)
-
-
-def near_kernel(keep_ref, got_ref, corner_ref, out_ref):
-    span = corner_ref.shape[0]
+        away_ref[:, k : k + step] = value[:rows].astype(jnp.bfloat16)
+        keep_ref[:, k : k + step] = value[rows:]
+
+
+def diag_kernel(keep_ref, got_ref, left_ref, right_ref):
+    span, half = left_ref.shape
+    total = keep_ref[3 * span :] + got_ref[3 * span :].astype(jnp.float32)
+    left_ref[...] = total[:, :half].astype(jnp.bfloat16)
+    right_ref[...] = total[:, half:].astype(jnp.bfloat16)
+
+
+def plane_kernel(keep_ref, got_ref, left_ref, right_ref, x_ref, y_ref):
+    span, half = left_ref.shape
     total = keep_ref[span : 3 * span] + got_ref[span : 3 * span].astype(jnp.float32)
-    out_ref[:span] = (total[:span] + corner_ref[...].astype(jnp.float32)).astype(jnp.bfloat16)
-    out_ref[span:] = total[span:].astype(jnp.bfloat16)
-
-
-def column_kernel(keep_ref, got_ref, near_ref, other_ref, *out_refs):
+    x_ref[:, :half] = (total[:span, :half] + left_ref[...].astype(jnp.float32)).astype(jnp.bfloat16)
+    x_ref[:, half:] = total[:span, half:].astype(jnp.bfloat16)
+    y_ref[:, :half] = total[span:, :half].astype(jnp.bfloat16)
+    y_ref[:, half:] = (total[span:, half:] + right_ref[...].astype(jnp.float32)).astype(
+        jnp.bfloat16
+    )
+
+
+def column_kernel(keep_ref, got_ref, x_ref, y_ref, *out_refs):
     count = out_refs[0].shape[0]
-    base = 3 * other_ref.shape[0]
     for i, out_ref in enumerate(out_refs):
         rows = slice(i * count, (i + 1) * count)
-        kept = slice(base + i * count, base + (i + 1) * count)
-        total = keep_ref[kept] + got_ref[kept].astype(jnp.float32)
-        total = total + near_ref[rows].astype(jnp.float32) + other_ref[rows].astype(jnp.float32)
+        total = keep_ref[rows] + got_ref[rows].astype(jnp.float32)
+        total = total + x_ref[rows].astype(jnp.float32) + y_ref[rows].astype(jnp.float32)
         out_ref[...] = total.astype(out_ref.dtype)
 
 
@@ -193,44 +180,51 @@
 def body(tokens, norm_gain, expert_ids, route_weight, placement, w_gate, w_up, w_down):
     count, width = tokens.shape
     owners = lax.axis_size("dev")
+    half = width // 2
     extra = -(-3 * owners // 128) * 128
     bf16, f32 = jnp.bfloat16, jnp.float32
     packed = prepare(tokens, norm_gain, expert_ids, route_weight, placement, owners, extra)
     offsets = list(range(0, owners, 4))
-    odd = [r for r in offsets if r // 4 % 2 == 1]
-    even = [r for r in offsets if r // 4 % 2 == 0]
-    groups = [group for group in (even, odd) if group]
+    far = [r for r in offsets if 2 * r >= owners]
+    close = [r for r in offsets if 2 * r < owners]
+    groups = [group for group in (far, close) if group]
     blocks = {r: swap(packed, "dev", r) for group in groups for r in group if r}
     *weights, blocks[0] = load(w_gate, w_up, w_down, packed)
     blocks, weights = lax.optimization_barrier((blocks, weights))
     pieces = []
     for group in groups:
-        mine = stack(*[blocks[r] for r in group])
-        span = mine.shape[0]
-        column = stack(mine, swap(mine, "side", 1))
-        near = turn(column, 1, 2)
-        corner = turn(near[:span], 2, 1)
-        far = swap(near, "side", 1)
-        if pieces:
-            corner = lax.optimization_barrier((corner, pieces[-1]))[0]
-        pieces.append(
-            local_call(
-                expert_kernel,
-                [((4 * span, width), bf16), ((4 * span, width), f32)],
-                column, near, far, corner, swap(corner, "side", 1), *weights,
-            )
+        column = stack(*[blocks[r] for r in group])
+        along_x = swap(column, "dev", 1)
+        along_y = swap(column, "dev", 2)
+        left = swap(along_y[:, :half], "dev", 1)
+        right = swap(along_x[:, half:], "dev", 2)
+        rows = 4 * column.shape[0]
+        own = local_call(
+            collect_kernel, [((rows, width + extra), bf16)], column, along_x, along_y, left, right
+        )[0]
+        other = swap(own, "side", 1)
+        away, keep = local_call(
+            expert_kernel,
+            [((rows, width), bf16), ((rows, width), f32)],
+            own, other, *weights,
         )
+        pieces.append((away, keep))
     sums = {}
     for group, (away, keep) in zip(groups, pieces):
         span = len(group) * count
         got = swap(away, "side", 1)
-        corner = turn(local_call(corner_kernel, [((span, width), bf16)], keep, got)[0], 2, 1)
-        near = local_call(near_kernel, [((2 * span, width), bf16)], keep, got, corner)[0]
-        near = turn(near, 1, 2)
+        left, right = local_call(diag_kernel, [((span, half), bf16)] * 2, keep, got)
+        left = swap(left, "dev", 2)
+        right = swap(right, "dev", 1)
+        along_x, along_y = local_call(
+            plane_kernel, [((span, width), bf16)] * 2, keep, got, left, right
+        )
+        along_x = swap(along_x, "dev", 1)
+        along_y = swap(along_y, "dev", 2)
         totals = local_call(
             column_kernel,
             [((count, width), bf16 if r else f32) for r in group],
-            keep, got, near, swap(near[span:], "side", 1),
+            keep, got, along_x, along_y,
         )
         for r, total in zip(group, totals):
             sums[r] = swap(total, "dev", r) if r else total

time: 59.8 us -> 55.1 us (0.921)
  waiting for transfers between devices: 24.7 us -> 14.8 us
  starting transfers between devices: 23.4 us -> 28.7 us
    ppermute x16 -> x26, starting transfers between devices: 11.3 us -> 28.7 us  [swap(): return lax.ppermute(block, axis, [(i, i ^ offset) for i in range(count)])]
    ppermute x8 -> x0, waiting for transfers between devices: 14.9 us -> none  [turn(): return lax.ppermute(block, ('side', 'dev'), route)]
    ppermute x8 -> x0, starting transfers between devices: 12.1 us -> none  [turn(): return lax.ppermute(block, ('side', 'dev'), route)]
    ppermute x16 -> x26, waiting for transfers between devices: 9.8 us -> 14.8 us  [swap(): return lax.ppermute(block, axis, [(i, i ^ offset) for i in range(count)])]
  transfers between devices with their start and end apart: 24 -> 26, of which waited for: 16 -> 11; matrix products, arithmetic and copies ran while one was open for 0% -> 0% of each run, Pallas kernels for 13% -> 15%
where the time goes in v3:
time: 55.1 us; the launch traced here: 54.9 us
  starting transfers between devices  28.7 us (52%)
  waiting for transfers between devices  14.8 us (27%)
  Pallas kernels  10.3 us (19%)
  local copies, waits for them, and re-layouts  0.97 us (2%)
    ppermute x26, starting transfers between devices, swap(): return lax.ppermute(block, axis, [(i, i ^ offset) for i in range(count)])  28.7 us
    ppermute x26, waiting for transfers between devices, swap(): return lax.ppermute(block, axis, [(i, i ^ offset) for i in range(count)])  14.8 us
    pallas_call x13, Pallas kernels, local_call(): pl.pallas_call(kernel, out_shape=[jax.ShapeDtypeStruct(shape, dtype) for...  4.86 us
    pallas_call x1, Pallas kernels, load(): pl.pallas_call(load_kernel, out_shape=[jax.ShapeDtypeStruct(x.shape, x.dt...  3.79 us
    pallas_call x1, Pallas kernels, prepare(): pl.pallas_call(functools.partial(prepare_kernel, slots), out_shape=jax.Sh...  1.63 us
  transfers between devices with their start and end apart: 26, of which 11 were waited for; matrix products, arithmetic and copies ran while one was open for 0% of the time, Pallas kernels for 15%

profile of v3, /device:TPU:0, one launch (start us, length us, event | category | flops | bytes accessed | tf_op | source)
XLA Modules:
  0.0 54.9 jit_solution(3178515317725817890)
XLA Ops:
  0.0 1.6 %shard_map.82.refs_3_ = bf16[8,4224]{1,0:T(8,128)(2,1)} custom-call(bf16[8,4096]{1,0:T(8,128)(2,1)} %tok_ref.1, f32[4096]{0:T(1024)} %gain_ref.1, s32[8,8]{1,0:T(8,128)} %ids_ref.1, f32[8,8]{1,0:T(8,128)} %weight_ref.1, s32[16]{0:T(128)} %placement_ref.1), custom_call_target="tpu_custom_call" | custom-call | tf_op jit(solution)/shard_map/pallas_call | solution.py:47
  1.6 3.0 %collective-permute-start = (bf16[8,4224]{1,0:T(8,128)(2,1)}, bf16[8,4224]{1,0:T(8,128)(2,1)S(1)}, u32[]{:S(2)}, u32[]{:S(2)}) collective-permute-start(bf16[8,4224]{1,0:T(8,128)(2,1)} %shard_map.82.refs_3_), channel_id=1, source_target_pairs={{0,4},{1,5},{2,6},{3,7},{4,0},{5,1},{6,2},{7,3},{8,12},{9,13},{10,... | collective-permute-start | bytes 202760 | tf_op jit(solution)/shard_map/ppermute | solution.py:14
  4.7 2.6 %collective-permute-start.1 = (bf16[8,4224]{1,0:T(8,128)(2,1)}, bf16[8,4224]{1,0:T(8,128)(2,1)S(1)}, u32[]{:S(2)}, u32[]{:S(2)}) collective-permute-start(bf16[8,4224]{1,0:T(8,128)(2,1)} %shard_map.82.refs_3_), channel_id=1, source_target_pairs={{0,8},{1,9},{2,10},{3,11},{4,12},{5,13},{6,14},{7,15},{8,0},{9,1},... | collective-permute-start | bytes 202760 | tf_op jit(solution)/shard_map/ppermute | solution.py:14
  7.2 0.0 collective-permute-start.2
  7.3 0.9 %copy-done = bf16[8,4224]{1,0:T(8,128)(2,1)S(1)} copy-done((bf16[8,4224]{1,0:T(8,128)(2,1)S(1)}, bf16[8,4224]{1,0:T(8,128)(2,1)}, u32[]{:S(2)}) %copy-start) | copy-done | bytes 67608
  8.2 3.8 %shard_map.83 = (bf16[1,4096,384]{2,1,0:T(8,128)(2,1)S(1)}, bf16[1,4096,384]{2,1,0:T(8,128)(2,1)S(1)}, bf16[1,384,4096]{2,1,0:T(8,128)(2,1)S(1)}, bf16[8,4224]{1,0:T(8,128)(2,1)S(1)}) custom-call(bf16[1,4096,384]{2,1,0:T(8,128)(2,1)} %refs_0_.1, bf16[1,4096,384]{2,1,0:T(8,128)(2,1)} %refs_1_.1, bf16[1,384,4096]{2,1,0:T(8,128)(2,1)} %refs_2_.1, ...), custom_call_target="tpu_custom_call" | custom-call | bytes 19009536 | tf_op jit(solution)/shard_map/pallas_call | solution.py:169
  12.0 0.3 collective-permute-done.1.refs_0_
  12.3 1.4 %collective-permute-done.2.refs_1_ = bf16[8,4224]{1,0:T(8,128)(2,1)S(1)} collective-permute-done((bf16[8,4224]{1,0:T(8,128)(2,1)}, bf16[8,4224]{1,0:T(8,128)(2,1)S(1)}, u32[]{:S(2)}, u32[]{:S(2)}) %collective-permute-start.2) | collective-permute-done | bytes 67616 | tf_op jit(solution)/shard_map/ppermute | solution.py:14
  13.7 1.6 %collective-permute-start.14 = (bf16[16,4224]{1,0:T(8,128)(2,1)S(1)}, bf16[16,4224]{1,0:T(8,128)(2,1)S(1)}, u32[]{:S(2)}, u32[]{:S(2)}) collective-permute-start(bf16[16,4224]{1,0:T(8,128)(2,1)S(1)} %shard_map.90.column_ref), channel_id=1, source_target_pairs={{0,1},{1,0},{2,3},{3,2},{4,5},{5,4},{6,7},{7,6},{8,9},{9,8},{10,11... | collective-permute-start | bytes 405512 | tf_op jit(solution)/shard_map/ppermute | solution.py:14
  15.2 0.6 %collective-permute-start.3 = (bf16[16,4224]{1,0:T(8,128)(2,1)S(1)}, bf16[16,4224]{1,0:T(8,128)(2,1)S(1)}, u32[]{:S(2)}, u32[]{:S(2)}) collective-permute-start(bf16[16,4224]{1,0:T(8,128)(2,1)S(1)} %shard_map.84.column_ref), channel_id=1, source_target_pairs={{0,1},{1,0},{2,3},{3,2},{4,5},{5,4},{6,7},{7,6},{8,9},{9,8},{10,11... | collective-permute-start | bytes 405512 | tf_op jit(solution)/shard_map/ppermute | solution.py:14
  15.8 1.5 %collective-permute-start.15 = (bf16[16,4224]{1,0:T(8,128)(2,1)S(1)}, bf16[16,4224]{1,0:T(8,128)(2,1)S(1)}, u32[]{:S(2)}, u32[]{:S(2)}) collective-permute-start(bf16[16,4224]{1,0:T(8,128)(2,1)S(1)} %shard_map.90.column_ref), channel_id=1, source_target_pairs={{0,2},{1,3},{2,0},{3,1},{4,6},{5,7},{6,4},{7,5},{8,10},{9,11},{10,... | collective-permute-start | bytes 405512 | tf_op jit(solution)/shard_map/ppermute | solution.py:14
  17.4 0.5 collective-permute-start.4
  17.9 0.9 %collective-permute-done.14.x_ref = bf16[16,4224]{1,0:T(8,128)(2,1)S(1)} collective-permute-done((bf16[16,4224]{1,0:T(8,128)(2,1)S(1)}, bf16[16,4224]{1,0:T(8,128)(2,1)S(1)}, u32[]{:S(2)}, u32[]{:S(2)}) %collective-permute-start.14) | collective-permute-done | bytes 135200 | tf_op jit(solution)/shard_map/ppermute | solution.py:14
  18.8 1.5 %collective-permute-start.17 = (bf16[16,2176]{1,0:T(8,128)(2,1)S(1)}, bf16[16,2176]{1,0:T(8,128)(2,1)S(1)}, u32[]{:S(2)}, u32[]{:S(2)}) collective-permute-start(bf16[16,2176]{1,0:T(8,128)(2,1)S(1)} %slice.19), channel_id=1, source_target_pairs={{0,2},{1,3},{2,0},{3,1},{4,6},{5,7},{6,4},{7,5},{8,10},{9,11},{10,... | collective-permute-start | bytes 208904 | tf_op jit(solution)/shard_map/ppermute | solution.py:14
  20.3 1.6 %collective-permute-start.6 = (bf16[16,2176]{1,0:T(8,128)(2,1)S(1)}, bf16[16,2176]{1,0:T(8,128)(2,1)S(1)}, u32[]{:S(2)}, u32[]{:S(2)}) collective-permute-start(bf16[16,2176]{1,0:T(8,128)(2,1)S(1)} %slice.17), channel_id=1, source_target_pairs={{0,2},{1,3},{2,0},{3,1},{4,6},{5,7},{6,4},{7,5},{8,10},{9,11},{10,... | collective-permute-start | bytes 208904 | tf_op jit(solution)/shard_map/ppermute | solution.py:14
  22.0 1.4 %collective-permute-start.16 = (bf16[16,2048]{1,0:T(8,128)(2,1)S(1)}, bf16[16,2048]{1,0:T(8,128)(2,1)S(1)}, u32[]{:S(2)}, u32[]{:S(2)}) collective-permute-start(bf16[16,2048]{1,0:T(8,128)(2,1)S(1)} %slice.18), channel_id=1, source_target_pairs={{0,1},{1,0},{2,3},{3,2},{4,5},{5,4},{6,7},{7,6},{8,9},{9,8},{10,11... | collective-permute-start | bytes 196616 | tf_op jit(solution)/shard_map/ppermute | solution.py:14
  23.4 1.4 %collective-permute-start.5 = (bf16[16,2048]{1,0:T(8,128)(2,1)S(1)}, bf16[16,2048]{1,0:T(8,128)(2,1)S(1)}, u32[]{:S(2)}, u32[]{:S(2)}) collective-permute-start(bf16[16,2048]{1,0:T(8,128)(2,1)S(1)} %slice.16), channel_id=1, source_target_pairs={{0,1},{1,0},{2,3},{3,2},{4,5},{5,4},{6,7},{7,6},{8,9},{9,8},{10,11... | collective-permute-start | bytes 196616 | tf_op jit(solution)/shard_map/ppermute | solution.py:14
  24.8 1.5 %collective-permute-done.16.left_ref = bf16[16,2048]{1,0:T(8,128)(2,1)S(1)} collective-permute-done((bf16[16,2048]{1,0:T(8,128)(2,1)S(1)}, bf16[16,2048]{1,0:T(8,128)(2,1)S(1)}, u32[]{:S(2)}, u32[]{:S(2)}) %collective-permute-start.16) | collective-permute-done | bytes 65568 | tf_op jit(solution)/shard_map/ppermute | solution.py:14
  26.3 0.1 collective-permute-start.18
  26.4 1.3 %collective-permute-done.5.left_ref = bf16[16,2048]{1,0:T(8,128)(2,1)S(1)} collective-permute-done((bf16[16,2048]{1,0:T(8,128)(2,1)S(1)}, bf16[16,2048]{1,0:T(8,128)(2,1)S(1)}, u32[]{:S(2)}, u32[]{:S(2)}) %collective-permute-start.5) | collective-permute-done | bytes 65568 | tf_op jit(solution)/shard_map/ppermute | solution.py:14
  27.7 0.1 collective-permute-start.7
  27.8 0.5 collective-permute-done.18.other_ref
  28.3 1.9 %shard_map.92 = (bf16[64,4096]{1,0:T(8,128)(2,1)S(1)}, f32[64,4096]{1,0:T(8,128)S(1)}) custom-call(bf16[64,4224]{1,0:T(8,128)(2,1)S(1)} %shard_map.91.own_ref, bf16[64,4224]{1,0:T(8,128)(2,1)S(1)} %collective-permute-done.18.other_ref, bf16[1,4096,384]{2,1,0:T(8,128)(2,1)S(1)} %get-tuple-element.38.gate_ref, ...), custom_call_target="tpu_custom_call" | custom-call | bytes 12091392 | tf_op jit(solution)/shard_map/pallas_call | solution.py:64
  30.3 0.2 collective-permute-start.19
  30.5 1.9 %shard_map.86 = (bf16[64,4096]{1,0:T(8,128)(2,1)S(1)}, f32[64,4096]{1,0:T(8,128)S(1)}) custom-call(bf16[64,4224]{1,0:T(8,128)(2,1)S(1)} %shard_map.85.own_ref, bf16[64,4224]{1,0:T(8,128)(2,1)S(1)} %collective-permute-done.7.other_ref, bf16[1,4096,384]{2,1,0:T(8,128)(2,1)S(1)} %get-tuple-element.38.gate_ref, ...), custom_call_target="tpu_custom_call" | custom-call | bytes 12091392 | tf_op jit(solution)/shard_map/pallas_call | solution.py:64
  32.4 0.4 collective-permute-start.8
  32.9 1.4 %collective-permute-start.20 = (bf16[16,2048]{1,0:T(8,128)(2,1)S(1)}, bf16[16,2048]{1,0:T(8,128)(2,1)S(1)}, u32[]{:S(2)}, u32[]{:S(2)}) collective-permute-start(bf16[16,2048]{1,0:T(8,128)(2,1)S(1)} %get-tuple-element.53), channel_id=1, source_target_pairs={{0,2},{1,3},{2,0},{3,1},{4,6},{5,7},{6,4},{7,5},{8,10},{9,11},{10,... | collective-permute-start | bytes 196616 | tf_op jit(solution)/shard_map/ppermute | solution.py:14
  34.2 1.5 %collective-permute-start.21 = (bf16[16,2048]{1,0:T(8,128)(2,1)S(1)}, bf16[16,2048]{1,0:T(8,128)(2,1)S(1)}, u32[]{:S(2)}, u32[]{:S(2)}) collective-permute-start(bf16[16,2048]{1,0:T(8,128)(2,1)S(1)} %get-tuple-element.54), channel_id=1, source_target_pairs={{0,1},{1,0},{2,3},{3,2},{4,5},{5,4},{6,7},{7,6},{8,9},{9,8},{10,11... | collective-permute-start | bytes 196616 | tf_op jit(solution)/shard_map/ppermute | solution.py:14
  35.8 0.6 %collective-permute-start.10 = (bf16[16,2048]{1,0:T(8,128)(2,1)S(1)}, bf16[16,2048]{1,0:T(8,128)(2,1)S(1)}, u32[]{:S(2)}, u32[]{:S(2)}) collective-permute-start(bf16[16,2048]{1,0:T(8,128)(2,1)S(1)} %get-tuple-element.44), channel_id=1, source_target_pairs={{0,1},{1,0},{2,3},{3,2},{4,5},{5,4},{6,7},{7,6},{8,9},{9,8},{10,11... | collective-permute-start | bytes 196616 | tf_op jit(solution)/shard_map/ppermute | solution.py:14
  36.4 0.9 %collective-permute-start.9 = (bf16[16,2048]{1,0:T(8,128)(2,1)S(1)}, bf16[16,2048]{1,0:T(8,128)(2,1)S(1)}, u32[]{:S(2)}, u32[]{:S(2)}) collective-permute-start(bf16[16,2048]{1,0:T(8,128)(2,1)S(1)} %get-tuple-element.43), channel_id=1, source_target_pairs={{0,2},{1,3},{2,0},{3,1},{4,6},{5,7},{6,4},{7,5},{8,10},{9,11},{10,... | collective-permute-start | bytes 196616 | tf_op jit(solution)/shard_map/ppermute | solution.py:14
  37.3 1.7 %collective-permute-done.21.right_ref = bf16[16,2048]{1,0:T(8,128)(2,1)S(1)} collective-permute-done((bf16[16,2048]{1,0:T(8,128)(2,1)S(1)}, bf16[16,2048]{1,0:T(8,128)(2,1)S(1)}, u32[]{:S(2)}, u32[]{:S(2)}) %collective-permute-start.21) | collective-permute-done | bytes 65568 | tf_op jit(solution)/shard_map/ppermute | solution.py:14
  39.0 0.1 shard_map.94
  39.1 1.3 %collective-permute-start.22 = (bf16[16,4096]{1,0:T(8,128)(2,1)S(1)}, bf16[16,4096]{1,0:T(8,128)(2,1)S(1)}, u32[]{:S(2)}, u32[]{:S(2)}) collective-permute-start(bf16[16,4096]{1,0:T(8,128)(2,1)S(1)} %get-tuple-element.55), channel_id=1, source_target_pairs={{0,1},{1,0},{2,3},{3,2},{4,5},{5,4},{6,7},{7,6},{8,9},{9,8},{10,11... | collective-permute-start | bytes 393224 | tf_op jit(solution)/shard_map/ppermute | solution.py:14
  40.4 0.6 %collective-permute-start.23 = (bf16[16,4096]{1,0:T(8,128)(2,1)S(1)}, bf16[16,4096]{1,0:T(8,128)(2,1)S(1)}, u32[]{:S(2)}, u32[]{:S(2)}) collective-permute-start(bf16[16,4096]{1,0:T(8,128)(2,1)S(1)} %get-tuple-element.56), channel_id=1, source_target_pairs={{0,2},{1,3},{2,0},{3,1},{4,6},{5,7},{6,4},{7,5},{8,10},{9,11},{10,... | collective-permute-start | bytes 393224 | tf_op jit(solution)/shard_map/ppermute | solution.py:14
  41.1 0.1 shard_map.88
  41.1 1.6 %collective-permute-start.11 = (bf16[16,4096]{1,0:T(8,128)(2,1)S(1)}, bf16[16,4096]{1,0:T(8,128)(2,1)S(1)}, u32[]{:S(2)}, u32[]{:S(2)}) collective-permute-start(bf16[16,4096]{1,0:T(8,128)(2,1)S(1)} %get-tuple-element.45), channel_id=1, source_target_pairs={{0,1},{1,0},{2,3},{3,2},{4,5},{5,4},{6,7},{7,6},{8,9},{9,8},{10,11... | collective-permute-start | bytes 393224 | tf_op jit(solution)/shard_map/ppermute | solution.py:14
  42.7 0.7 %collective-permute-start.12 = (bf16[16,4096]{1,0:T(8,128)(2,1)S(1)}, bf16[16,4096]{1,0:T(8,128)(2,1)S(1)}, u32[]{:S(2)}, u32[]{:S(2)}) collective-permute-start(bf16[16,4096]{1,0:T(8,128)(2,1)S(1)} %get-tuple-element.46), channel_id=1, source_target_pairs={{0,2},{1,3},{2,0},{3,1},{4,6},{5,7},{6,4},{7,5},{8,10},{9,11},{10,... | collective-permute-start | bytes 393224 | tf_op jit(solution)/shard_map/ppermute | solution.py:14
  43.3 1.3 %collective-permute-done.22.x_ref = bf16[16,4096]{1,0:T(8,128)(2,1)S(1)} collective-permute-done((bf16[16,4096]{1,0:T(8,128)(2,1)S(1)}, bf16[16,4096]{1,0:T(8,128)(2,1)S(1)}, u32[]{:S(2)}, u32[]{:S(2)}) %collective-permute-start.22) | collective-permute-done | bytes 131104 | tf_op jit(solution)/shard_map/ppermute | solution.py:14
  44.7 1.1 %collective-permute-done.23.y_ref = bf16[16,4096]{1,0:T(8,128)(2,1)S(1)} collective-permute-done((bf16[16,4096]{1,0:T(8,128)(2,1)S(1)}, bf16[16,4096]{1,0:T(8,128)(2,1)S(1)}, u32[]{:S(2)}, u32[]{:S(2)}) %collective-permute-start.23) | collective-permute-done | bytes 131104 | tf_op jit(solution)/shard_map/ppermute | solution.py:14
  45.8 0.1 shard_map.95
  45.9 2.1 %collective-permute-start.24 = (bf16[8,4096]{1,0:T(8,128)(2,1)S(1)}, bf16[8,4096]{1,0:T(8,128)(2,1)S(1)}, u32[]{:S(2)}, u32[]{:S(2)}) collective-permute-start(bf16[8,4096]{1,0:T(8,128)(2,1)S(1)} %get-tuple-element.57), channel_id=1, source_target_pairs={{0,8},{1,9},{2,10},{3,11},{4,12},{5,13},{6,14},{7,15},{8,0},{9,1},... | collective-permute-start | bytes 196616 | tf_op jit(solution)/shard_map/ppermute | solution.py:14
  48.0 1.1 %collective-permute-start.25 = (bf16[8,4096]{1,0:T(8,128)(2,1)S(1)}, bf16[8,4096]{1,0:T(8,128)(2,1)S(1)}, u32[]{:S(2)}, u32[]{:S(2)}) collective-permute-start(bf16[8,4096]{1,0:T(8,128)(2,1)S(1)} %get-tuple-element.58), channel_id=1, source_target_pairs={{0,12},{1,13},{2,14},{3,15},{4,8},{5,9},{6,10},{7,11},{8,4},{9,5},... | collective-permute-start | bytes 196616 | tf_op jit(solution)/shard_map/ppermute | solution.py:14
  49.1 0.1 shard_map.89
  49.2 0.4 collective-permute-start.13
  49.6 2.2 %collective-permute-done.24.refs_1_ = bf16[8,4096]{1,0:T(8,128)(2,1)S(1)} collective-permute-done((bf16[8,4096]{1,0:T(8,128)(2,1)S(1)}, bf16[8,4096]{1,0:T(8,128)(2,1)S(1)}, u32[]{:S(2)}, u32[]{:S(2)}) %collective-permute-start.24) | collective-permute-done | bytes 65568 | tf_op jit(solution)/shard_map/ppermute | solution.py:14
  51.8 2.4 %collective-permute-done.25.refs_2_ = bf16[8,4096]{1,0:T(8,128)(2,1)S(1)} collective-permute-done((bf16[8,4096]{1,0:T(8,128)(2,1)S(1)}, bf16[8,4096]{1,0:T(8,128)(2,1)S(1)}, u32[]{:S(2)}, u32[]{:S(2)}) %collective-permute-start.25) | collective-permute-done | bytes 65568 | tf_op jit(solution)/shard_map/ppermute | solution.py:14
  54.2 0.0 collective-permute-done.13.refs_0_
  54.2 0.7 %shard_map.96 = bf16[8,4096]{1,0:T(8,128)(2,1)} custom-call(f32[8,4096]{1,0:T(8,128)S(1)} %get-tuple-element.47.first_ref, bf16[8,4096]{1,0:T(8,128)(2,1)S(1)} %collective-permute-done.13.refs_0_, bf16[8,4096]{1,0:T(8,128)(2,1)S(1)} %collective-permute-done.24.refs_1_, bf16[8,4096]{1,0:T(8,128)(2,1)S(1)} %collective-permute-done.25.refs_2_), custom_call_target="tpu_custom_call" | custom-call | bytes 393216 | tf_op jit(solution)/shard_map/pallas_call | solution.py:64
  (25 shorter events, 0.2 us)
Async XLA Ops:
  1.6 10.4 %collective-permute-start = (bf16[8,4224]{1,0:T(8,128)(2,1)}, bf16[8,4224]{1,0:T(8,128)(2,1)S(1)}, u32[]{:S(2)}, u32[]{:S(2)}) collective-permute-start(bf16[8,4224]{1,0:T(8,128)(2,1)} %shard_map.82.refs_3_), channel_id=1, source_target_pairs={{0,4},{1,5},{2,6},{3,7},{4,0},{5,1},{6,2},{7,3},{8,12},{9,13},{10,... | collective-permute-start | bytes 202760 | tf_op jit(solution)/shard_map/ppermute | solution.py:14
  4.7 7.6 %collective-permute-start.1 = (bf16[8,4224]{1,0:T(8,128)(2,1)}, bf16[8,4224]{1,0:T(8,128)(2,1)S(1)}, u32[]{:S(2)}, u32[]{:S(2)}) collective-permute-start(bf16[8,4224]{1,0:T(8,128)(2,1)} %shard_map.82.refs_3_), channel_id=1, source_target_pairs={{0,8},{1,9},{2,10},{3,11},{4,12},{5,13},{6,14},{7,15},{8,0},{9,1},... | collective-permute-start | bytes 202760 | tf_op jit(solution)/shard_map/ppermute | solution.py:14
  7.2 6.4 %collective-permute-start.2 = (bf16[8,4224]{1,0:T(8,128)(2,1)}, bf16[8,4224]{1,0:T(8,128)(2,1)S(1)}, u32[]{:S(2)}, u32[]{:S(2)}) collective-permute-start(bf16[8,4224]{1,0:T(8,128)(2,1)} %shard_map.82.refs_3_), channel_id=1, source_target_pairs={{0,12},{1,13},{2,14},{3,15},{4,8},{5,9},{6,10},{7,11},{8,4},{9,5},... | collective-permute-start | bytes 202760 | tf_op jit(solution)/shard_map/ppermute | solution.py:14
  7.2 0.9 %copy-start = (bf16[8,4224]{1,0:T(8,128)(2,1)S(1)}, bf16[8,4224]{1,0:T(8,128)(2,1)}, u32[]{:S(2)}) copy-start(bf16[8,4224]{1,0:T(8,128)(2,1)} %shard_map.82.refs_3_) | copy-start | bytes 202756
  13.7 5.1 %collective-permute-start.14 = (bf16[16,4224]{1,0:T(8,128)(2,1)S(1)}, bf16[16,4224]{1,0:T(8,128)(2,1)S(1)}, u32[]{:S(2)}, u32[]{:S(2)}) collective-permute-start(bf16[16,4224]{1,0:T(8,128)(2,1)S(1)} %shard_map.90.column_ref), channel_id=1, source_target_pairs={{0,1},{1,0},{2,3},{3,2},{4,5},{5,4},{6,7},{7,6},{8,9},{9,8},{10,11... | collective-permute-start | bytes 405512 | tf_op jit(solution)/shard_map/ppermute | solution.py:14
  15.2 5.1 %collective-permute-start.3 = (bf16[16,4224]{1,0:T(8,128)(2,1)S(1)}, bf16[16,4224]{1,0:T(8,128)(2,1)S(1)}, u32[]{:S(2)}, u32[]{:S(2)}) collective-permute-start(bf16[16,4224]{1,0:T(8,128)(2,1)S(1)} %shard_map.84.column_ref), channel_id=1, source_target_pairs={{0,1},{1,0},{2,3},{3,2},{4,5},{5,4},{6,7},{7,6},{8,9},{9,8},{10,11... | collective-permute-start | bytes 405512 | tf_op jit(solution)/shard_map/ppermute | solution.py:14
  15.8 6.1 %collective-permute-start.15 = (bf16[16,4224]{1,0:T(8,128)(2,1)S(1)}, bf16[16,4224]{1,0:T(8,128)(2,1)S(1)}, u32[]{:S(2)}, u32[]{:S(2)}) collective-permute-start(bf16[16,4224]{1,0:T(8,128)(2,1)S(1)} %shard_map.90.column_ref), channel_id=1, source_target_pairs={{0,2},{1,3},{2,0},{3,1},{4,6},{5,7},{6,4},{7,5},{8,10},{9,11},{10,... | collective-permute-start | bytes 405512 | tf_op jit(solution)/shard_map/ppermute | solution.py:14
  17.4 6.0 %collective-permute-start.4 = (bf16[16,4224]{1,0:T(8,128)(2,1)S(1)}, bf16[16,4224]{1,0:T(8,128)(2,1)S(1)}, u32[]{:S(2)}, u32[]{:S(2)}) collective-permute-start(bf16[16,4224]{1,0:T(8,128)(2,1)S(1)} %shard_map.84.column_ref), channel_id=1, source_target_pairs={{0,2},{1,3},{2,0},{3,1},{4,6},{5,7},{6,4},{7,5},{8,10},{9,11},{10,... | collective-permute-start | bytes 405512 | tf_op jit(solution)/shard_map/ppermute | solution.py:14
  18.8 7.5 %collective-permute-start.17 = (bf16[16,2176]{1,0:T(8,128)(2,1)S(1)}, bf16[16,2176]{1,0:T(8,128)(2,1)S(1)}, u32[]{:S(2)}, u32[]{:S(2)}) collective-permute-start(bf16[16,2176]{1,0:T(8,128)(2,1)S(1)} %slice.19), channel_id=1, source_target_pairs={{0,2},{1,3},{2,0},{3,1},{4,6},{5,7},{6,4},{7,5},{8,10},{9,11},{10,... | collective-permute-start | bytes 208904 | tf_op jit(solution)/shard_map/ppermute | solution.py:14
  20.3 7.4 %collective-permute-start.6 = (bf16[16,2176]{1,0:T(8,128)(2,1)S(1)}, bf16[16,2176]{1,0:T(8,128)(2,1)S(1)}, u32[]{:S(2)}, u32[]{:S(2)}) collective-permute-start(bf16[16,2176]{1,0:T(8,128)(2,1)S(1)} %slice.17), channel_id=1, source_target_pairs={{0,2},{1,3},{2,0},{3,1},{4,6},{5,7},{6,4},{7,5},{8,10},{9,11},{10,... | collective-permute-start | bytes 208904 | tf_op jit(solution)/shard_map/ppermute | solution.py:14
  22.0 4.3 %collective-permute-start.16 = (bf16[16,2048]{1,0:T(8,128)(2,1)S(1)}, bf16[16,2048]{1,0:T(8,128)(2,1)S(1)}, u32[]{:S(2)}, u32[]{:S(2)}) collective-permute-start(bf16[16,2048]{1,0:T(8,128)(2,1)S(1)} %slice.18), channel_id=1, source_target_pairs={{0,1},{1,0},{2,3},{3,2},{4,5},{5,4},{6,7},{7,6},{8,9},{9,8},{10,11... | collective-permute-start | bytes 196616 | tf_op jit(solution)/shard_map/ppermute | solution.py:14
  23.4 4.3 %collective-permute-start.5 = (bf16[16,2048]{1,0:T(8,128)(2,1)S(1)}, bf16[16,2048]{1,0:T(8,128)(2,1)S(1)}, u32[]{:S(2)}, u32[]{:S(2)}) collective-permute-start(bf16[16,2048]{1,0:T(8,128)(2,1)S(1)} %slice.16), channel_id=1, source_target_pairs={{0,1},{1,0},{2,3},{3,2},{4,5},{5,4},{6,7},{7,6},{8,9},{9,8},{10,11... | collective-permute-start | bytes 196616 | tf_op jit(solution)/shard_map/ppermute | solution.py:14
  26.3 2.0 %collective-permute-start.18 = (bf16[64,4224]{1,0:T(8,128)(2,1)S(1)}, bf16[64,4224]{1,0:T(8,128)(2,1)S(1)}, u32[]{:S(2)}, u32[]{:S(2)}) collective-permute-start(bf16[64,4224]{1,0:T(8,128)(2,1)S(1)} %shard_map.91.own_ref), channel_id=1, source_target_pairs={{0,16},{16,0},{1,17},{17,1},{2,18},{18,2},{3,19},{19,3},{4,20},{20... | collective-permute-start | bytes 1622024 | tf_op jit(solution)/shard_map/ppermute | solution.py:14
  27.7 2.7 %collective-permute-start.7 = (bf16[64,4224]{1,0:T(8,128)(2,1)S(1)}, bf16[64,4224]{1,0:T(8,128)(2,1)S(1)}, u32[]{:S(2)}, u32[]{:S(2)}) collective-permute-start(bf16[64,4224]{1,0:T(8,128)(2,1)S(1)} %shard_map.85.own_ref), channel_id=1, source_target_pairs={{0,16},{16,0},{1,17},{17,1},{2,18},{18,2},{3,19},{19,3},{4,20},{20... | collective-permute-start | bytes 1622024 | tf_op jit(solution)/shard_map/ppermute | solution.py:14
  30.3 2.6 %collective-permute-start.19 = (bf16[64,4096]{1,0:T(8,128)(2,1)S(1)}, bf16[64,4096]{1,0:T(8,128)(2,1)S(1)}, u32[]{:S(2)}, u32[]{:S(2)}) collective-permute-start(bf16[64,4096]{1,0:T(8,128)(2,1)S(1)} %get-tuple-element.52), channel_id=1, source_target_pairs={{0,16},{16,0},{1,17},{17,1},{2,18},{18,2},{3,19},{19,3},{4,20},{20... | collective-permute-start | bytes 1572872 | tf_op jit(solution)/shard_map/ppermute | solution.py:14
  32.4 3.3 %collective-permute-start.8 = (bf16[64,4096]{1,0:T(8,128)(2,1)S(1)}, bf16[64,4096]{1,0:T(8,128)(2,1)S(1)}, u32[]{:S(2)}, u32[]{:S(2)}) collective-permute-start(bf16[64,4096]{1,0:T(8,128)(2,1)S(1)} %get-tuple-element.42), channel_id=1, source_target_pairs={{0,16},{16,0},{1,17},{17,1},{2,18},{18,2},{3,19},{19,3},{4,20},{20... | collective-permute-start | bytes 1572872 | tf_op jit(solution)/shard_map/ppermute | solution.py:14
  32.9 4.4 %collective-permute-start.20 = (bf16[16,2048]{1,0:T(8,128)(2,1)S(1)}, bf16[16,2048]{1,0:T(8,128)(2,1)S(1)}, u32[]{:S(2)}, u32[]{:S(2)}) collective-permute-start(bf16[16,2048]{1,0:T(8,128)(2,1)S(1)} %get-tuple-element.53), channel_id=1, source_target_pairs={{0,2},{1,3},{2,0},{3,1},{4,6},{5,7},{6,4},{7,5},{8,10},{9,11},{10,... | collective-permute-start | bytes 196616 | tf_op jit(solution)/shard_map/ppermute | solution.py:14
  34.2 4.8 %collective-permute-start.21 = (bf16[16,2048]{1,0:T(8,128)(2,1)S(1)}, bf16[16,2048]{1,0:T(8,128)(2,1)S(1)}, u32[]{:S(2)}, u32[]{:S(2)}) collective-permute-start(bf16[16,2048]{1,0:T(8,128)(2,1)S(1)} %get-tuple-element.54), channel_id=1, source_target_pairs={{0,1},{1,0},{2,3},{3,2},{4,5},{5,4},{6,7},{7,6},{8,9},{9,8},{10,11... | collective-permute-start | bytes 196616 | tf_op jit(solution)/shard_map/ppermute | solution.py:14
  35.8 5.3 %collective-permute-start.10 = (bf16[16,2048]{1,0:T(8,128)(2,1)S(1)}, bf16[16,2048]{1,0:T(8,128)(2,1)S(1)}, u32[]{:S(2)}, u32[]{:S(2)}) collective-permute-start(bf16[16,2048]{1,0:T(8,128)(2,1)S(1)} %get-tuple-element.44), channel_id=1, source_target_pairs={{0,1},{1,0},{2,3},{3,2},{4,5},{5,4},{6,7},{7,6},{8,9},{9,8},{10,11... | collective-permute-start | bytes 196616 | tf_op jit(solution)/shard_map/ppermute | solution.py:14
  36.4 4.7 %collective-permute-start.9 = (bf16[16,2048]{1,0:T(8,128)(2,1)S(1)}, bf16[16,2048]{1,0:T(8,128)(2,1)S(1)}, u32[]{:S(2)}, u32[]{:S(2)}) collective-permute-start(bf16[16,2048]{1,0:T(8,128)(2,1)S(1)} %get-tuple-element.43), channel_id=1, source_target_pairs={{0,2},{1,3},{2,0},{3,1},{4,6},{5,7},{6,4},{7,5},{8,10},{9,11},{10,... | collective-permute-start | bytes 196616 | tf_op jit(solution)/shard_map/ppermute | solution.py:14
  39.1 5.6 %collective-permute-start.22 = (bf16[16,4096]{1,0:T(8,128)(2,1)S(1)}, bf16[16,4096]{1,0:T(8,128)(2,1)S(1)}, u32[]{:S(2)}, u32[]{:S(2)}) collective-permute-start(bf16[16,4096]{1,0:T(8,128)(2,1)S(1)} %get-tuple-element.55), channel_id=1, source_target_pairs={{0,1},{1,0},{2,3},{3,2},{4,5},{5,4},{6,7},{7,6},{8,9},{9,8},{10,11... | collective-permute-start | bytes 393224 | tf_op jit(solution)/shard_map/ppermute | solution.py:14
  40.4 5.4 %collective-permute-start.23 = (bf16[16,4096]{1,0:T(8,128)(2,1)S(1)}, bf16[16,4096]{1,0:T(8,128)(2,1)S(1)}, u32[]{:S(2)}, u32[]{:S(2)}) collective-permute-start(bf16[16,4096]{1,0:T(8,128)(2,1)S(1)} %get-tuple-element.56), channel_id=1, source_target_pairs={{0,2},{1,3},{2,0},{3,1},{4,6},{5,7},{6,4},{7,5},{8,10},{9,11},{10,... | collective-permute-start | bytes 393224 | tf_op jit(solution)/shard_map/ppermute | solution.py:14
  41.1 8.0 %collective-permute-start.11 = (bf16[16,4096]{1,0:T(8,128)(2,1)S(1)}, bf16[16,4096]{1,0:T(8,128)(2,1)S(1)}, u32[]{:S(2)}, u32[]{:S(2)}) collective-permute-start(bf16[16,4096]{1,0:T(8,128)(2,1)S(1)} %get-tuple-element.45), channel_id=1, source_target_pairs={{0,1},{1,0},{2,3},{3,2},{4,5},{5,4},{6,7},{7,6},{8,9},{9,8},{10,11... | collective-permute-start | bytes 393224 | tf_op jit(solution)/shard_map/ppermute | solution.py:14
  42.7 6.4 %collective-permute-start.12 = (bf16[16,4096]{1,0:T(8,128)(2,1)S(1)}, bf16[16,4096]{1,0:T(8,128)(2,1)S(1)}, u32[]{:S(2)}, u32[]{:S(2)}) collective-permute-start(bf16[16,4096]{1,0:T(8,128)(2,1)S(1)} %get-tuple-element.46), channel_id=1, source_target_pairs={{0,2},{1,3},{2,0},{3,1},{4,6},{5,7},{6,4},{7,5},{8,10},{9,11},{10,... | collective-permute-start | bytes 393224 | tf_op jit(solution)/shard_map/ppermute | solution.py:14
  45.9 5.9 %collective-permute-start.24 = (bf16[8,4096]{1,0:T(8,128)(2,1)S(1)}, bf16[8,4096]{1,0:T(8,128)(2,1)S(1)}, u32[]{:S(2)}, u32[]{:S(2)}) collective-permute-start(bf16[8,4096]{1,0:T(8,128)(2,1)S(1)} %get-tuple-element.57), channel_id=1, source_target_pairs={{0,8},{1,9},{2,10},{3,11},{4,12},{5,13},{6,14},{7,15},{8,0},{9,1},... | collective-permute-start | bytes 196616 | tf_op jit(solution)/shard_map/ppermute | solution.py:14
  48.0 6.2 %collective-permute-start.25 = (bf16[8,4096]{1,0:T(8,128)(2,1)S(1)}, bf16[8,4096]{1,0:T(8,128)(2,1)S(1)}, u32[]{:S(2)}, u32[]{:S(2)}) collective-permute-start(bf16[8,4096]{1,0:T(8,128)(2,1)S(1)} %get-tuple-element.58), channel_id=1, source_target_pairs={{0,12},{1,13},{2,14},{3,15},{4,8},{5,9},{6,10},{7,11},{8,4},{9,5},... | collective-permute-start | bytes 196616 | tf_op jit(solution)/shard_map/ppermute | solution.py:14
  49.2 5.0 %collective-permute-start.13 = (bf16[8,4096]{1,0:T(8,128)(2,1)S(1)}, bf16[8,4096]{1,0:T(8,128)(2,1)S(1)}, u32[]{:S(2)}, u32[]{:S(2)}) collective-permute-start(bf16[8,4096]{1,0:T(8,128)(2,1)S(1)} %get-tuple-element.48), channel_id=1, source_target_pairs={{0,4},{1,5},{2,6},{3,7},{4,0},{5,1},{6,2},{7,3},{8,12},{9,13},{10,... | collective-permute-start | bytes 196616 | tf_op jit(solution)/shard_map/ppermute | solution.py:14

commit v4 on v3

--- a/solution.py
+++ b/solution.py
@@ -24,8 +24,8 @@
     for expert in range(placement_ref.shape[0]):
         slot = jnp.where(ids == expert, placement_ref[expert], slot)
     lane = lax.broadcasted_iota(jnp.int32, (ids.shape[0], out_ref.shape[1] - width), 1)
-    place = lax.rem(lane, slots)
-    section = lax.div(lane, slots)
+    section = sum((lane >= i * slots).astype(jnp.int32) for i in range(1, 4))
+    place = lane - section * slots
     mixing = jnp.zeros(lane.shape, jnp.float32)
     for k in range(ids.shape[1]):
         mixing += jnp.where(place == slot[:, k : k + 1], weight_ref[:, k : k + 1], 0.0)
@@ -214,8 +214,8 @@
         span = len(group) * count
         got = swap(away, "side", 1)
         left, right = local_call(diag_kernel, [((span, half), bf16)] * 2, keep, got)
+        right = swap(right, "dev", 1)
         left = swap(left, "dev", 2)
-        right = swap(right, "dev", 1)
         along_x, along_y = local_call(
             plane_kernel, [((span, width), bf16)] * 2, keep, got, left, right
         )

time: 55.1 us -> 55.1 us (level)
  no operation moved by 1% of the time
where the time goes in v4:
time: 55.1 us; the launch traced here: 54.9 us
  starting transfers between devices  28.7 us (52%)
  waiting for transfers between devices  14.8 us (27%)
  Pallas kernels  10.3 us (19%)
  local copies, waits for them, and re-layouts  0.97 us (2%)
    ppermute x26, starting transfers between devices, swap(): return lax.ppermute(block, axis, [(i, i ^ offset) for i in range(count)])  28.7 us
    ppermute x26, waiting for transfers between devices, swap(): return lax.ppermute(block, axis, [(i, i ^ offset) for i in range(count)])  14.8 us
    pallas_call x13, Pallas kernels, local_call(): pl.pallas_call(kernel, out_shape=[jax.ShapeDtypeStruct(shape, dtype) for...  4.86 us
    pallas_call x1, Pallas kernels, load(): pl.pallas_call(load_kernel, out_shape=[jax.ShapeDtypeStruct(x.shape, x.dt...  3.79 us
    pallas_call x1, Pallas kernels, prepare(): pl.pallas_call(functools.partial(prepare_kernel, slots), out_shape=jax.Sh...  1.63 us
  transfers between devices with their start and end apart: 26, of which 11 were waited for; matrix products, arithmetic and copies ran while one was open for 0% of the time, Pallas kernels for 15%

profile of v4, /device:TPU:0, one launch (start us, length us, event | category | flops | bytes accessed | tf_op | source)
XLA Modules:
  0.0 54.9 jit_solution(5930049770469315423)
XLA Ops:
  0.0 1.6 %shard_map.82.refs_3_ = bf16[8,4224]{1,0:T(8,128)(2,1)} custom-call(bf16[8,4096]{1,0:T(8,128)(2,1)} %tok_ref.1, f32[4096]{0:T(1024)} %gain_ref.1, s32[8,8]{1,0:T(8,128)} %ids_ref.1, f32[8,8]{1,0:T(8,128)} %weight_ref.1, s32[16]{0:T(128)} %placement_ref.1), custom_call_target="tpu_custom_call" | custom-call | tf_op jit(solution)/shard_map/pallas_call | solution.py:47
  1.6 3.0 %collective-permute-start = (bf16[8,4224]{1,0:T(8,128)(2,1)}, bf16[8,4224]{1,0:T(8,128)(2,1)S(1)}, u32[]{:S(2)}, u32[]{:S(2)}) collective-permute-start(bf16[8,4224]{1,0:T(8,128)(2,1)} %shard_map.82.refs_3_), channel_id=1, source_target_pairs={{0,4},{1,5},{2,6},{3,7},{4,0},{5,1},{6,2},{7,3},{8,12},{9,13},{10,... | collective-permute-start | bytes 202760 | tf_op jit(solution)/shard_map/ppermute | solution.py:14
  4.7 2.6 %collective-permute-start.1 = (bf16[8,4224]{1,0:T(8,128)(2,1)}, bf16[8,4224]{1,0:T(8,128)(2,1)S(1)}, u32[]{:S(2)}, u32[]{:S(2)}) collective-permute-start(bf16[8,4224]{1,0:T(8,128)(2,1)} %shard_map.82.refs_3_), channel_id=1, source_target_pairs={{0,8},{1,9},{2,10},{3,11},{4,12},{5,13},{6,14},{7,15},{8,0},{9,1},... | collective-permute-start | bytes 202760 | tf_op jit(solution)/shard_map/ppermute | solution.py:14
  7.2 0.0 collective-permute-start.2
  7.3 0.9 %copy-done = bf16[8,4224]{1,0:T(8,128)(2,1)S(1)} copy-done((bf16[8,4224]{1,0:T(8,128)(2,1)S(1)}, bf16[8,4224]{1,0:T(8,128)(2,1)}, u32[]{:S(2)}) %copy-start) | copy-done | bytes 67608
  8.2 3.8 %shard_map.83 = (bf16[1,4096,384]{2,1,0:T(8,128)(2,1)S(1)}, bf16[1,4096,384]{2,1,0:T(8,128)(2,1)S(1)}, bf16[1,384,4096]{2,1,0:T(8,128)(2,1)S(1)}, bf16[8,4224]{1,0:T(8,128)(2,1)S(1)}) custom-call(bf16[1,4096,384]{2,1,0:T(8,128)(2,1)} %refs_0_.1, bf16[1,4096,384]{2,1,0:T(8,128)(2,1)} %refs_1_.1, bf16[1,384,4096]{2,1,0:T(8,128)(2,1)} %refs_2_.1, ...), custom_call_target="tpu_custom_call" | custom-call | bytes 19009536 | tf_op jit(solution)/shard_map/pallas_call | solution.py:169
  12.0 0.3 collective-permute-done.1.refs_0_
  12.3 1.4 %collective-permute-done.2.refs_1_ = bf16[8,4224]{1,0:T(8,128)(2,1)S(1)} collective-permute-done((bf16[8,4224]{1,0:T(8,128)(2,1)}, bf16[8,4224]{1,0:T(8,128)(2,1)S(1)}, u32[]{:S(2)}, u32[]{:S(2)}) %collective-permute-start.2) | collective-permute-done | bytes 67616 | tf_op jit(solution)/shard_map/ppermute | solution.py:14
  13.7 1.6 %collective-permute-start.14 = (bf16[16,4224]{1,0:T(8,128)(2,1)S(1)}, bf16[16,4224]{1,0:T(8,128)(2,1)S(1)}, u32[]{:S(2)}, u32[]{:S(2)}) collective-permute-start(bf16[16,4224]{1,0:T(8,128)(2,1)S(1)} %shard_map.90.column_ref), channel_id=1, source_target_pairs={{0,1},{1,0},{2,3},{3,2},{4,5},{5,4},{6,7},{7,6},{8,9},{9,8},{10,11... | collective-permute-start | bytes 405512 | tf_op jit(solution)/shard_map/ppermute | solution.py:14
  15.2 0.6 %collective-permute-start.3 = (bf16[16,4224]{1,0:T(8,128)(2,1)S(1)}, bf16[16,4224]{1,0:T(8,128)(2,1)S(1)}, u32[]{:S(2)}, u32[]{:S(2)}) collective-permute-start(bf16[16,4224]{1,0:T(8,128)(2,1)S(1)} %shard_map.84.column_ref), channel_id=1, source_target_pairs={{0,1},{1,0},{2,3},{3,2},{4,5},{5,4},{6,7},{7,6},{8,9},{9,8},{10,11... | collective-permute-start | bytes 405512 | tf_op jit(solution)/shard_map/ppermute | solution.py:14
  15.8 1.5 %collective-permute-start.15 = (bf16[16,4224]{1,0:T(8,128)(2,1)S(1)}, bf16[16,4224]{1,0:T(8,128)(2,1)S(1)}, u32[]{:S(2)}, u32[]{:S(2)}) collective-permute-start(bf16[16,4224]{1,0:T(8,128)(2,1)S(1)} %shard_map.90.column_ref), channel_id=1, source_target_pairs={{0,2},{1,3},{2,0},{3,1},{4,6},{5,7},{6,4},{7,5},{8,10},{9,11},{10,... | collective-permute-start | bytes 405512 | tf_op jit(solution)/shard_map/ppermute | solution.py:14
  17.4 0.5 collective-permute-start.4
  17.9 0.9 %collective-permute-done.14.x_ref = bf16[16,4224]{1,0:T(8,128)(2,1)S(1)} collective-permute-done((bf16[16,4224]{1,0:T(8,128)(2,1)S(1)}, bf16[16,4224]{1,0:T(8,128)(2,1)S(1)}, u32[]{:S(2)}, u32[]{:S(2)}) %collective-permute-start.14) | collective-permute-done | bytes 135200 | tf_op jit(solution)/shard_map/ppermute | solution.py:14
  18.8 1.5 %collective-permute-start.17 = (bf16[16,2176]{1,0:T(8,128)(2,1)S(1)}, bf16[16,2176]{1,0:T(8,128)(2,1)S(1)}, u32[]{:S(2)}, u32[]{:S(2)}) collective-permute-start(bf16[16,2176]{1,0:T(8,128)(2,1)S(1)} %slice.19), channel_id=1, source_target_pairs={{0,2},{1,3},{2,0},{3,1},{4,6},{5,7},{6,4},{7,5},{8,10},{9,11},{10,... | collective-permute-start | bytes 208904 | tf_op jit(solution)/shard_map/ppermute | solution.py:14
  20.3 1.6 %collective-permute-start.6 = (bf16[16,2176]{1,0:T(8,128)(2,1)S(1)}, bf16[16,2176]{1,0:T(8,128)(2,1)S(1)}, u32[]{:S(2)}, u32[]{:S(2)}) collective-permute-start(bf16[16,2176]{1,0:T(8,128)(2,1)S(1)} %slice.17), channel_id=1, source_target_pairs={{0,2},{1,3},{2,0},{3,1},{4,6},{5,7},{6,4},{7,5},{8,10},{9,11},{10,... | collective-permute-start | bytes 208904 | tf_op jit(solution)/shard_map/ppermute | solution.py:14
  22.0 1.4 %collective-permute-start.16 = (bf16[16,2048]{1,0:T(8,128)(2,1)S(1)}, bf16[16,2048]{1,0:T(8,128)(2,1)S(1)}, u32[]{:S(2)}, u32[]{:S(2)}) collective-permute-start(bf16[16,2048]{1,0:T(8,128)(2,1)S(1)} %slice.18), channel_id=1, source_target_pairs={{0,1},{1,0},{2,3},{3,2},{4,5},{5,4},{6,7},{7,6},{8,9},{9,8},{10,11... | collective-permute-start | bytes 196616 | tf_op jit(solution)/shard_map/ppermute | solution.py:14
  23.4 1.4 %collective-permute-start.5 = (bf16[16,2048]{1,0:T(8,128)(2,1)S(1)}, bf16[16,2048]{1,0:T(8,128)(2,1)S(1)}, u32[]{:S(2)}, u32[]{:S(2)}) collective-permute-start(bf16[16,2048]{1,0:T(8,128)(2,1)S(1)} %slice.16), channel_id=1, source_target_pairs={{0,1},{1,0},{2,3},{3,2},{4,5},{5,4},{6,7},{7,6},{8,9},{9,8},{10,11... | collective-permute-start | bytes 196616 | tf_op jit(solution)/shard_map/ppermute | solution.py:14
  24.8 1.5 %collective-permute-done.16.left_ref = bf16[16,2048]{1,0:T(8,128)(2,1)S(1)} collective-permute-done((bf16[16,2048]{1,0:T(8,128)(2,1)S(1)}, bf16[16,2048]{1,0:T(8,128)(2,1)S(1)}, u32[]{:S(2)}, u32[]{:S(2)}) %collective-permute-start.16) | collective-permute-done | bytes 65568 | tf_op jit(solution)/shard_map/ppermute | solution.py:14
  26.3 0.1 collective-permute-start.18
  26.4 1.3 %collective-permute-done.5.left_ref = bf16[16,2048]{1,0:T(8,128)(2,1)S(1)} collective-permute-done((bf16[16,2048]{1,0:T(8,128)(2,1)S(1)}, bf16[16,2048]{1,0:T(8,128)(2,1)S(1)}, u32[]{:S(2)}, u32[]{:S(2)}) %collective-permute-start.5) | collective-permute-done | bytes 65568 | tf_op jit(solution)/shard_map/ppermute | solution.py:14
  27.7 0.1 collective-permute-start.7
  27.8 0.5 collective-permute-done.18.other_ref
  28.3 1.9 %shard_map.92 = (bf16[64,4096]{1,0:T(8,128)(2,1)S(1)}, f32[64,4096]{1,0:T(8,128)S(1)}) custom-call(bf16[64,4224]{1,0:T(8,128)(2,1)S(1)} %shard_map.91.own_ref, bf16[64,4224]{1,0:T(8,128)(2,1)S(1)} %collective-permute-done.18.other_ref, bf16[1,4096,384]{2,1,0:T(8,128)(2,1)S(1)} %get-tuple-element.38.gate_ref, ...), custom_call_target="tpu_custom_call" | custom-call | bytes 12091392 | tf_op jit(solution)/shard_map/pallas_call | solution.py:64
  30.3 0.2 collective-permute-start.19
  30.5 1.9 %shard_map.86 = (bf16[64,4096]{1,0:T(8,128)(2,1)S(1)}, f32[64,4096]{1,0:T(8,128)S(1)}) custom-call(bf16[64,4224]{1,0:T(8,128)(2,1)S(1)} %shard_map.85.own_ref, bf16[64,4224]{1,0:T(8,128)(2,1)S(1)} %collective-permute-done.7.other_ref, bf16[1,4096,384]{2,1,0:T(8,128)(2,1)S(1)} %get-tuple-element.38.gate_ref, ...), custom_call_target="tpu_custom_call" | custom-call | bytes 12091392 | tf_op jit(solution)/shard_map/pallas_call | solution.py:64
  32.4 0.4 collective-permute-start.8
  32.9 1.4 %collective-permute-start.20 = (bf16[16,2048]{1,0:T(8,128)(2,1)S(1)}, bf16[16,2048]{1,0:T(8,128)(2,1)S(1)}, u32[]{:S(2)}, u32[]{:S(2)}) collective-permute-start(bf16[16,2048]{1,0:T(8,128)(2,1)S(1)} %get-tuple-element.53), channel_id=1, source_target_pairs={{0,2},{1,3},{2,0},{3,1},{4,6},{5,7},{6,4},{7,5},{8,10},{9,11},{10,... | collective-permute-start | bytes 196616 | tf_op jit(solution)/shard_map/ppermute | solution.py:14
  34.2 1.5 %collective-permute-start.21 = (bf16[16,2048]{1,0:T(8,128)(2,1)S(1)}, bf16[16,2048]{1,0:T(8,128)(2,1)S(1)}, u32[]{:S(2)}, u32[]{:S(2)}) collective-permute-start(bf16[16,2048]{1,0:T(8,128)(2,1)S(1)} %get-tuple-element.54), channel_id=1, source_target_pairs={{0,1},{1,0},{2,3},{3,2},{4,5},{5,4},{6,7},{7,6},{8,9},{9,8},{10,11... | collective-permute-start | bytes 196616 | tf_op jit(solution)/shard_map/ppermute | solution.py:14
  35.8 0.6 %collective-permute-start.10 = (bf16[16,2048]{1,0:T(8,128)(2,1)S(1)}, bf16[16,2048]{1,0:T(8,128)(2,1)S(1)}, u32[]{:S(2)}, u32[]{:S(2)}) collective-permute-start(bf16[16,2048]{1,0:T(8,128)(2,1)S(1)} %get-tuple-element.44), channel_id=1, source_target_pairs={{0,1},{1,0},{2,3},{3,2},{4,5},{5,4},{6,7},{7,6},{8,9},{9,8},{10,11... | collective-permute-start | bytes 196616 | tf_op jit(solution)/shard_map/ppermute | solution.py:14
  36.4 0.9 %collective-permute-start.9 = (bf16[16,2048]{1,0:T(8,128)(2,1)S(1)}, bf16[16,2048]{1,0:T(8,128)(2,1)S(1)}, u32[]{:S(2)}, u32[]{:S(2)}) collective-permute-start(bf16[16,2048]{1,0:T(8,128)(2,1)S(1)} %get-tuple-element.43), channel_id=1, source_target_pairs={{0,2},{1,3},{2,0},{3,1},{4,6},{5,7},{6,4},{7,5},{8,10},{9,11},{10,... | collective-permute-start | bytes 196616 | tf_op jit(solution)/shard_map/ppermute | solution.py:14
  37.3 1.7 %collective-permute-done.21.right_ref = bf16[16,2048]{1,0:T(8,128)(2,1)S(1)} collective-permute-done((bf16[16,2048]{1,0:T(8,128)(2,1)S(1)}, bf16[16,2048]{1,0:T(8,128)(2,1)S(1)}, u32[]{:S(2)}, u32[]{:S(2)}) %collective-permute-start.21) | collective-permute-done | bytes 65568 | tf_op jit(solution)/shard_map/ppermute | solution.py:14
  39.0 0.1 shard_map.94
  39.1 1.3 %collective-permute-start.22 = (bf16[16,4096]{1,0:T(8,128)(2,1)S(1)}, bf16[16,4096]{1,0:T(8,128)(2,1)S(1)}, u32[]{:S(2)}, u32[]{:S(2)}) collective-permute-start(bf16[16,4096]{1,0:T(8,128)(2,1)S(1)} %get-tuple-element.55), channel_id=1, source_target_pairs={{0,1},{1,0},{2,3},{3,2},{4,5},{5,4},{6,7},{7,6},{8,9},{9,8},{10,11... | collective-permute-start | bytes 393224 | tf_op jit(solution)/shard_map/ppermute | solution.py:14
  40.4 0.6 %collective-permute-start.23 = (bf16[16,4096]{1,0:T(8,128)(2,1)S(1)}, bf16[16,4096]{1,0:T(8,128)(2,1)S(1)}, u32[]{:S(2)}, u32[]{:S(2)}) collective-permute-start(bf16[16,4096]{1,0:T(8,128)(2,1)S(1)} %get-tuple-element.56), channel_id=1, source_target_pairs={{0,2},{1,3},{2,0},{3,1},{4,6},{5,7},{6,4},{7,5},{8,10},{9,11},{10,... | collective-permute-start | bytes 393224 | tf_op jit(solution)/shard_map/ppermute | solution.py:14
  41.1 0.1 shard_map.88
  41.1 1.6 %collective-permute-start.11 = (bf16[16,4096]{1,0:T(8,128)(2,1)S(1)}, bf16[16,4096]{1,0:T(8,128)(2,1)S(1)}, u32[]{:S(2)}, u32[]{:S(2)}) collective-permute-start(bf16[16,4096]{1,0:T(8,128)(2,1)S(1)} %get-tuple-element.45), channel_id=1, source_target_pairs={{0,1},{1,0},{2,3},{3,2},{4,5},{5,4},{6,7},{7,6},{8,9},{9,8},{10,11... | collective-permute-start | bytes 393224 | tf_op jit(solution)/shard_map/ppermute | solution.py:14
  42.7 0.7 %collective-permute-start.12 = (bf16[16,4096]{1,0:T(8,128)(2,1)S(1)}, bf16[16,4096]{1,0:T(8,128)(2,1)S(1)}, u32[]{:S(2)}, u32[]{:S(2)}) collective-permute-start(bf16[16,4096]{1,0:T(8,128)(2,1)S(1)} %get-tuple-element.46), channel_id=1, source_target_pairs={{0,2},{1,3},{2,0},{3,1},{4,6},{5,7},{6,4},{7,5},{8,10},{9,11},{10,... | collective-permute-start | bytes 393224 | tf_op jit(solution)/shard_map/ppermute | solution.py:14
  43.3 1.3 %collective-permute-done.22.x_ref = bf16[16,4096]{1,0:T(8,128)(2,1)S(1)} collective-permute-done((bf16[16,4096]{1,0:T(8,128)(2,1)S(1)}, bf16[16,4096]{1,0:T(8,128)(2,1)S(1)}, u32[]{:S(2)}, u32[]{:S(2)}) %collective-permute-start.22) | collective-permute-done | bytes 131104 | tf_op jit(solution)/shard_map/ppermute | solution.py:14
  44.7 1.1 %collective-permute-done.23.y_ref = bf16[16,4096]{1,0:T(8,128)(2,1)S(1)} collective-permute-done((bf16[16,4096]{1,0:T(8,128)(2,1)S(1)}, bf16[16,4096]{1,0:T(8,128)(2,1)S(1)}, u32[]{:S(2)}, u32[]{:S(2)}) %collective-permute-start.23) | collective-permute-done | bytes 131104 | tf_op jit(solution)/shard_map/ppermute | solution.py:14
  45.8 0.1 shard_map.95
  45.9 2.1 %collective-permute-start.24 = (bf16[8,4096]{1,0:T(8,128)(2,1)S(1)}, bf16[8,4096]{1,0:T(8,128)(2,1)S(1)}, u32[]{:S(2)}, u32[]{:S(2)}) collective-permute-start(bf16[8,4096]{1,0:T(8,128)(2,1)S(1)} %get-tuple-element.57), channel_id=1, source_target_pairs={{0,8},{1,9},{2,10},{3,11},{4,12},{5,13},{6,14},{7,15},{8,0},{9,1},... | collective-permute-start | bytes 196616 | tf_op jit(solution)/shard_map/ppermute | solution.py:14
  48.0 1.1 %collective-permute-start.25 = (bf16[8,4096]{1,0:T(8,128)(2,1)S(1)}, bf16[8,4096]{1,0:T(8,128)(2,1)S(1)}, u32[]{:S(2)}, u32[]{:S(2)}) collective-permute-start(bf16[8,4096]{1,0:T(8,128)(2,1)S(1)} %get-tuple-element.58), channel_id=1, source_target_pairs={{0,12},{1,13},{2,14},{3,15},{4,8},{5,9},{6,10},{7,11},{8,4},{9,5},... | collective-permute-start | bytes 196616 | tf_op jit(solution)/shard_map/ppermute | solution.py:14
  49.1 0.1 shard_map.89
  49.2 0.4 collective-permute-start.13
  49.6 2.2 %collective-permute-done.24.refs_1_ = bf16[8,4096]{1,0:T(8,128)(2,1)S(1)} collective-permute-done((bf16[8,4096]{1,0:T(8,128)(2,1)S(1)}, bf16[8,4096]{1,0:T(8,128)(2,1)S(1)}, u32[]{:S(2)}, u32[]{:S(2)}) %collective-permute-start.24) | collective-permute-done | bytes 65568 | tf_op jit(solution)/shard_map/ppermute | solution.py:14
  51.8 2.4 %collective-permute-done.25.refs_2_ = bf16[8,4096]{1,0:T(8,128)(2,1)S(1)} collective-permute-done((bf16[8,4096]{1,0:T(8,128)(2,1)S(1)}, bf16[8,4096]{1,0:T(8,128)(2,1)S(1)}, u32[]{:S(2)}, u32[]{:S(2)}) %collective-permute-start.25) | collective-permute-done | bytes 65568 | tf_op jit(solution)/shard_map/ppermute | solution.py:14
  54.2 0.0 collective-permute-done.13.refs_0_
  54.2 0.7 %shard_map.96 = bf16[8,4096]{1,0:T(8,128)(2,1)} custom-call(f32[8,4096]{1,0:T(8,128)S(1)} %get-tuple-element.47.first_ref, bf16[8,4096]{1,0:T(8,128)(2,1)S(1)} %collective-permute-done.13.refs_0_, bf16[8,4096]{1,0:T(8,128)(2,1)S(1)} %collective-permute-done.24.refs_1_, bf16[8,4096]{1,0:T(8,128)(2,1)S(1)} %collective-permute-done.25.refs_2_), custom_call_target="tpu_custom_call" | custom-call | bytes 393216 | tf_op jit(solution)/shard_map/pallas_call | solution.py:64
  (25 shorter events, 0.2 us)
Async XLA Ops:
  1.6 10.4 %collective-permute-start = (bf16[8,4224]{1,0:T(8,128)(2,1)}, bf16[8,4224]{1,0:T(8,128)(2,1)S(1)}, u32[]{:S(2)}, u32[]{:S(2)}) collective-permute-start(bf16[8,4224]{1,0:T(8,128)(2,1)} %shard_map.82.refs_3_), channel_id=1, source_target_pairs={{0,4},{1,5},{2,6},{3,7},{4,0},{5,1},{6,2},{7,3},{8,12},{9,13},{10,... | collective-permute-start | bytes 202760 | tf_op jit(solution)/shard_map/ppermute | solution.py:14
  4.7 7.6 %collective-permute-start.1 = (bf16[8,4224]{1,0:T(8,128)(2,1)}, bf16[8,4224]{1,0:T(8,128)(2,1)S(1)}, u32[]{:S(2)}, u32[]{:S(2)}) collective-permute-start(bf16[8,4224]{1,0:T(8,128)(2,1)} %shard_map.82.refs_3_), channel_id=1, source_target_pairs={{0,8},{1,9},{2,10},{3,11},{4,12},{5,13},{6,14},{7,15},{8,0},{9,1},... | collective-permute-start | bytes 202760 | tf_op jit(solution)/shard_map/ppermute | solution.py:14
  7.2 6.4 %collective-permute-start.2 = (bf16[8,4224]{1,0:T(8,128)(2,1)}, bf16[8,4224]{1,0:T(8,128)(2,1)S(1)}, u32[]{:S(2)}, u32[]{:S(2)}) collective-permute-start(bf16[8,4224]{1,0:T(8,128)(2,1)} %shard_map.82.refs_3_), channel_id=1, source_target_pairs={{0,12},{1,13},{2,14},{3,15},{4,8},{5,9},{6,10},{7,11},{8,4},{9,5},... | collective-permute-start | bytes 202760 | tf_op jit(solution)/shard_map/ppermute | solution.py:14
  7.2 0.9 %copy-start = (bf16[8,4224]{1,0:T(8,128)(2,1)S(1)}, bf16[8,4224]{1,0:T(8,128)(2,1)}, u32[]{:S(2)}) copy-start(bf16[8,4224]{1,0:T(8,128)(2,1)} %shard_map.82.refs_3_) | copy-start | bytes 202756
  13.7 5.1 %collective-permute-start.14 = (bf16[16,4224]{1,0:T(8,128)(2,1)S(1)}, bf16[16,4224]{1,0:T(8,128)(2,1)S(1)}, u32[]{:S(2)}, u32[]{:S(2)}) collective-permute-start(bf16[16,4224]{1,0:T(8,128)(2,1)S(1)} %shard_map.90.column_ref), channel_id=1, source_target_pairs={{0,1},{1,0},{2,3},{3,2},{4,5},{5,4},{6,7},{7,6},{8,9},{9,8},{10,11... | collective-permute-start | bytes 405512 | tf_op jit(solution)/shard_map/ppermute | solution.py:14
  15.2 5.1 %collective-permute-start.3 = (bf16[16,4224]{1,0:T(8,128)(2,1)S(1)}, bf16[16,4224]{1,0:T(8,128)(2,1)S(1)}, u32[]{:S(2)}, u32[]{:S(2)}) collective-permute-start(bf16[16,4224]{1,0:T(8,128)(2,1)S(1)} %shard_map.84.column_ref), channel_id=1, source_target_pairs={{0,1},{1,0},{2,3},{3,2},{4,5},{5,4},{6,7},{7,6},{8,9},{9,8},{10,11... | collective-permute-start | bytes 405512 | tf_op jit(solution)/shard_map/ppermute | solution.py:14
  15.8 6.1 %collective-permute-start.15 = (bf16[16,4224]{1,0:T(8,128)(2,1)S(1)}, bf16[16,4224]{1,0:T(8,128)(2,1)S(1)}, u32[]{:S(2)}, u32[]{:S(2)}) collective-permute-start(bf16[16,4224]{1,0:T(8,128)(2,1)S(1)} %shard_map.90.column_ref), channel_id=1, source_target_pairs={{0,2},{1,3},{2,0},{3,1},{4,6},{5,7},{6,4},{7,5},{8,10},{9,11},{10,... | collective-permute-start | bytes 405512 | tf_op jit(solution)/shard_map/ppermute | solution.py:14
  17.4 6.0 %collective-permute-start.4 = (bf16[16,4224]{1,0:T(8,128)(2,1)S(1)}, bf16[16,4224]{1,0:T(8,128)(2,1)S(1)}, u32[]{:S(2)}, u32[]{:S(2)}) collective-permute-start(bf16[16,4224]{1,0:T(8,128)(2,1)S(1)} %shard_map.84.column_ref), channel_id=1, source_target_pairs={{0,2},{1,3},{2,0},{3,1},{4,6},{5,7},{6,4},{7,5},{8,10},{9,11},{10,... | collective-permute-start | bytes 405512 | tf_op jit(solution)/shard_map/ppermute | solution.py:14
  18.8 7.5 %collective-permute-start.17 = (bf16[16,2176]{1,0:T(8,128)(2,1)S(1)}, bf16[16,2176]{1,0:T(8,128)(2,1)S(1)}, u32[]{:S(2)}, u32[]{:S(2)}) collective-permute-start(bf16[16,2176]{1,0:T(8,128)(2,1)S(1)} %slice.19), channel_id=1, source_target_pairs={{0,2},{1,3},{2,0},{3,1},{4,6},{5,7},{6,4},{7,5},{8,10},{9,11},{10,... | collective-permute-start | bytes 208904 | tf_op jit(solution)/shard_map/ppermute | solution.py:14
  20.3 7.4 %collective-permute-start.6 = (bf16[16,2176]{1,0:T(8,128)(2,1)S(1)}, bf16[16,2176]{1,0:T(8,128)(2,1)S(1)}, u32[]{:S(2)}, u32[]{:S(2)}) collective-permute-start(bf16[16,2176]{1,0:T(8,128)(2,1)S(1)} %slice.17), channel_id=1, source_target_pairs={{0,2},{1,3},{2,0},{3,1},{4,6},{5,7},{6,4},{7,5},{8,10},{9,11},{10,... | collective-permute-start | bytes 208904 | tf_op jit(solution)/shard_map/ppermute | solution.py:14
  22.0 4.3 %collective-permute-start.16 = (bf16[16,2048]{1,0:T(8,128)(2,1)S(1)}, bf16[16,2048]{1,0:T(8,128)(2,1)S(1)}, u32[]{:S(2)}, u32[]{:S(2)}) collective-permute-start(bf16[16,2048]{1,0:T(8,128)(2,1)S(1)} %slice.18), channel_id=1, source_target_pairs={{0,1},{1,0},{2,3},{3,2},{4,5},{5,4},{6,7},{7,6},{8,9},{9,8},{10,11... | collective-permute-start | bytes 196616 | tf_op jit(solution)/shard_map/ppermute | solution.py:14
  23.4 4.3 %collective-permute-start.5 = (bf16[16,2048]{1,0:T(8,128)(2,1)S(1)}, bf16[16,2048]{1,0:T(8,128)(2,1)S(1)}, u32[]{:S(2)}, u32[]{:S(2)}) collective-permute-start(bf16[16,2048]{1,0:T(8,128)(2,1)S(1)} %slice.16), channel_id=1, source_target_pairs={{0,1},{1,0},{2,3},{3,2},{4,5},{5,4},{6,7},{7,6},{8,9},{9,8},{10,11... | collective-permute-start | bytes 196616 | tf_op jit(solution)/shard_map/ppermute | solution.py:14
  26.3 2.0 %collective-permute-start.18 = (bf16[64,4224]{1,0:T(8,128)(2,1)S(1)}, bf16[64,4224]{1,0:T(8,128)(2,1)S(1)}, u32[]{:S(2)}, u32[]{:S(2)}) collective-permute-start(bf16[64,4224]{1,0:T(8,128)(2,1)S(1)} %shard_map.91.own_ref), channel_id=1, source_target_pairs={{0,16},{16,0},{1,17},{17,1},{2,18},{18,2},{3,19},{19,3},{4,20},{20... | collective-permute-start | bytes 1622024 | tf_op jit(solution)/shard_map/ppermute | solution.py:14
  27.7 2.7 %collective-permute-start.7 = (bf16[64,4224]{1,0:T(8,128)(2,1)S(1)}, bf16[64,4224]{1,0:T(8,128)(2,1)S(1)}, u32[]{:S(2)}, u32[]{:S(2)}) collective-permute-start(bf16[64,4224]{1,0:T(8,128)(2,1)S(1)} %shard_map.85.own_ref), channel_id=1, source_target_pairs={{0,16},{16,0},{1,17},{17,1},{2,18},{18,2},{3,19},{19,3},{4,20},{20... | collective-permute-start | bytes 1622024 | tf_op jit(solution)/shard_map/ppermute | solution.py:14
  30.3 2.6 %collective-permute-start.19 = (bf16[64,4096]{1,0:T(8,128)(2,1)S(1)}, bf16[64,4096]{1,0:T(8,128)(2,1)S(1)}, u32[]{:S(2)}, u32[]{:S(2)}) collective-permute-start(bf16[64,4096]{1,0:T(8,128)(2,1)S(1)} %get-tuple-element.52), channel_id=1, source_target_pairs={{0,16},{16,0},{1,17},{17,1},{2,18},{18,2},{3,19},{19,3},{4,20},{20... | collective-permute-start | bytes 1572872 | tf_op jit(solution)/shard_map/ppermute | solution.py:14
  32.4 3.3 %collective-permute-start.8 = (bf16[64,4096]{1,0:T(8,128)(2,1)S(1)}, bf16[64,4096]{1,0:T(8,128)(2,1)S(1)}, u32[]{:S(2)}, u32[]{:S(2)}) collective-permute-start(bf16[64,4096]{1,0:T(8,128)(2,1)S(1)} %get-tuple-element.42), channel_id=1, source_target_pairs={{0,16},{16,0},{1,17},{17,1},{2,18},{18,2},{3,19},{19,3},{4,20},{20... | collective-permute-start | bytes 1572872 | tf_op jit(solution)/shard_map/ppermute | solution.py:14
  32.9 4.4 %collective-permute-start.20 = (bf16[16,2048]{1,0:T(8,128)(2,1)S(1)}, bf16[16,2048]{1,0:T(8,128)(2,1)S(1)}, u32[]{:S(2)}, u32[]{:S(2)}) collective-permute-start(bf16[16,2048]{1,0:T(8,128)(2,1)S(1)} %get-tuple-element.53), channel_id=1, source_target_pairs={{0,2},{1,3},{2,0},{3,1},{4,6},{5,7},{6,4},{7,5},{8,10},{9,11},{10,... | collective-permute-start | bytes 196616 | tf_op jit(solution)/shard_map/ppermute | solution.py:14
  34.2 4.8 %collective-permute-start.21 = (bf16[16,2048]{1,0:T(8,128)(2,1)S(1)}, bf16[16,2048]{1,0:T(8,128)(2,1)S(1)}, u32[]{:S(2)}, u32[]{:S(2)}) collective-permute-start(bf16[16,2048]{1,0:T(8,128)(2,1)S(1)} %get-tuple-element.54), channel_id=1, source_target_pairs={{0,1},{1,0},{2,3},{3,2},{4,5},{5,4},{6,7},{7,6},{8,9},{9,8},{10,11... | collective-permute-start | bytes 196616 | tf_op jit(solution)/shard_map/ppermute | solution.py:14
  35.8 5.3 %collective-permute-start.10 = (bf16[16,2048]{1,0:T(8,128)(2,1)S(1)}, bf16[16,2048]{1,0:T(8,128)(2,1)S(1)}, u32[]{:S(2)}, u32[]{:S(2)}) collective-permute-start(bf16[16,2048]{1,0:T(8,128)(2,1)S(1)} %get-tuple-element.44), channel_id=1, source_target_pairs={{0,1},{1,0},{2,3},{3,2},{4,5},{5,4},{6,7},{7,6},{8,9},{9,8},{10,11... | collective-permute-start | bytes 196616 | tf_op jit(solution)/shard_map/ppermute | solution.py:14
  36.4 4.7 %collective-permute-start.9 = (bf16[16,2048]{1,0:T(8,128)(2,1)S(1)}, bf16[16,2048]{1,0:T(8,128)(2,1)S(1)}, u32[]{:S(2)}, u32[]{:S(2)}) collective-permute-start(bf16[16,2048]{1,0:T(8,128)(2,1)S(1)} %get-tuple-element.43), channel_id=1, source_target_pairs={{0,2},{1,3},{2,0},{3,1},{4,6},{5,7},{6,4},{7,5},{8,10},{9,11},{10,... | collective-permute-start | bytes 196616 | tf_op jit(solution)/shard_map/ppermute | solution.py:14
  39.1 5.6 %collective-permute-start.22 = (bf16[16,4096]{1,0:T(8,128)(2,1)S(1)}, bf16[16,4096]{1,0:T(8,128)(2,1)S(1)}, u32[]{:S(2)}, u32[]{:S(2)}) collective-permute-start(bf16[16,4096]{1,0:T(8,128)(2,1)S(1)} %get-tuple-element.55), channel_id=1, source_target_pairs={{0,1},{1,0},{2,3},{3,2},{4,5},{5,4},{6,7},{7,6},{8,9},{9,8},{10,11... | collective-permute-start | bytes 393224 | tf_op jit(solution)/shard_map/ppermute | solution.py:14
  40.4 5.4 %collective-permute-start.23 = (bf16[16,4096]{1,0:T(8,128)(2,1)S(1)}, bf16[16,4096]{1,0:T(8,128)(2,1)S(1)}, u32[]{:S(2)}, u32[]{:S(2)}) collective-permute-start(bf16[16,4096]{1,0:T(8,128)(2,1)S(1)} %get-tuple-element.56), channel_id=1, source_target_pairs={{0,2},{1,3},{2,0},{3,1},{4,6},{5,7},{6,4},{7,5},{8,10},{9,11},{10,... | collective-permute-start | bytes 393224 | tf_op jit(solution)/shard_map/ppermute | solution.py:14
  41.1 8.0 %collective-permute-start.11 = (bf16[16,4096]{1,0:T(8,128)(2,1)S(1)}, bf16[16,4096]{1,0:T(8,128)(2,1)S(1)}, u32[]{:S(2)}, u32[]{:S(2)}) collective-permute-start(bf16[16,4096]{1,0:T(8,128)(2,1)S(1)} %get-tuple-element.45), channel_id=1, source_target_pairs={{0,1},{1,0},{2,3},{3,2},{4,5},{5,4},{6,7},{7,6},{8,9},{9,8},{10,11... | collective-permute-start | bytes 393224 | tf_op jit(solution)/shard_map/ppermute | solution.py:14
  42.7 6.4 %collective-permute-start.12 = (bf16[16,4096]{1,0:T(8,128)(2,1)S(1)}, bf16[16,4096]{1,0:T(8,128)(2,1)S(1)}, u32[]{:S(2)}, u32[]{:S(2)}) collective-permute-start(bf16[16,4096]{1,0:T(8,128)(2,1)S(1)} %get-tuple-element.46), channel_id=1, source_target_pairs={{0,2},{1,3},{2,0},{3,1},{4,6},{5,7},{6,4},{7,5},{8,10},{9,11},{10,... | collective-permute-start | bytes 393224 | tf_op jit(solution)/shard_map/ppermute | solution.py:14
  45.9 5.9 %collective-permute-start.24 = (bf16[8,4096]{1,0:T(8,128)(2,1)S(1)}, bf16[8,4096]{1,0:T(8,128)(2,1)S(1)}, u32[]{:S(2)}, u32[]{:S(2)}) collective-permute-start(bf16[8,4096]{1,0:T(8,128)(2,1)S(1)} %get-tuple-element.57), channel_id=1, source_target_pairs={{0,8},{1,9},{2,10},{3,11},{4,12},{5,13},{6,14},{7,15},{8,0},{9,1},... | collective-permute-start | bytes 196616 | tf_op jit(solution)/shard_map/ppermute | solution.py:14
  48.0 6.2 %collective-permute-start.25 = (bf16[8,4096]{1,0:T(8,128)(2,1)S(1)}, bf16[8,4096]{1,0:T(8,128)(2,1)S(1)}, u32[]{:S(2)}, u32[]{:S(2)}) collective-permute-start(bf16[8,4096]{1,0:T(8,128)(2,1)S(1)} %get-tuple-element.58), channel_id=1, source_target_pairs={{0,12},{1,13},{2,14},{3,15},{4,8},{5,9},{6,10},{7,11},{8,4},{9,5},... | collective-permute-start | bytes 196616 | tf_op jit(solution)/shard_map/ppermute | solution.py:14
  49.2 5.0 %collective-permute-start.13 = (bf16[8,4096]{1,0:T(8,128)(2,1)S(1)}, bf16[8,4096]{1,0:T(8,128)(2,1)S(1)}, u32[]{:S(2)}, u32[]{:S(2)}) collective-permute-start(bf16[8,4096]{1,0:T(8,128)(2,1)S(1)} %get-tuple-element.48), channel_id=1, source_target_pairs={{0,4},{1,5},{2,6},{3,7},{4,0},{5,1},{6,2},{7,3},{8,12},{9,13},{10,... | collective-permute-start | bytes 196616 | tf_op jit(solution)/shard_map/ppermute | solution.py:14

commit v5 on v3

--- a/solution.py
+++ b/solution.py
@@ -103,7 +103,7 @@
     extra = own_ref.shape[1] - width
     owners = lax.axis_size("dev")
     me = lax.axis_index("dev")
-    step = min(width, 1024)
+    step = min(width, 2048)
     gate = up = 0.0
     for k in range(0, width, step):
         part = jnp.concatenate([other_ref[:, k : k + step], own_ref[:, k : k + step]])
@@ -113,6 +113,7 @@
     parts = jnp.concatenate([other_ref[:, width:], own_ref[:, width:]]).astype(jnp.float32)
     lane = lax.broadcasted_iota(jnp.int32, (1, extra), 1)
     weight = jnp.sum(jnp.where(lax.rem(lane, owners) == me, parts, 0.0), axis=1, keepdims=True)
+    step = min(width, 512)
     for k in range(0, width, step):
         down = down_ref[0, :, k : k + step]
         value = jnp.dot(hidden, down, preferred_element_type=jnp.float32) * weight

time: 55.1 us -> 55.1 us (level)
  no operation moved by 1% of the time
where the time goes in v5:
time: 55.1 us; the launch traced here: 54.9 us
  starting transfers between devices  28.7 us (52%)
  waiting for transfers between devices  14.8 us (27%)
  Pallas kernels  10.3 us (19%)
  local copies, waits for them, and re-layouts  0.97 us (2%)
    ppermute x26, starting transfers between devices, swap(): return lax.ppermute(block, axis, [(i, i ^ offset) for i in range(count)])  28.7 us
    ppermute x26, waiting for transfers between devices, swap(): return lax.ppermute(block, axis, [(i, i ^ offset) for i in range(count)])  14.8 us
    pallas_call x13, Pallas kernels, local_call(): pl.pallas_call(kernel, out_shape=[jax.ShapeDtypeStruct(shape, dtype) for...  4.86 us
    pallas_call x1, Pallas kernels, load(): pl.pallas_call(load_kernel, out_shape=[jax.ShapeDtypeStruct(x.shape, x.dt...  3.79 us
    pallas_call x1, Pallas kernels, prepare(): pl.pallas_call(functools.partial(prepare_kernel, slots), out_shape=jax.Sh...  1.63 us
  transfers between devices with their start and end apart: 26, of which 11 were waited for; matrix products, arithmetic and copies ran while one was open for 0% of the time, Pallas kernels for 15%

profile of v5, /device:TPU:0, one launch (start us, length us, event | category | flops | bytes accessed | tf_op | source)
XLA Modules:
  0.0 54.9 jit_solution(13023583785381492011)
XLA Ops:
  0.0 1.6 %shard_map.82.refs_3_ = bf16[8,4224]{1,0:T(8,128)(2,1)} custom-call(bf16[8,4096]{1,0:T(8,128)(2,1)} %tok_ref.1, f32[4096]{0:T(1024)} %gain_ref.1, s32[8,8]{1,0:T(8,128)} %ids_ref.1, f32[8,8]{1,0:T(8,128)} %weight_ref.1, s32[16]{0:T(128)} %placement_ref.1), custom_call_target="tpu_custom_call" | custom-call | tf_op jit(solution)/shard_map/pallas_call | solution.py:47
  1.6 3.0 %collective-permute-start = (bf16[8,4224]{1,0:T(8,128)(2,1)}, bf16[8,4224]{1,0:T(8,128)(2,1)S(1)}, u32[]{:S(2)}, u32[]{:S(2)}) collective-permute-start(bf16[8,4224]{1,0:T(8,128)(2,1)} %shard_map.82.refs_3_), channel_id=1, source_target_pairs={{0,4},{1,5},{2,6},{3,7},{4,0},{5,1},{6,2},{7,3},{8,12},{9,13},{10,... | collective-permute-start | bytes 202760 | tf_op jit(solution)/shard_map/ppermute | solution.py:14
  4.7 2.6 %collective-permute-start.1 = (bf16[8,4224]{1,0:T(8,128)(2,1)}, bf16[8,4224]{1,0:T(8,128)(2,1)S(1)}, u32[]{:S(2)}, u32[]{:S(2)}) collective-permute-start(bf16[8,4224]{1,0:T(8,128)(2,1)} %shard_map.82.refs_3_), channel_id=1, source_target_pairs={{0,8},{1,9},{2,10},{3,11},{4,12},{5,13},{6,14},{7,15},{8,0},{9,1},... | collective-permute-start | bytes 202760 | tf_op jit(solution)/shard_map/ppermute | solution.py:14
  7.2 0.0 collective-permute-start.2
  7.3 0.9 %copy-done = bf16[8,4224]{1,0:T(8,128)(2,1)S(1)} copy-done((bf16[8,4224]{1,0:T(8,128)(2,1)S(1)}, bf16[8,4224]{1,0:T(8,128)(2,1)}, u32[]{:S(2)}) %copy-start) | copy-done | bytes 67608
  8.2 3.8 %shard_map.83 = (bf16[1,4096,384]{2,1,0:T(8,128)(2,1)S(1)}, bf16[1,4096,384]{2,1,0:T(8,128)(2,1)S(1)}, bf16[1,384,4096]{2,1,0:T(8,128)(2,1)S(1)}, bf16[8,4224]{1,0:T(8,128)(2,1)S(1)}) custom-call(bf16[1,4096,384]{2,1,0:T(8,128)(2,1)} %refs_0_.1, bf16[1,4096,384]{2,1,0:T(8,128)(2,1)} %refs_1_.1, bf16[1,384,4096]{2,1,0:T(8,128)(2,1)} %refs_2_.1, ...), custom_call_target="tpu_custom_call" | custom-call | bytes 19009536 | tf_op jit(solution)/shard_map/pallas_call | solution.py:170
  12.0 0.3 collective-permute-done.1.refs_0_
  12.3 1.4 %collective-permute-done.2.refs_1_ = bf16[8,4224]{1,0:T(8,128)(2,1)S(1)} collective-permute-done((bf16[8,4224]{1,0:T(8,128)(2,1)}, bf16[8,4224]{1,0:T(8,128)(2,1)S(1)}, u32[]{:S(2)}, u32[]{:S(2)}) %collective-permute-start.2) | collective-permute-done | bytes 67616 | tf_op jit(solution)/shard_map/ppermute | solution.py:14
  13.7 1.6 %collective-permute-start.14 = (bf16[16,4224]{1,0:T(8,128)(2,1)S(1)}, bf16[16,4224]{1,0:T(8,128)(2,1)S(1)}, u32[]{:S(2)}, u32[]{:S(2)}) collective-permute-start(bf16[16,4224]{1,0:T(8,128)(2,1)S(1)} %shard_map.90.column_ref), channel_id=1, source_target_pairs={{0,1},{1,0},{2,3},{3,2},{4,5},{5,4},{6,7},{7,6},{8,9},{9,8},{10,11... | collective-permute-start | bytes 405512 | tf_op jit(solution)/shard_map/ppermute | solution.py:14
  15.2 0.6 %collective-permute-start.3 = (bf16[16,4224]{1,0:T(8,128)(2,1)S(1)}, bf16[16,4224]{1,0:T(8,128)(2,1)S(1)}, u32[]{:S(2)}, u32[]{:S(2)}) collective-permute-start(bf16[16,4224]{1,0:T(8,128)(2,1)S(1)} %shard_map.84.column_ref), channel_id=1, source_target_pairs={{0,1},{1,0},{2,3},{3,2},{4,5},{5,4},{6,7},{7,6},{8,9},{9,8},{10,11... | collective-permute-start | bytes 405512 | tf_op jit(solution)/shard_map/ppermute | solution.py:14
  15.8 1.5 %collective-permute-start.15 = (bf16[16,4224]{1,0:T(8,128)(2,1)S(1)}, bf16[16,4224]{1,0:T(8,128)(2,1)S(1)}, u32[]{:S(2)}, u32[]{:S(2)}) collective-permute-start(bf16[16,4224]{1,0:T(8,128)(2,1)S(1)} %shard_map.90.column_ref), channel_id=1, source_target_pairs={{0,2},{1,3},{2,0},{3,1},{4,6},{5,7},{6,4},{7,5},{8,10},{9,11},{10,... | collective-permute-start | bytes 405512 | tf_op jit(solution)/shard_map/ppermute | solution.py:14
  17.4 0.5 collective-permute-start.4
  17.9 0.9 %collective-permute-done.14.x_ref = bf16[16,4224]{1,0:T(8,128)(2,1)S(1)} collective-permute-done((bf16[16,4224]{1,0:T(8,128)(2,1)S(1)}, bf16[16,4224]{1,0:T(8,128)(2,1)S(1)}, u32[]{:S(2)}, u32[]{:S(2)}) %collective-permute-start.14) | collective-permute-done | bytes 135200 | tf_op jit(solution)/shard_map/ppermute | solution.py:14
  18.8 1.5 %collective-permute-start.17 = (bf16[16,2176]{1,0:T(8,128)(2,1)S(1)}, bf16[16,2176]{1,0:T(8,128)(2,1)S(1)}, u32[]{:S(2)}, u32[]{:S(2)}) collective-permute-start(bf16[16,2176]{1,0:T(8,128)(2,1)S(1)} %slice.19), channel_id=1, source_target_pairs={{0,2},{1,3},{2,0},{3,1},{4,6},{5,7},{6,4},{7,5},{8,10},{9,11},{10,... | collective-permute-start | bytes 208904 | tf_op jit(solution)/shard_map/ppermute | solution.py:14
  20.3 1.6 %collective-permute-start.6 = (bf16[16,2176]{1,0:T(8,128)(2,1)S(1)}, bf16[16,2176]{1,0:T(8,128)(2,1)S(1)}, u32[]{:S(2)}, u32[]{:S(2)}) collective-permute-start(bf16[16,2176]{1,0:T(8,128)(2,1)S(1)} %slice.17), channel_id=1, source_target_pairs={{0,2},{1,3},{2,0},{3,1},{4,6},{5,7},{6,4},{7,5},{8,10},{9,11},{10,... | collective-permute-start | bytes 208904 | tf_op jit(solution)/shard_map/ppermute | solution.py:14
  22.0 1.4 %collective-permute-start.16 = (bf16[16,2048]{1,0:T(8,128)(2,1)S(1)}, bf16[16,2048]{1,0:T(8,128)(2,1)S(1)}, u32[]{:S(2)}, u32[]{:S(2)}) collective-permute-start(bf16[16,2048]{1,0:T(8,128)(2,1)S(1)} %slice.18), channel_id=1, source_target_pairs={{0,1},{1,0},{2,3},{3,2},{4,5},{5,4},{6,7},{7,6},{8,9},{9,8},{10,11... | collective-permute-start | bytes 196616 | tf_op jit(solution)/shard_map/ppermute | solution.py:14
  23.4 1.4 %collective-permute-start.5 = (bf16[16,2048]{1,0:T(8,128)(2,1)S(1)}, bf16[16,2048]{1,0:T(8,128)(2,1)S(1)}, u32[]{:S(2)}, u32[]{:S(2)}) collective-permute-start(bf16[16,2048]{1,0:T(8,128)(2,1)S(1)} %slice.16), channel_id=1, source_target_pairs={{0,1},{1,0},{2,3},{3,2},{4,5},{5,4},{6,7},{7,6},{8,9},{9,8},{10,11... | collective-permute-start | bytes 196616 | tf_op jit(solution)/shard_map/ppermute | solution.py:14
  24.8 1.5 %collective-permute-done.16.left_ref = bf16[16,2048]{1,0:T(8,128)(2,1)S(1)} collective-permute-done((bf16[16,2048]{1,0:T(8,128)(2,1)S(1)}, bf16[16,2048]{1,0:T(8,128)(2,1)S(1)}, u32[]{:S(2)}, u32[]{:S(2)}) %collective-permute-start.16) | collective-permute-done | bytes 65568 | tf_op jit(solution)/shard_map/ppermute | solution.py:14
  26.3 0.1 collective-permute-start.18
  26.4 1.3 %collective-permute-done.5.left_ref = bf16[16,2048]{1,0:T(8,128)(2,1)S(1)} collective-permute-done((bf16[16,2048]{1,0:T(8,128)(2,1)S(1)}, bf16[16,2048]{1,0:T(8,128)(2,1)S(1)}, u32[]{:S(2)}, u32[]{:S(2)}) %collective-permute-start.5) | collective-permute-done | bytes 65568 | tf_op jit(solution)/shard_map/ppermute | solution.py:14
  27.7 0.1 collective-permute-start.7
  27.8 0.5 collective-permute-done.18.other_ref
  28.3 1.9 %shard_map.92 = (bf16[64,4096]{1,0:T(8,128)(2,1)S(1)}, f32[64,4096]{1,0:T(8,128)S(1)}) custom-call(bf16[64,4224]{1,0:T(8,128)(2,1)S(1)} %shard_map.91.own_ref, bf16[64,4224]{1,0:T(8,128)(2,1)S(1)} %collective-permute-done.18.other_ref, bf16[1,4096,384]{2,1,0:T(8,128)(2,1)S(1)} %get-tuple-element.38.gate_ref, ...), custom_call_target="tpu_custom_call" | custom-call | bytes 12091392 | tf_op jit(solution)/shard_map/pallas_call | solution.py:64
  30.3 0.2 collective-permute-start.19
  30.5 1.9 %shard_map.86 = (bf16[64,4096]{1,0:T(8,128)(2,1)S(1)}, f32[64,4096]{1,0:T(8,128)S(1)}) custom-call(bf16[64,4224]{1,0:T(8,128)(2,1)S(1)} %shard_map.85.own_ref, bf16[64,4224]{1,0:T(8,128)(2,1)S(1)} %collective-permute-done.7.other_ref, bf16[1,4096,384]{2,1,0:T(8,128)(2,1)S(1)} %get-tuple-element.38.gate_ref, ...), custom_call_target="tpu_custom_call" | custom-call | bytes 12091392 | tf_op jit(solution)/shard_map/pallas_call | solution.py:64
  32.4 0.4 collective-permute-start.8
  32.9 1.4 %collective-permute-start.20 = (bf16[16,2048]{1,0:T(8,128)(2,1)S(1)}, bf16[16,2048]{1,0:T(8,128)(2,1)S(1)}, u32[]{:S(2)}, u32[]{:S(2)}) collective-permute-start(bf16[16,2048]{1,0:T(8,128)(2,1)S(1)} %get-tuple-element.53), channel_id=1, source_target_pairs={{0,2},{1,3},{2,0},{3,1},{4,6},{5,7},{6,4},{7,5},{8,10},{9,11},{10,... | collective-permute-start | bytes 196616 | tf_op jit(solution)/shard_map/ppermute | solution.py:14
  34.2 1.5 %collective-permute-start.21 = (bf16[16,2048]{1,0:T(8,128)(2,1)S(1)}, bf16[16,2048]{1,0:T(8,128)(2,1)S(1)}, u32[]{:S(2)}, u32[]{:S(2)}) collective-permute-start(bf16[16,2048]{1,0:T(8,128)(2,1)S(1)} %get-tuple-element.54), channel_id=1, source_target_pairs={{0,1},{1,0},{2,3},{3,2},{4,5},{5,4},{6,7},{7,6},{8,9},{9,8},{10,11... | collective-permute-start | bytes 196616 | tf_op jit(solution)/shard_map/ppermute | solution.py:14
  35.8 0.6 %collective-permute-start.10 = (bf16[16,2048]{1,0:T(8,128)(2,1)S(1)}, bf16[16,2048]{1,0:T(8,128)(2,1)S(1)}, u32[]{:S(2)}, u32[]{:S(2)}) collective-permute-start(bf16[16,2048]{1,0:T(8,128)(2,1)S(1)} %get-tuple-element.44), channel_id=1, source_target_pairs={{0,1},{1,0},{2,3},{3,2},{4,5},{5,4},{6,7},{7,6},{8,9},{9,8},{10,11... | collective-permute-start | bytes 196616 | tf_op jit(solution)/shard_map/ppermute | solution.py:14
  36.4 0.9 %collective-permute-start.9 = (bf16[16,2048]{1,0:T(8,128)(2,1)S(1)}, bf16[16,2048]{1,0:T(8,128)(2,1)S(1)}, u32[]{:S(2)}, u32[]{:S(2)}) collective-permute-start(bf16[16,2048]{1,0:T(8,128)(2,1)S(1)} %get-tuple-element.43), channel_id=1, source_target_pairs={{0,2},{1,3},{2,0},{3,1},{4,6},{5,7},{6,4},{7,5},{8,10},{9,11},{10,... | collective-permute-start | bytes 196616 | tf_op jit(solution)/shard_map/ppermute | solution.py:14
  37.3 1.7 %collective-permute-done.21.right_ref = bf16[16,2048]{1,0:T(8,128)(2,1)S(1)} collective-permute-done((bf16[16,2048]{1,0:T(8,128)(2,1)S(1)}, bf16[16,2048]{1,0:T(8,128)(2,1)S(1)}, u32[]{:S(2)}, u32[]{:S(2)}) %collective-permute-start.21) | collective-permute-done | bytes 65568 | tf_op jit(solution)/shard_map/ppermute | solution.py:14
  39.0 0.1 shard_map.94
  39.1 1.3 %collective-permute-start.22 = (bf16[16,4096]{1,0:T(8,128)(2,1)S(1)}, bf16[16,4096]{1,0:T(8,128)(2,1)S(1)}, u32[]{:S(2)}, u32[]{:S(2)}) collective-permute-start(bf16[16,4096]{1,0:T(8,128)(2,1)S(1)} %get-tuple-element.55), channel_id=1, source_target_pairs={{0,1},{1,0},{2,3},{3,2},{4,5},{5,4},{6,7},{7,6},{8,9},{9,8},{10,11... | collective-permute-start | bytes 393224 | tf_op jit(solution)/shard_map/ppermute | solution.py:14
  40.4 0.6 %collective-permute-start.23 = (bf16[16,4096]{1,0:T(8,128)(2,1)S(1)}, bf16[16,4096]{1,0:T(8,128)(2,1)S(1)}, u32[]{:S(2)}, u32[]{:S(2)}) collective-permute-start(bf16[16,4096]{1,0:T(8,128)(2,1)S(1)} %get-tuple-element.56), channel_id=1, source_target_pairs={{0,2},{1,3},{2,0},{3,1},{4,6},{5,7},{6,4},{7,5},{8,10},{9,11},{10,... | collective-permute-start | bytes 393224 | tf_op jit(solution)/shard_map/ppermute | solution.py:14
  41.1 0.1 shard_map.88
  41.1 1.6 %collective-permute-start.11 = (bf16[16,4096]{1,0:T(8,128)(2,1)S(1)}, bf16[16,4096]{1,0:T(8,128)(2,1)S(1)}, u32[]{:S(2)}, u32[]{:S(2)}) collective-permute-start(bf16[16,4096]{1,0:T(8,128)(2,1)S(1)} %get-tuple-element.45), channel_id=1, source_target_pairs={{0,1},{1,0},{2,3},{3,2},{4,5},{5,4},{6,7},{7,6},{8,9},{9,8},{10,11... | collective-permute-start | bytes 393224 | tf_op jit(solution)/shard_map/ppermute | solution.py:14
  42.7 0.7 %collective-permute-start.12 = (bf16[16,4096]{1,0:T(8,128)(2,1)S(1)}, bf16[16,4096]{1,0:T(8,128)(2,1)S(1)}, u32[]{:S(2)}, u32[]{:S(2)}) collective-permute-start(bf16[16,4096]{1,0:T(8,128)(2,1)S(1)} %get-tuple-element.46), channel_id=1, source_target_pairs={{0,2},{1,3},{2,0},{3,1},{4,6},{5,7},{6,4},{7,5},{8,10},{9,11},{10,... | collective-permute-start | bytes 393224 | tf_op jit(solution)/shard_map/ppermute | solution.py:14
  43.3 1.3 %collective-permute-done.22.x_ref = bf16[16,4096]{1,0:T(8,128)(2,1)S(1)} collective-permute-done((bf16[16,4096]{1,0:T(8,128)(2,1)S(1)}, bf16[16,4096]{1,0:T(8,128)(2,1)S(1)}, u32[]{:S(2)}, u32[]{:S(2)}) %collective-permute-start.22) | collective-permute-done | bytes 131104 | tf_op jit(solution)/shard_map/ppermute | solution.py:14
  44.7 1.1 %collective-permute-done.23.y_ref = bf16[16,4096]{1,0:T(8,128)(2,1)S(1)} collective-permute-done((bf16[16,4096]{1,0:T(8,128)(2,1)S(1)}, bf16[16,4096]{1,0:T(8,128)(2,1)S(1)}, u32[]{:S(2)}, u32[]{:S(2)}) %collective-permute-start.23) | collective-permute-done | bytes 131104 | tf_op jit(solution)/shard_map/ppermute | solution.py:14
  45.8 0.1 shard_map.95
  45.9 2.1 %collective-permute-start.24 = (bf16[8,4096]{1,0:T(8,128)(2,1)S(1)}, bf16[8,4096]{1,0:T(8,128)(2,1)S(1)}, u32[]{:S(2)}, u32[]{:S(2)}) collective-permute-start(bf16[8,4096]{1,0:T(8,128)(2,1)S(1)} %get-tuple-element.57), channel_id=1, source_target_pairs={{0,8},{1,9},{2,10},{3,11},{4,12},{5,13},{6,14},{7,15},{8,0},{9,1},... | collective-permute-start | bytes 196616 | tf_op jit(solution)/shard_map/ppermute | solution.py:14
  48.0 1.1 %collective-permute-start.25 = (bf16[8,4096]{1,0:T(8,128)(2,1)S(1)}, bf16[8,4096]{1,0:T(8,128)(2,1)S(1)}, u32[]{:S(2)}, u32[]{:S(2)}) collective-permute-start(bf16[8,4096]{1,0:T(8,128)(2,1)S(1)} %get-tuple-element.58), channel_id=1, source_target_pairs={{0,12},{1,13},{2,14},{3,15},{4,8},{5,9},{6,10},{7,11},{8,4},{9,5},... | collective-permute-start | bytes 196616 | tf_op jit(solution)/shard_map/ppermute | solution.py:14
  49.1 0.1 shard_map.89
  49.2 0.4 collective-permute-start.13
  49.6 2.2 %collective-permute-done.24.refs_1_ = bf16[8,4096]{1,0:T(8,128)(2,1)S(1)} collective-permute-done((bf16[8,4096]{1,0:T(8,128)(2,1)S(1)}, bf16[8,4096]{1,0:T(8,128)(2,1)S(1)}, u32[]{:S(2)}, u32[]{:S(2)}) %collective-permute-start.24) | collective-permute-done | bytes 65568 | tf_op jit(solution)/shard_map/ppermute | solution.py:14
  51.8 2.4 %collective-permute-done.25.refs_2_ = bf16[8,4096]{1,0:T(8,128)(2,1)S(1)} collective-permute-done((bf16[8,4096]{1,0:T(8,128)(2,1)S(1)}, bf16[8,4096]{1,0:T(8,128)(2,1)S(1)}, u32[]{:S(2)}, u32[]{:S(2)}) %collective-permute-start.25) | collective-permute-done | bytes 65568 | tf_op jit(solution)/shard_map/ppermute | solution.py:14
  54.2 0.0 collective-permute-done.13.refs_0_
  54.2 0.7 %shard_map.96 = bf16[8,4096]{1,0:T(8,128)(2,1)} custom-call(f32[8,4096]{1,0:T(8,128)S(1)} %get-tuple-element.47.first_ref, bf16[8,4096]{1,0:T(8,128)(2,1)S(1)} %collective-permute-done.13.refs_0_, bf16[8,4096]{1,0:T(8,128)(2,1)S(1)} %collective-permute-done.24.refs_1_, bf16[8,4096]{1,0:T(8,128)(2,1)S(1)} %collective-permute-done.25.refs_2_), custom_call_target="tpu_custom_call" | custom-call | bytes 393216 | tf_op jit(solution)/shard_map/pallas_call | solution.py:64
  (25 shorter events, 0.2 us)
Async XLA Ops:
  1.6 10.4 %collective-permute-start = (bf16[8,4224]{1,0:T(8,128)(2,1)}, bf16[8,4224]{1,0:T(8,128)(2,1)S(1)}, u32[]{:S(2)}, u32[]{:S(2)}) collective-permute-start(bf16[8,4224]{1,0:T(8,128)(2,1)} %shard_map.82.refs_3_), channel_id=1, source_target_pairs={{0,4},{1,5},{2,6},{3,7},{4,0},{5,1},{6,2},{7,3},{8,12},{9,13},{10,... | collective-permute-start | bytes 202760 | tf_op jit(solution)/shard_map/ppermute | solution.py:14
  4.7 7.6 %collective-permute-start.1 = (bf16[8,4224]{1,0:T(8,128)(2,1)}, bf16[8,4224]{1,0:T(8,128)(2,1)S(1)}, u32[]{:S(2)}, u32[]{:S(2)}) collective-permute-start(bf16[8,4224]{1,0:T(8,128)(2,1)} %shard_map.82.refs_3_), channel_id=1, source_target_pairs={{0,8},{1,9},{2,10},{3,11},{4,12},{5,13},{6,14},{7,15},{8,0},{9,1},... | collective-permute-start | bytes 202760 | tf_op jit(solution)/shard_map/ppermute | solution.py:14
  7.2 6.4 %collective-permute-start.2 = (bf16[8,4224]{1,0:T(8,128)(2,1)}, bf16[8,4224]{1,0:T(8,128)(2,1)S(1)}, u32[]{:S(2)}, u32[]{:S(2)}) collective-permute-start(bf16[8,4224]{1,0:T(8,128)(2,1)} %shard_map.82.refs_3_), channel_id=1, source_target_pairs={{0,12},{1,13},{2,14},{3,15},{4,8},{5,9},{6,10},{7,11},{8,4},{9,5},... | collective-permute-start | bytes 202760 | tf_op jit(solution)/shard_map/ppermute | solution.py:14
  7.2 0.9 %copy-start = (bf16[8,4224]{1,0:T(8,128)(2,1)S(1)}, bf16[8,4224]{1,0:T(8,128)(2,1)}, u32[]{:S(2)}) copy-start(bf16[8,4224]{1,0:T(8,128)(2,1)} %shard_map.82.refs_3_) | copy-start | bytes 202756
  13.7 5.1 %collective-permute-start.14 = (bf16[16,4224]{1,0:T(8,128)(2,1)S(1)}, bf16[16,4224]{1,0:T(8,128)(2,1)S(1)}, u32[]{:S(2)}, u32[]{:S(2)}) collective-permute-start(bf16[16,4224]{1,0:T(8,128)(2,1)S(1)} %shard_map.90.column_ref), channel_id=1, source_target_pairs={{0,1},{1,0},{2,3},{3,2},{4,5},{5,4},{6,7},{7,6},{8,9},{9,8},{10,11... | collective-permute-start | bytes 405512 | tf_op jit(solution)/shard_map/ppermute | solution.py:14
  15.2 5.1 %collective-permute-start.3 = (bf16[16,4224]{1,0:T(8,128)(2,1)S(1)}, bf16[16,4224]{1,0:T(8,128)(2,1)S(1)}, u32[]{:S(2)}, u32[]{:S(2)}) collective-permute-start(bf16[16,4224]{1,0:T(8,128)(2,1)S(1)} %shard_map.84.column_ref), channel_id=1, source_target_pairs={{0,1},{1,0},{2,3},{3,2},{4,5},{5,4},{6,7},{7,6},{8,9},{9,8},{10,11... | collective-permute-start | bytes 405512 | tf_op jit(solution)/shard_map/ppermute | solution.py:14
  15.8 6.1 %collective-permute-start.15 = (bf16[16,4224]{1,0:T(8,128)(2,1)S(1)}, bf16[16,4224]{1,0:T(8,128)(2,1)S(1)}, u32[]{:S(2)}, u32[]{:S(2)}) collective-permute-start(bf16[16,4224]{1,0:T(8,128)(2,1)S(1)} %shard_map.90.column_ref), channel_id=1, source_target_pairs={{0,2},{1,3},{2,0},{3,1},{4,6},{5,7},{6,4},{7,5},{8,10},{9,11},{10,... | collective-permute-start | bytes 405512 | tf_op jit(solution)/shard_map/ppermute | solution.py:14
  17.4 6.0 %collective-permute-start.4 = (bf16[16,4224]{1,0:T(8,128)(2,1)S(1)}, bf16[16,4224]{1,0:T(8,128)(2,1)S(1)}, u32[]{:S(2)}, u32[]{:S(2)}) collective-permute-start(bf16[16,4224]{1,0:T(8,128)(2,1)S(1)} %shard_map.84.column_ref), channel_id=1, source_target_pairs={{0,2},{1,3},{2,0},{3,1},{4,6},{5,7},{6,4},{7,5},{8,10},{9,11},{10,... | collective-permute-start | bytes 405512 | tf_op jit(solution)/shard_map/ppermute | solution.py:14
  18.8 7.5 %collective-permute-start.17 = (bf16[16,2176]{1,0:T(8,128)(2,1)S(1)}, bf16[16,2176]{1,0:T(8,128)(2,1)S(1)}, u32[]{:S(2)}, u32[]{:S(2)}) collective-permute-start(bf16[16,2176]{1,0:T(8,128)(2,1)S(1)} %slice.19), channel_id=1, source_target_pairs={{0,2},{1,3},{2,0},{3,1},{4,6},{5,7},{6,4},{7,5},{8,10},{9,11},{10,... | collective-permute-start | bytes 208904 | tf_op jit(solution)/shard_map/ppermute | solution.py:14
  20.3 7.4 %collective-permute-start.6 = (bf16[16,2176]{1,0:T(8,128)(2,1)S(1)}, bf16[16,2176]{1,0:T(8,128)(2,1)S(1)}, u32[]{:S(2)}, u32[]{:S(2)}) collective-permute-start(bf16[16,2176]{1,0:T(8,128)(2,1)S(1)} %slice.17), channel_id=1, source_target_pairs={{0,2},{1,3},{2,0},{3,1},{4,6},{5,7},{6,4},{7,5},{8,10},{9,11},{10,... | collective-permute-start | bytes 208904 | tf_op jit(solution)/shard_map/ppermute | solution.py:14
  22.0 4.3 %collective-permute-start.16 = (bf16[16,2048]{1,0:T(8,128)(2,1)S(1)}, bf16[16,2048]{1,0:T(8,128)(2,1)S(1)}, u32[]{:S(2)}, u32[]{:S(2)}) collective-permute-start(bf16[16,2048]{1,0:T(8,128)(2,1)S(1)} %slice.18), channel_id=1, source_target_pairs={{0,1},{1,0},{2,3},{3,2},{4,5},{5,4},{6,7},{7,6},{8,9},{9,8},{10,11... | collective-permute-start | bytes 196616 | tf_op jit(solution)/shard_map/ppermute | solution.py:14
  23.4 4.3 %collective-permute-start.5 = (bf16[16,2048]{1,0:T(8,128)(2,1)S(1)}, bf16[16,2048]{1,0:T(8,128)(2,1)S(1)}, u32[]{:S(2)}, u32[]{:S(2)}) collective-permute-start(bf16[16,2048]{1,0:T(8,128)(2,1)S(1)} %slice.16), channel_id=1, source_target_pairs={{0,1},{1,0},{2,3},{3,2},{4,5},{5,4},{6,7},{7,6},{8,9},{9,8},{10,11... | collective-permute-start | bytes 196616 | tf_op jit(solution)/shard_map/ppermute | solution.py:14
  26.3 2.0 %collective-permute-start.18 = (bf16[64,4224]{1,0:T(8,128)(2,1)S(1)}, bf16[64,4224]{1,0:T(8,128)(2,1)S(1)}, u32[]{:S(2)}, u32[]{:S(2)}) collective-permute-start(bf16[64,4224]{1,0:T(8,128)(2,1)S(1)} %shard_map.91.own_ref), channel_id=1, source_target_pairs={{0,16},{16,0},{1,17},{17,1},{2,18},{18,2},{3,19},{19,3},{4,20},{20... | collective-permute-start | bytes 1622024 | tf_op jit(solution)/shard_map/ppermute | solution.py:14
  27.7 2.7 %collective-permute-start.7 = (bf16[64,4224]{1,0:T(8,128)(2,1)S(1)}, bf16[64,4224]{1,0:T(8,128)(2,1)S(1)}, u32[]{:S(2)}, u32[]{:S(2)}) collective-permute-start(bf16[64,4224]{1,0:T(8,128)(2,1)S(1)} %shard_map.85.own_ref), channel_id=1, source_target_pairs={{0,16},{16,0},{1,17},{17,1},{2,18},{18,2},{3,19},{19,3},{4,20},{20... | collective-permute-start | bytes 1622024 | tf_op jit(solution)/shard_map/ppermute | solution.py:14
  30.3 2.6 %collective-permute-start.19 = (bf16[64,4096]{1,0:T(8,128)(2,1)S(1)}, bf16[64,4096]{1,0:T(8,128)(2,1)S(1)}, u32[]{:S(2)}, u32[]{:S(2)}) collective-permute-start(bf16[64,4096]{1,0:T(8,128)(2,1)S(1)} %get-tuple-element.52), channel_id=1, source_target_pairs={{0,16},{16,0},{1,17},{17,1},{2,18},{18,2},{3,19},{19,3},{4,20},{20... | collective-permute-start | bytes 1572872 | tf_op jit(solution)/shard_map/ppermute | solution.py:14
  32.4 3.3 %collective-permute-start.8 = (bf16[64,4096]{1,0:T(8,128)(2,1)S(1)}, bf16[64,4096]{1,0:T(8,128)(2,1)S(1)}, u32[]{:S(2)}, u32[]{:S(2)}) collective-permute-start(bf16[64,4096]{1,0:T(8,128)(2,1)S(1)} %get-tuple-element.42), channel_id=1, source_target_pairs={{0,16},{16,0},{1,17},{17,1},{2,18},{18,2},{3,19},{19,3},{4,20},{20... | collective-permute-start | bytes 1572872 | tf_op jit(solution)/shard_map/ppermute | solution.py:14
  32.9 4.4 %collective-permute-start.20 = (bf16[16,2048]{1,0:T(8,128)(2,1)S(1)}, bf16[16,2048]{1,0:T(8,128)(2,1)S(1)}, u32[]{:S(2)}, u32[]{:S(2)}) collective-permute-start(bf16[16,2048]{1,0:T(8,128)(2,1)S(1)} %get-tuple-element.53), channel_id=1, source_target_pairs={{0,2},{1,3},{2,0},{3,1},{4,6},{5,7},{6,4},{7,5},{8,10},{9,11},{10,... | collective-permute-start | bytes 196616 | tf_op jit(solution)/shard_map/ppermute | solution.py:14
  34.2 4.8 %collective-permute-start.21 = (bf16[16,2048]{1,0:T(8,128)(2,1)S(1)}, bf16[16,2048]{1,0:T(8,128)(2,1)S(1)}, u32[]{:S(2)}, u32[]{:S(2)}) collective-permute-start(bf16[16,2048]{1,0:T(8,128)(2,1)S(1)} %get-tuple-element.54), channel_id=1, source_target_pairs={{0,1},{1,0},{2,3},{3,2},{4,5},{5,4},{6,7},{7,6},{8,9},{9,8},{10,11... | collective-permute-start | bytes 196616 | tf_op jit(solution)/shard_map/ppermute | solution.py:14
  35.8 5.3 %collective-permute-start.10 = (bf16[16,2048]{1,0:T(8,128)(2,1)S(1)}, bf16[16,2048]{1,0:T(8,128)(2,1)S(1)}, u32[]{:S(2)}, u32[]{:S(2)}) collective-permute-start(bf16[16,2048]{1,0:T(8,128)(2,1)S(1)} %get-tuple-element.44), channel_id=1, source_target_pairs={{0,1},{1,0},{2,3},{3,2},{4,5},{5,4},{6,7},{7,6},{8,9},{9,8},{10,11... | collective-permute-start | bytes 196616 | tf_op jit(solution)/shard_map/ppermute | solution.py:14
  36.4 4.7 %collective-permute-start.9 = (bf16[16,2048]{1,0:T(8,128)(2,1)S(1)}, bf16[16,2048]{1,0:T(8,128)(2,1)S(1)}, u32[]{:S(2)}, u32[]{:S(2)}) collective-permute-start(bf16[16,2048]{1,0:T(8,128)(2,1)S(1)} %get-tuple-element.43), channel_id=1, source_target_pairs={{0,2},{1,3},{2,0},{3,1},{4,6},{5,7},{6,4},{7,5},{8,10},{9,11},{10,... | collective-permute-start | bytes 196616 | tf_op jit(solution)/shard_map/ppermute | solution.py:14
  39.1 5.6 %collective-permute-start.22 = (bf16[16,4096]{1,0:T(8,128)(2,1)S(1)}, bf16[16,4096]{1,0:T(8,128)(2,1)S(1)}, u32[]{:S(2)}, u32[]{:S(2)}) collective-permute-start(bf16[16,4096]{1,0:T(8,128)(2,1)S(1)} %get-tuple-element.55), channel_id=1, source_target_pairs={{0,1},{1,0},{2,3},{3,2},{4,5},{5,4},{6,7},{7,6},{8,9},{9,8},{10,11... | collective-permute-start | bytes 393224 | tf_op jit(solution)/shard_map/ppermute | solution.py:14
  40.4 5.4 %collective-permute-start.23 = (bf16[16,4096]{1,0:T(8,128)(2,1)S(1)}, bf16[16,4096]{1,0:T(8,128)(2,1)S(1)}, u32[]{:S(2)}, u32[]{:S(2)}) collective-permute-start(bf16[16,4096]{1,0:T(8,128)(2,1)S(1)} %get-tuple-element.56), channel_id=1, source_target_pairs={{0,2},{1,3},{2,0},{3,1},{4,6},{5,7},{6,4},{7,5},{8,10},{9,11},{10,... | collective-permute-start | bytes 393224 | tf_op jit(solution)/shard_map/ppermute | solution.py:14
  41.1 8.0 %collective-permute-start.11 = (bf16[16,4096]{1,0:T(8,128)(2,1)S(1)}, bf16[16,4096]{1,0:T(8,128)(2,1)S(1)}, u32[]{:S(2)}, u32[]{:S(2)}) collective-permute-start(bf16[16,4096]{1,0:T(8,128)(2,1)S(1)} %get-tuple-element.45), channel_id=1, source_target_pairs={{0,1},{1,0},{2,3},{3,2},{4,5},{5,4},{6,7},{7,6},{8,9},{9,8},{10,11... | collective-permute-start | bytes 393224 | tf_op jit(solution)/shard_map/ppermute | solution.py:14
  42.7 6.4 %collective-permute-start.12 = (bf16[16,4096]{1,0:T(8,128)(2,1)S(1)}, bf16[16,4096]{1,0:T(8,128)(2,1)S(1)}, u32[]{:S(2)}, u32[]{:S(2)}) collective-permute-start(bf16[16,4096]{1,0:T(8,128)(2,1)S(1)} %get-tuple-element.46), channel_id=1, source_target_pairs={{0,2},{1,3},{2,0},{3,1},{4,6},{5,7},{6,4},{7,5},{8,10},{9,11},{10,... | collective-permute-start | bytes 393224 | tf_op jit(solution)/shard_map/ppermute | solution.py:14
  45.9 5.9 %collective-permute-start.24 = (bf16[8,4096]{1,0:T(8,128)(2,1)S(1)}, bf16[8,4096]{1,0:T(8,128)(2,1)S(1)}, u32[]{:S(2)}, u32[]{:S(2)}) collective-permute-start(bf16[8,4096]{1,0:T(8,128)(2,1)S(1)} %get-tuple-element.57), channel_id=1, source_target_pairs={{0,8},{1,9},{2,10},{3,11},{4,12},{5,13},{6,14},{7,15},{8,0},{9,1},... | collective-permute-start | bytes 196616 | tf_op jit(solution)/shard_map/ppermute | solution.py:14
  48.0 6.2 %collective-permute-start.25 = (bf16[8,4096]{1,0:T(8,128)(2,1)S(1)}, bf16[8,4096]{1,0:T(8,128)(2,1)S(1)}, u32[]{:S(2)}, u32[]{:S(2)}) collective-permute-start(bf16[8,4096]{1,0:T(8,128)(2,1)S(1)} %get-tuple-element.58), channel_id=1, source_target_pairs={{0,12},{1,13},{2,14},{3,15},{4,8},{5,9},{6,10},{7,11},{8,4},{9,5},... | collective-permute-start | bytes 196616 | tf_op jit(solution)/shard_map/ppermute | solution.py:14
  49.2 5.0 %collective-permute-start.13 = (bf16[8,4096]{1,0:T(8,128)(2,1)S(1)}, bf16[8,4096]{1,0:T(8,128)(2,1)S(1)}, u32[]{:S(2)}, u32[]{:S(2)}) collective-permute-start(bf16[8,4096]{1,0:T(8,128)(2,1)S(1)} %get-tuple-element.48), channel_id=1, source_target_pairs={{0,4},{1,5},{2,6},{3,7},{4,0},{5,1},{6,2},{7,3},{8,12},{9,13},{10,... | collective-permute-start | bytes 196616 | tf_op jit(solution)/shard_map/ppermute | solution.py:14
